TPU v7x, 128 devices: a whole 4x4x4 slice. The times are simulated.
128 devices in a mesh: dp: 32 (over x, z_hi, y), tensor: 4 (over z_lo, core).
Axes of the slice: x: 4, y: 4, z: 4 (z_hi: 2, z_lo: 2; z = z_hi * 2 + z_lo), core: 2. Of those that a mesh axis runs over, the one named last changes fastest.
Arguments:
- tokens_in: bfloat16 [16384, 1024], P(('dp', 'tensor')), may hold values from -6 to 6
- image_starts: int32 [11], replicated, may hold values from 0 to 15014, as said below
- norm_gain: float32 [2, 2, 1024], replicated, may hold values from 0.5 to 1.5
- norm_bias: float32 [2, 2, 1024], replicated, may hold values from -1.5 to 1.5
- qkv_weight: bfloat16 [2, 1024, 3, 1024], P(None, None, None, 'tensor'), may hold values from -0.1875 to 0.1875
- qv_bias: float32 [2, 2, 1024], P(None, None, 'tensor'), may hold values from -0.1 to 0.1
- proj_weight: bfloat16 [2, 1024, 1024], P(None, 'tensor'), may hold values from -4 to 4
- out_bias: float32 [2, 2, 1024], replicated, may hold values from -1.5 to 1.5
- layer_scale: float32 [2, 2, 1024], replicated, may hold values from 0.5 to 1.5
- fc1_weight: bfloat16 [2, 1024, 4096], P(None, None, 'tensor'), may hold values from -0.1875 to 0.1875
- fc1_bias: float32 [2, 4096], P(None, 'tensor'), may hold values from -1.5 to 1.5
- fc2_weight: bfloat16 [2, 4096, 1024], P(None, 'tensor'), may hold values from -0.125 to 0.125
- out_grad: float32 [16384, 1024], P(('dp', 'tensor')), may hold values from -6 to 6
Outputs:
- tokens_out: bfloat16 [16384, 1024], P(('dp', 'tensor'))
- tokens_grad: float32 [16384, 1024], P(('dp', 'tensor'))
- norm_gain_grad: float32 [2, 2, 1024], replicated
- norm_bias_grad: float32 [2, 2, 1024], replicated
- qkv_weight_grad: float32 [2, 1024, 3, 1024], P(None, 'dp', None, 'tensor')
- qv_bias_grad: float32 [2, 2, 1024], P(None, None, 'tensor')
- proj_weight_grad: float32 [2, 1024, 1024], P(None, 'tensor', 'dp')
- out_bias_grad: float32 [2, 2, 1024], replicated
- layer_scale_grad: float32 [2, 2, 1024], replicated
- fc1_weight_grad: float32 [2, 1024, 4096], P(None, 'dp', 'tensor')
- fc1_bias_grad: float32 [2, 4096], P(None, 'tensor')
- fc2_weight_grad: float32 [2, 4096, 1024], P(None, 'tensor', 'dp')
Inputs may be any that keep to these rules, and one draw needn't show every extreme that they name: `image_starts`: starts increase; every image is 1370 consecutive tokens and images do not intersect; the last image ends at the last token.
All inputs are finite; a program needn't handle non-finite values.
Results may differ from a plain program's by a relative error of at most 0.024.
Values may be sent and summed in bfloat16 or wider, within the bound.
A program may use at most 320 MiB of HBM per device.

v0:
```python
import jax
import jax.numpy as jnp
from jax import lax
from jax.sharding import PartitionSpec as P

HEAD_DIM = 64
IMG_LEN = 1370


EPS = 1e-06
NEG = -1e30


def copy_for_each(x, axis):
    copies = jnp.broadcast_to(x, (lax.axis_size(axis), *x.shape))
    return lax.all_to_all(copies, axis, split_axis=0, concat_axis=0, tiled=True)


def laid_out(parts, dim):
    shape = list(parts.shape[1:])
    shape[dim] *= parts.shape[0]
    return jnp.moveaxis(parts, 0, dim).reshape(shape)


def collect(x, axis, dim):
    parts = copy_for_each(x, axis)
    return laid_out(parts, dim)


def split_up(x, dim, devices):
    shape = x.shape
    parts = x.reshape(*shape[:dim], devices, shape[dim] // devices, *shape[dim + 1 :])
    return jnp.moveaxis(parts, dim, 0)


def sum_at_owner(x, axis, dim):
    parts = split_up(x, dim, lax.axis_size(axis))
    arrived = lax.all_to_all(parts, axis, split_axis=0, concat_axis=0, tiled=True)
    return arrived.astype(jnp.float32).sum(axis=0)


def shifted(value, axis, steps):
    count = lax.axis_size(axis)
    initial, last = (max(0, -steps), min(count, count - steps))
    return lax.ppermute(value, axis, [(source, source + steps) for source in range(initial, last)])


def one_scatter(arrays, axis, dims):
    devices = lax.axis_size(axis)
    parts = [split_up(a, dim, devices) for a, dim in zip(arrays, dims)]
    lines = jnp.concatenate([b.reshape(devices, -1) for b in parts], axis=1)
    rows = max(16, -(-lines.shape[1] // 1024) * 8)
    lines = jnp.pad(lines, ((0, 0), (0, rows * 128 - lines.shape[1]))).reshape(-1, 128)
    vector, at, done = (lax.psum_scatter(lines, axis, tiled=True).reshape(-1), 0, [])
    for b in parts:
        part = b[0]
        done.append(vector[at : at + part.size].reshape(part.shape))
        at += part.size
    return tuple(done)


def layer_norm(values, gain_row, bias_row):
    average = jnp.mean(values, axis=-1, keepdims=True)
    centered = values - average
    spread = jnp.mean(centered * centered, axis=-1, keepdims=True)
    return centered * lax.rsqrt(spread + EPS) * gain_row + bias_row


def gelu_exact(values):
    return jax.nn.gelu(values, approximate=False)


def segment_ids(positions, image_starts, total_rows):
    started = positions[:, None] >= image_starts[None, :]
    inside = started & (positions[:, None] < image_starts[None, :] + IMG_LEN)
    passed = jnp.sum(started.astype(jnp.int32), axis=1)
    within = jnp.sum(inside.astype(jnp.int32), axis=1)
    in_range = (positions >= 0) & (positions < total_rows)
    return jnp.where(in_range, 2 * passed - within, -1)


def split_heads(matrix):
    return matrix.reshape(matrix.shape[0], matrix.shape[1] // HEAD_DIM, HEAD_DIM)


def rows_inner(left_side, right_side):
    return lax.dot_general(
        left_side, right_side, (((0,), (0,)), ((), ())), preferred_element_type=jnp.float32
    )


def gather_rows(rows_low):
    return collect(rows_low, "tensor", 0)


def gather_grads(rows_low):
    return collect(rows_low, "tensor", 0)


def branch_total(left_side, right_side):
    return sum_at_owner(
        jnp.dot(left_side, right_side, preferred_element_type=jnp.float32).astype(jnp.bfloat16),
        "tensor",
        0,
    )


def input_total(left_side, right_side):
    return sum_at_owner(
        lax.dot_general(
            left_side, right_side, (((1,), (1,)), ((), ())), preferred_element_type=jnp.float32
        ).astype(jnp.bfloat16),
        "tensor",
        0,
    )


def fetch_keys(pieces, offset):
    return shifted((pieces[0], pieces[1]), "dp", offset)


def return_grads(pieces, offset):
    return (
        shifted(pieces[0].astype(jnp.bfloat16), "dp", offset).astype(jnp.float32),
        shifted(pieces[1].astype(jnp.bfloat16), "dp", offset).astype(jnp.float32),
    )


def attend_forward(queries, keys_win, vals_win, same_image):
    factor = HEAD_DIM ** (-0.5)
    scores = (
        jnp.einsum(
            "qhe,khe->hqk",
            split_heads(queries),
            split_heads(keys_win),
            preferred_element_type=jnp.float32,
        )
        * factor
    )
    scores = jnp.where(same_image[None], scores, NEG)
    highest = jnp.max(scores, axis=-1, keepdims=True)
    raised = jnp.exp(scores - highest)
    totals = jnp.sum(raised, axis=-1, keepdims=True)
    probs = (raised / totals).astype(jnp.bfloat16)
    attended = jnp.einsum(
        "hqk,khe->qhe", probs, split_heads(vals_win), preferred_element_type=jnp.float32
    )
    return (attended.reshape(queries.shape).astype(jnp.bfloat16), highest + jnp.log(totals))


def attend_backward(queries, keys_win, vals_win, same_image, log_total, grad_attended):
    factor = HEAD_DIM ** (-0.5)
    query_heads = split_heads(queries)
    key_heads = split_heads(keys_win)
    val_heads = split_heads(vals_win)
    grad_heads = split_heads(grad_attended)
    scores = (
        jnp.einsum("qhe,khe->hqk", query_heads, key_heads, preferred_element_type=jnp.float32)
        * factor
    )
    scores = jnp.where(same_image[None], scores, NEG)
    probs = jnp.exp(scores - log_total)
    grad_probs = jnp.einsum(
        "qhe,khe->hqk", grad_heads, val_heads, preferred_element_type=jnp.float32
    )
    grad_vals = jnp.einsum(
        "hqk,qhe->khe", probs.astype(jnp.bfloat16), grad_heads, preferred_element_type=jnp.float32
    )
    inner = jnp.sum(probs * grad_probs, axis=-1, keepdims=True)
    grad_scores = (probs * (grad_probs - inner)).astype(jnp.bfloat16)
    grad_query = (
        jnp.einsum("hqk,khe->qhe", grad_scores, key_heads, preferred_element_type=jnp.float32)
        * factor
    )
    grad_keys = (
        jnp.einsum("hqk,qhe->khe", grad_scores, query_heads, preferred_element_type=jnp.float32)
        * factor
    )
    return (
        grad_query.reshape(queries.shape),
        grad_keys.reshape(keys_win.shape),
        grad_vals.reshape(vals_win.shape),
    )


def shards(
    tokens_in,
    image_starts,
    norm_gain,
    norm_bias,
    qkv_weight,
    qv_bias,
    proj_weight,
    out_bias,
    layer_scale,
    fc1_weight,
    fc1_bias,
    fc2_weight,
    out_grad,
):
    own_rows = tokens_in.shape[0]
    tensor_count = lax.axis_size("tensor")
    stretch_rows = own_rows * tensor_count
    total_rows = stretch_rows * lax.axis_size("dp")
    width = tokens_in.shape[1]
    local_width = qkv_weight.shape[3]
    ff_local = fc1_weight.shape[2]
    layer_count = qkv_weight.shape[0]
    halo_rows = IMG_LEN - 1
    reach = (halo_rows + stretch_rows - 1) // stretch_rows
    plan = [
        (distance, min(stretch_rows, halo_rows - (distance - 1) * stretch_rows))
        for distance in range(1, reach + 1)
    ]
    tensor_index = lax.axis_index("tensor")
    stretch_first = lax.axis_index("dp") * stretch_rows
    query_ids = segment_ids(
        stretch_first + jnp.arange(stretch_rows, dtype=jnp.int32), image_starts, total_rows
    )
    key_ids = segment_ids(
        stretch_first - halo_rows + jnp.arange(stretch_rows + 2 * halo_rows, dtype=jnp.int32),
        image_starts,
        total_rows,
    )
    same_image = query_ids[:, None] == key_ids[None, :]
    hidden = tokens_in.astype(jnp.float32)
    saved = []
    for layer_index in range(layer_count):
        gain_rows = norm_gain[layer_index]
        bias_rows = norm_bias[layer_index]
        scales = layer_scale[layer_index]
        offsets = out_bias[layer_index]
        normed_one, norm_one_back = jax.vjp(layer_norm, hidden, gain_rows[0], bias_rows[0])
        rows_one = gather_rows(normed_one.astype(jnp.bfloat16))
        w_qkv = qkv_weight[layer_index].reshape(width, 3 * local_width)
        bias_three = jnp.concatenate(
            [
                qv_bias[layer_index, 0],
                jnp.zeros((local_width,), jnp.float32),
                qv_bias[layer_index, 1],
            ]
        )
        projected = (
            jnp.dot(rows_one, w_qkv, preferred_element_type=jnp.float32) + bias_three
        ).astype(jnp.bfloat16)
        queries = projected[:, :local_width]
        keys_own = projected[:, local_width : 2 * local_width]
        vals_own = projected[:, 2 * local_width :]
        lower_keys, lower_vals, upper_keys, upper_vals = ([], [], [], [])
        for distance, rows_taken in plan:
            got_keys, got_vals = fetch_keys(
                (keys_own[stretch_rows - rows_taken :], vals_own[stretch_rows - rows_taken :]),
                distance,
            )
            lower_keys.insert(0, got_keys)
            lower_vals.insert(0, got_vals)
            got_keys, got_vals = fetch_keys(
                (keys_own[:rows_taken], vals_own[:rows_taken]), -distance
            )
            upper_keys.append(got_keys)
            upper_vals.append(got_vals)
        keys_win = jnp.concatenate(lower_keys + [keys_own] + upper_keys, 0)
        vals_win = jnp.concatenate(lower_vals + [vals_own] + upper_vals, 0)
        attended, log_total = attend_forward(queries, keys_win, vals_win, same_image)
        branch_one = branch_total(attended, proj_weight[layer_index])
        mixed = hidden + scales[0] * (branch_one + offsets[0])
        normed_two, norm_two_back = jax.vjp(layer_norm, mixed, gain_rows[1], bias_rows[1])
        rows_two = gather_rows(normed_two.astype(jnp.bfloat16))
        pre_act = (
            jnp.dot(rows_two, fc1_weight[layer_index], preferred_element_type=jnp.float32)
            + fc1_bias[layer_index]
        )
        activated = gelu_exact(pre_act).astype(jnp.bfloat16)
        branch_two = branch_total(activated, fc2_weight[layer_index])
        saved.append(
            (
                norm_one_back,
                rows_one,
                w_qkv,
                queries,
                keys_win,
                vals_win,
                log_total,
                attended,
                branch_one,
                norm_two_back,
                rows_two,
                pre_act,
                activated,
                branch_two,
            )
        )
        hidden = mixed + scales[1] * (branch_two + offsets[1])
    grad_hidden = out_grad
    weight_parts = [None] * layer_count
    vector_parts = [None] * layer_count
    for layer_index in reversed(range(layer_count)):
        (
            norm_one_back,
            rows_one,
            w_qkv,
            queries,
            keys_win,
            vals_win,
            log_total,
            attended,
            branch_one,
            norm_two_back,
            rows_two,
            pre_act,
            activated,
            branch_two,
        ) = saved[layer_index]
        scales = layer_scale[layer_index]
        offsets = out_bias[layer_index]
        grad_scale_two = jnp.sum(grad_hidden * (branch_two + offsets[1]), axis=0)
        grad_offset_two = scales[1] * jnp.sum(grad_hidden, axis=0)
        grad_two = gather_grads((grad_hidden * scales[1]).astype(jnp.bfloat16))
        grad_fc2 = rows_inner(activated, grad_two)
        grad_act = lax.dot_general(
            grad_two,
            fc2_weight[layer_index],
            (((1,), (1,)), ((), ())),
            preferred_element_type=jnp.float32,
        )
        gelu_value, gelu_back = jax.vjp(gelu_exact, pre_act)
        grad_pre = gelu_back(grad_act)[0].astype(jnp.bfloat16)
        grad_fc1_bias = jnp.sum(grad_pre, axis=0, dtype=jnp.float32)
        grad_fc1 = rows_inner(rows_two, grad_pre)
        grad_norm_two = input_total(grad_pre, fc1_weight[layer_index])
        grad_mixed_part, grad_gain_two, grad_shift_two = norm_two_back(grad_norm_two)
        grad_mixed = grad_hidden + grad_mixed_part
        grad_scale_one = jnp.sum(grad_mixed * (branch_one + offsets[0]), axis=0)
        grad_offset_one = scales[0] * jnp.sum(grad_mixed, axis=0)
        grad_one = gather_grads((grad_mixed * scales[0]).astype(jnp.bfloat16))
        grad_proj = rows_inner(attended, grad_one)
        grad_attended = lax.dot_general(
            grad_one,
            proj_weight[layer_index],
            (((1,), (1,)), ((), ())),
            preferred_element_type=jnp.float32,
        ).astype(jnp.bfloat16)
        grad_query, grad_keys_win, grad_vals_win = attend_backward(
            queries, keys_win, vals_win, same_image, log_total, grad_attended
        )
        grad_keys = grad_keys_win[halo_rows : halo_rows + stretch_rows]
        grad_vals = grad_vals_win[halo_rows : halo_rows + stretch_rows]
        for distance, rows_taken in plan:
            lower_first = halo_rows - (distance - 1) * stretch_rows - rows_taken
            came_keys, came_vals = return_grads(
                (
                    grad_keys_win[lower_first : lower_first + rows_taken],
                    grad_vals_win[lower_first : lower_first + rows_taken],
                ),
                -distance,
            )
            grad_keys = grad_keys.at[stretch_rows - rows_taken :].add(came_keys)
            grad_vals = grad_vals.at[stretch_rows - rows_taken :].add(came_vals)
            upper_first = halo_rows + distance * stretch_rows
            came_keys, came_vals = return_grads(
                (
                    grad_keys_win[upper_first : upper_first + rows_taken],
                    grad_vals_win[upper_first : upper_first + rows_taken],
                ),
                distance,
            )
            grad_keys = grad_keys.at[:rows_taken].add(came_keys)
            grad_vals = grad_vals.at[:rows_taken].add(came_vals)
        grad_projected = jnp.concatenate([grad_query, grad_keys, grad_vals], 1).astype(jnp.bfloat16)
        grad_bias_qv = jnp.stack(
            [
                jnp.sum(grad_projected[:, :local_width], axis=0, dtype=jnp.float32),
                jnp.sum(grad_projected[:, 2 * local_width :], axis=0, dtype=jnp.float32),
            ]
        )
        grad_qkv = rows_inner(rows_one, grad_projected).reshape(width, 3, local_width)
        grad_norm_one = input_total(grad_projected, w_qkv)
        grad_in_part, grad_gain_one, grad_shift_one = norm_one_back(grad_norm_one)
        grad_hidden = grad_mixed + grad_in_part
        vector_rows = jnp.stack(
            [
                jnp.stack([grad_gain_one, grad_gain_two]),
                jnp.stack([grad_shift_one, grad_shift_two]),
                jnp.stack([grad_offset_one, grad_offset_two]),
                jnp.stack([grad_scale_one, grad_scale_two]),
            ]
        )
        qv_full = lax.dynamic_update_slice_in_dim(
            jnp.zeros((2, width), jnp.float32), grad_bias_qv, tensor_index * local_width, 1
        )
        fc1_full = lax.dynamic_update_slice_in_dim(
            jnp.zeros((ff_local * tensor_count,), jnp.float32),
            grad_fc1_bias,
            tensor_index * ff_local,
            0,
        )
        weight_terms = (grad_qkv, grad_proj, grad_fc1, grad_fc2)
        vector_terms = (vector_rows, qv_full, fc1_full)
        weight_parts[layer_index] = weight_terms
        vector_parts[layer_index] = vector_terms
    weight_stack = tuple(
        (
            jnp.stack([weight_parts[layer_index][member] for layer_index in range(layer_count)])
            for member in range(4)
        )
    )
    vector_stack = tuple(
        (
            jnp.stack([vector_parts[layer_index][member] for layer_index in range(layer_count)])
            for member in range(3)
        )
    )
    weight_sums = tuple(
        (
            part.astype(jnp.float32)
            for part in one_scatter(
                (
                    weight_stack[0].astype(jnp.bfloat16),
                    weight_stack[1].astype(jnp.bfloat16),
                    weight_stack[2].astype(jnp.bfloat16),
                    weight_stack[3].astype(jnp.bfloat16),
                ),
                "dp",
                (1, 2, 1, 2),
            )
        )
    )
    vector_sums = lax.psum(vector_stack, ("dp", "tensor"))
    vector_rows, qv_full, fc1_full = vector_sums
    qv_grad = lax.dynamic_slice_in_dim(qv_full, tensor_index * local_width, local_width, 2)
    fc1_bias_grad = lax.dynamic_slice_in_dim(fc1_full, tensor_index * ff_local, ff_local, 1)
    return (
        hidden.astype(jnp.bfloat16),
        grad_hidden,
        vector_rows[:, 0],
        vector_rows[:, 1],
        weight_sums[0],
        qv_grad,
        weight_sums[1],
        vector_rows[:, 2],
        vector_rows[:, 3],
        weight_sums[2],
        fc1_bias_grad,
        weight_sums[3],
    )


def solution(mesh):
    return jax.shard_map(
        shards,
        mesh=mesh,
        in_specs=(
            P(("dp", "tensor"), None),
            P(),
            P(),
            P(),
            P(None, None, None, "tensor"),
            P(None, None, "tensor"),
            P(None, "tensor", None),
            P(),
            P(),
            P(None, None, "tensor"),
            P(None, "tensor"),
            P(None, "tensor", None),
            P(("dp", "tensor"), None),
        ),
        out_specs=(
            P(("dp", "tensor"), None),
            P(("dp", "tensor"), None),
            P(),
            P(),
            P(None, "dp", None, "tensor"),
            P(None, None, "tensor"),
            P(None, "tensor", "dp"),
            P(),
            P(),
            P(None, "dp", "tensor"),
            P(None, "tensor"),
            P(None, "tensor", "dp"),
        ),
        check_vma=False,
    )
```

profile of v0, /device:TPU:0, one launch (start us, length us, event | category | flops | bytes accessed | tf_op | source)
XLA Modules:
  0.0 1286.4 jit_solution(4337384710801781527)
XLA Ops:
  60.9 15.0 %collective-permute-done.5 = bf16[345,256]{1,0:T(8,128)(2,1)S(1)} collective-permute-done((bf16[345,256]{1,0:T(8,128)(2,1)S(1)}, bf16[345,256]{1,0:T(8,128)(2,1)S(1)}, u32[]{:S(2)}, u32[]{:S(2)}) %collective-permute-start.5) | collective-permute-done | bytes 176672 | tf_op jit(solution)/shard_map/ppermute | solution.py:45
  105.2 16.3 %concatenate.102 = bf16[3250,256]{1,0:T(8,128)(2,1)} concatenate(bf16[345,256]{1,0:T(8,128)(2,1)} %collective-permute-done, bf16[512,256]{1,0:T(8,128)(2,1)} %collective-permute-done.1, bf16[512,256]{1,0:T(8,128)(2,1)} %collective-permute-done.2, bf16[512,256]{1,0:T(8,128)(2,1)} %get-tuple-element.568, bf16[512,256]{1,0:T(8,128)(2,1)} %collective-permute-done.3, ...), dimensions={0} | concatenate | bytes 3328000 | tf_op jit(solution)/shard_map/concatenate | solution.py:263
  124.3 13.3 %fusion.157 = (f32[4,512]{1,0:T(4,128)S(1)}, f32[4,512,3250]{1,2,0:T(8,128)}) fusion(bf16[512,4,64]{0,2,1:T(8,128)(2,1)} %bitcast.414, bf16[3250,4,64]{0,2,1:T(8,128)(2,1)S(1)} %bitcast.383, pred[512,3250]{0,1:T(8,128)(4,1)} %broadcast_compare_fusion), kind=kOutput, calls=%fused_computation.325 | convolution fusion | flops 871933952 | bytes 30222336 | tf_op jit(solution)/shard_map/qhe,khe->hqk/dot_general | solution.py:132
  165.8 13.2 %all-to-all-done.1 = bf16[4,128,1024]{2,1,0:T(8,128)(2,1)S(1)} async-done(((bf16[4,128,1024]{2,1,0:T(8,128)(2,1)}), bf16[4,128,1024]{2,1,0:T(8,128)(2,1)S(1)}, u32[]{:S(2)}, u32[]{:S(2)}) %all-to-all-start.1) | async-done | bytes 1048608 | tf_op jit(solution)/shard_map/all_to_all | solution.py:38
  186.4 14.4 %all-to-all-done.2 = bf16[4,128,1024]{1,2,0:T(8,128)(2,1)S(1)} async-done(((bf16[4,128,1024]{1,2,0:T(8,128)(2,1)}), bf16[4,128,1024]{1,2,0:T(8,128)(2,1)S(1)}, u32[]{:S(2)}, u32[]{:S(2)}) %all-to-all-start.2) | async-done | bytes 1048608 | tf_op jit(solution)/shard_map/all_to_all | solution.py:16
  211.3 16.9 %all_to_all.80 = bf16[4,128,1024]{2,1,0:T(8,128)(2,1)S(1)} all-to-all(bf16[4,128,1024]{2,1,0:T(8,128)(2,1)S(1)} %bitcast.433), channel_id=1, replica_groups=mesh['dp'=32,'tensor'=4] {'tensor'}, dimensions={0} | all-to-all | bytes 2097152 | tf_op jit(solution)/shard_map/all_to_all | solution.py:38
  312.3 14.0 %concatenate.106 = bf16[3250,256]{1,0:T(8,128)(2,1)} concatenate(bf16[345,256]{1,0:T(8,128)(2,1)} %copy-done.62, bf16[512,256]{1,0:T(8,128)(2,1)S(1)} %collective-permute-done.19, bf16[512,256]{1,0:T(8,128)(2,1)S(1)} %collective-permute-done.20, bf16[512,256]{1,0:T(8,128)(2,1)S(1)} %get-tuple-element.559, bf16[512,256]{1,0:T(8,128)(2,1)S(1)} %collective-permute-done.21, ...), dimensions={0} | concatenate | bytes 3328000 | tf_op jit(solution)/shard_map/concatenate | solution.py:262
  329.1 14.3 %concatenate.105 = bf16[3250,256]{1,0:T(8,128)(2,1)} concatenate(bf16[345,256]{1,0:T(8,128)(2,1)} %collective-permute-done.12, bf16[512,256]{1,0:T(8,128)(2,1)} %collective-permute-done.13, bf16[512,256]{1,0:T(8,128)(2,1)S(1)} %collective-permute-done.14, bf16[512,256]{1,0:T(8,128)(2,1)S(1)} %get-tuple-element.561, bf16[512,256]{1,0:T(8,128)(2,1)S(1)} %collective-permute-done.15, ...), dimensions={0} | concatenate | bytes 3328000 | tf_op jit(solution)/shard_map/concatenate | solution.py:263
  382.0 16.9 %all_to_all.81 = bf16[4,128,1024]{2,1,0:T(8,128)(2,1)S(1)} all-to-all(bf16[4,128,1024]{2,1,0:T(8,128)(2,1)S(1)} %bitcast.393), channel_id=1, replica_groups=mesh['dp'=32,'tensor'=4] {'tensor'}, dimensions={0} | all-to-all | bytes 2097152 | tf_op jit(solution)/shard_map/all_to_all | solution.py:38
  400.7 17.8 %all_to_all.82 = bf16[4,128,1024]{1,2,0:T(8,128)(2,1)} all-to-all(bf16[4,128,1024]{1,2,0:T(8,128)(2,1)S(1)} %broadcast_in_dim.117), channel_id=1, replica_groups=mesh['dp'=32,'tensor'=4] {'tensor'}, dimensions={0} | all-to-all | bytes 2097152 | tf_op jit(solution)/shard_map/all_to_all | solution.py:16
  430.8 17.0 %all_to_all.83 = bf16[4,128,1024]{2,1,0:T(8,128)(2,1)S(1)} all-to-all(bf16[4,128,1024]{2,1,0:T(8,128)(2,1)S(1)} %bitcast.434), channel_id=1, replica_groups=mesh['dp'=32,'tensor'=4] {'tensor'}, dimensions={0} | all-to-all | bytes 2097152 | tf_op jit(solution)/shard_map/all_to_all | solution.py:38
  449.8 17.6 %all_to_all.84 = bf16[4,128,1024]{1,2,0:T(8,128)(2,1)} all-to-all(bf16[4,128,1024]{1,2,0:T(8,128)(2,1)S(1)} %broadcast_in_dim.118), channel_id=1, replica_groups=mesh['dp'=32,'tensor'=4] {'tensor'}, dimensions={0} | all-to-all | bytes 2097152 | tf_op jit(solution)/shard_map/all_to_all | solution.py:16
  476.8 16.9 %all_to_all.85 = bf16[4,128,1024]{2,1,0:T(8,128)(2,1)S(1)} all-to-all(bf16[4,128,1024]{2,1,0:T(8,128)(2,1)S(1)} %bitcast.435), channel_id=1, replica_groups=mesh['dp'=32,'tensor'=4] {'tensor'}, dimensions={0} | all-to-all | bytes 2097152 | tf_op jit(solution)/shard_map/all_to_all | solution.py:38
  521.3 13.3 %fusion.159 = (bf16[3250,4,64]{0,2,1:T(8,128)(2,1)}, f32[3250,4,64]{0,2,1:T(8,128)}) fusion(bf16[512,4,64]{0,2,1:T(8,128)(2,1)S(1)} %bitcast.422, f32[4,512,3250]{1,2,0:T(8,128)} %get-tuple-element.609, f32[4,512]{1,0:T(4,128)S(1)} %log_add_fusion.1), kind=kOutput, calls=%fused_computation.327 | convolution fusion | flops 866112000 | bytes 31886336 | tf_op jit(solution)/shard_map/hqk,qhe->khe/dot_general | solution.py:166
  539.1 17.0 %multiply_reduce_fusion.1 = (f32[4,512]{1,0:T(4,128)S(1)}, f32[4,512,3250]{1,2,0:T(8,128)}) fusion(f32[4,512,3250]{1,2,0:T(8,128)} %get-tuple-element.609, f32[4,512]{1,0:T(4,128)S(1)} %log_add_fusion.1, bf16[512,4,64]{0,2,1:T(8,128)(2,1)S(1)} %bitcast.423, bf16[3250,4,64]{0,2,1:T(8,128)(2,1)} %bitcast.389), kind=kOutput, calls=%fused_computation.4 | convolution fusion | flops 871933952 | bytes 55190528 | tf_op jit(solution)/shard_map/qhe,khe->hqk/dot_general | solution.py:163
  556.1 23.2 %multiply_convert_fusion.1 = bf16[4,512,3250]{1,2,0:T(8,128)(2,1)} fusion(f32[4,512,3250]{1,2,0:T(8,128)} %get-tuple-element.614, f32[4,512,3250]{1,2,0:T(8,128)} %get-tuple-element.609, f32[4,512]{1,0:T(4,128)S(1)} %get-tuple-element.613, f32[4,512]{1,0:T(4,128)S(1)} %log_add_fusion.1), kind=kLoop, calls=%fused_computation.3 | loop fusion | flops 26624000 | bytes 66576384 | tf_op jit(solution)/shard_map/convert_element_type | solution.py:170
  763.5 14.3 %copy.175 = bf16[32,2,1024,32]{3,2,1,0:T(8,128)(2,1)} copy(bf16[32,2,1024,32]{2,3,0,1:T(8,128)(2,1)} %maximum_bitcast_fusion.1) | data formatting | bytes 8388608 | tf_op jit(solution)/shard_map/transpose | solution.py:33
  777.8 21.1 %reshape.1242 = bf16[32,65536]{1,0:T(8,128)(2,1)} reshape(bf16[32,2,1024,32]{3,2,1,0:T(8,128)(2,1)} %copy.175) | data formatting | bytes 8388608 | tf_op jit(solution)/shard_map/reshape | solution.py:51
  817.3 16.7 %multiply_reduce_fusion = (f32[4,512]{1,0:T(4,128)S(1)}, f32[4,512,3250]{1,2,0:T(8,128)}) fusion(f32[4,512,3250]{1,2,0:T(8,128)} %get-tuple-element.606, f32[4,512]{1,0:T(4,128)S(1)} %log_add_fusion, bf16[512,4,64]{0,2,1:T(8,128)(2,1)} %bitcast.425, bf16[3250,4,64]{0,2,1:T(8,128)(2,1)S(1)} %bitcast.386), kind=kOutput, calls=%fused_computation.1 | convolution fusion | flops 871933952 | bytes 55190528 | tf_op jit(solution)/shard_map/qhe,khe->hqk/dot_general | solution.py:163
  834.1 23.2 %multiply_convert_fusion = bf16[4,512,3250]{1,2,0:T(8,128)(2,1)} fusion(f32[4,512,3250]{1,2,0:T(8,128)} %get-tuple-element.620, f32[4,512,3250]{1,2,0:T(8,128)} %get-tuple-element.606, f32[4,512]{1,0:T(4,128)S(1)} %get-tuple-element.619, f32[4,512]{1,0:T(4,128)S(1)} %log_add_fusion), kind=kLoop, calls=%fused_computation | loop fusion | flops 26624000 | bytes 66576384 | tf_op jit(solution)/shard_map/convert_element_type | solution.py:170
  984.0 17.3 %pad_maximum_fusion = bf16[32,196608]{1,0:T(8,128)(2,1)} fusion(bf16[32,65536]{1,0:T(8,128)(2,1)} %reshape.1242, bf16[32,65536]{1,0:T(8,128)(2,1)} %bitcast.382, bf16[32,16384]{1,0:T(8,128)(2,1)} %reshape.1238, bf16[32,49152]{1,0:T(8,128)(2,1)S(1)} %reshape.1237), kind=kLoop, calls=%fused_computation.22 | loop fusion | flops 50331648 | bytes 25165824 | tf_op jit(solution)/shard_map/concatenate | solution.py:51
  1014.8 74.5 %all-reduce = (f32[2,2,1024]{2,1,0:T(2,128)S(1)}, f32[2,4096]{1,0:T(2,128)S(1)}) all-reduce(f32[2,2,1024]{2,1,0:T(2,128)S(1)} %pad_maximum_fusion.5, f32[2,4096]{1,0:T(2,128)S(1)} %pad_maximum_fusion.4), channel_id=1, replica_groups=mesh['dp'=32,'tensor'=4] {'dp','tensor'}, use_global_device_ids=true, to_apply=%region_56.57 | all-reduce | flops 12288 | bytes 98304 | tf_op jit(solution)/shard_map/psum | solution.py:428
  1091.5 39.6 %all-reduce.3.cloned.1.call-done = f32[2,4,2,1024]{3,2,0,1:T(2,128)} async-done(((f32[2,4,2,1024]{3,2,0,1:T(2,128)}), f32[2,4,2,1024]{3,2,0,1:T(2,128)}) %all-reduce.3.cloned.1.call-update) | async-done | bytes 65552 | tf_op jit(solution)/shard_map/psum | solution.py:428
  1132.5 140.7 %reduce-scatter.2.cloned.1.call-done = bf16[1536,128]{1,0:T(8,128)(2,1)} async-done(((bf16[49152,128]{1,0:T(8,128)(2,1)}), bf16[1536,128]{1,0:T(8,128)(2,1)}) %reduce-scatter.2.cloned.1.call-update) | async-done | bytes 393232 | tf_op jit(solution)/shard_map/reduce_scatter | solution.py:54
  (624 shorter events, 663.6 us)
Async XLA Ops:
  44.8 32.4 %collective-permute-start.10 = (bf16[512,256]{1,0:T(8,128)(2,1)S(1)}, bf16[512,256]{1,0:T(8,128)(2,1)S(1)}, u32[]{:S(2)}, u32[]{:S(2)}) collective-permute-start(bf16[512,256]{1,0:T(8,128)(2,1)S(1)} %get-tuple-element.566), channel_id=1, source_target_pairs={{8,0},{12,4},{16,8},{20,12},{24,16},{28,20},{32,24},{36,28},{40,32... | collective-permute-start | bytes 786440 | tf_op jit(solution)/shard_map/ppermute | solution.py:45
  46.1 32.4 %collective-permute-start.9 = (bf16[512,256]{1,0:T(8,128)(2,1)S(1)}, bf16[512,256]{1,0:T(8,128)(2,1)S(1)}, u32[]{:S(2)}, u32[]{:S(2)}) collective-permute-start(bf16[512,256]{1,0:T(8,128)(2,1)S(1)} %get-tuple-element.566), channel_id=1, source_target_pairs={{4,0},{8,4},{12,8},{16,12},{20,16},{24,20},{28,24},{32,28},{36,32}... | collective-permute-start | bytes 786440 | tf_op jit(solution)/shard_map/ppermute | solution.py:45
  47.4 36.3 %collective-permute-start.8 = (bf16[512,256]{1,0:T(8,128)(2,1)S(1)}, bf16[512,256]{1,0:T(8,128)(2,1)S(1)}, u32[]{:S(2)}, u32[]{:S(2)}) collective-permute-start(bf16[512,256]{1,0:T(8,128)(2,1)S(1)} %get-tuple-element.566), channel_id=1, source_target_pairs={{0,4},{4,8},{8,12},{12,16},{16,20},{20,24},{24,28},{28,32},{32,36}... | collective-permute-start | bytes 786440 | tf_op jit(solution)/shard_map/ppermute | solution.py:45
  52.8 37.0 %collective-permute-start.7 = (bf16[512,256]{1,0:T(8,128)(2,1)S(1)}, bf16[512,256]{1,0:T(8,128)(2,1)S(1)}, u32[]{:S(2)}, u32[]{:S(2)}) collective-permute-start(bf16[512,256]{1,0:T(8,128)(2,1)S(1)} %get-tuple-element.566), channel_id=1, source_target_pairs={{0,8},{4,12},{8,16},{12,20},{16,24},{20,28},{24,32},{28,36},{32,40... | collective-permute-start | bytes 786440 | tf_op jit(solution)/shard_map/ppermute | solution.py:45
  75.9 29.3 %collective-permute-start.4 = (bf16[512,256]{1,0:T(8,128)(2,1)}, bf16[512,256]{1,0:T(8,128)(2,1)}, u32[]{:S(2)}, u32[]{:S(2)}) collective-permute-start(bf16[512,256]{1,0:T(8,128)(2,1)} %get-tuple-element.568), channel_id=1, source_target_pairs={{8,0},{12,4},{16,8},{20,12},{24,16},{28,20},{32,24},{36,28},{40,32... | collective-permute-start | bytes 786440 | tf_op jit(solution)/shard_map/ppermute | solution.py:45
  77.2 28.0 %collective-permute-start.3 = (bf16[512,256]{1,0:T(8,128)(2,1)}, bf16[512,256]{1,0:T(8,128)(2,1)}, u32[]{:S(2)}, u32[]{:S(2)}) collective-permute-start(bf16[512,256]{1,0:T(8,128)(2,1)} %get-tuple-element.568), channel_id=1, source_target_pairs={{4,0},{8,4},{12,8},{16,12},{20,16},{24,20},{28,24},{32,28},{36,32}... | collective-permute-start | bytes 786440 | tf_op jit(solution)/shard_map/ppermute | solution.py:45
  263.2 31.0 %collective-permute-start.22 = (bf16[512,256]{1,0:T(8,128)(2,1)S(1)}, bf16[512,256]{1,0:T(8,128)(2,1)S(1)}, u32[]{:S(2)}, u32[]{:S(2)}) collective-permute-start(bf16[512,256]{1,0:T(8,128)(2,1)S(1)} %get-tuple-element.559), channel_id=1, source_target_pairs={{8,0},{12,4},{16,8},{20,12},{24,16},{28,20},{32,24},{36,28},{40,32... | collective-permute-start | bytes 786440 | tf_op jit(solution)/shard_map/ppermute | solution.py:45
  264.5 31.0 %collective-permute-start.21 = (bf16[512,256]{1,0:T(8,128)(2,1)S(1)}, bf16[512,256]{1,0:T(8,128)(2,1)S(1)}, u32[]{:S(2)}, u32[]{:S(2)}) collective-permute-start(bf16[512,256]{1,0:T(8,128)(2,1)S(1)} %get-tuple-element.559), channel_id=1, source_target_pairs={{4,0},{8,4},{12,8},{16,12},{20,16},{24,20},{28,24},{32,28},{36,32}... | collective-permute-start | bytes 786440 | tf_op jit(solution)/shard_map/ppermute | solution.py:45
  265.8 34.3 %collective-permute-start.20 = (bf16[512,256]{1,0:T(8,128)(2,1)S(1)}, bf16[512,256]{1,0:T(8,128)(2,1)S(1)}, u32[]{:S(2)}, u32[]{:S(2)}) collective-permute-start(bf16[512,256]{1,0:T(8,128)(2,1)S(1)} %get-tuple-element.559), channel_id=1, source_target_pairs={{0,4},{4,8},{8,12},{12,16},{16,20},{20,24},{24,28},{28,32},{32,36}... | collective-permute-start | bytes 786440 | tf_op jit(solution)/shard_map/ppermute | solution.py:45
  271.7 35.1 %collective-permute-start.19 = (bf16[512,256]{1,0:T(8,128)(2,1)S(1)}, bf16[512,256]{1,0:T(8,128)(2,1)S(1)}, u32[]{:S(2)}, u32[]{:S(2)}) collective-permute-start(bf16[512,256]{1,0:T(8,128)(2,1)S(1)} %get-tuple-element.559), channel_id=1, source_target_pairs={{0,8},{4,12},{8,16},{12,20},{16,24},{20,28},{24,32},{28,36},{32,40... | collective-permute-start | bytes 786440 | tf_op jit(solution)/shard_map/ppermute | solution.py:45
  292.9 36.2 %collective-permute-start.16 = (bf16[512,256]{1,0:T(8,128)(2,1)S(1)}, bf16[512,256]{1,0:T(8,128)(2,1)S(1)}, u32[]{:S(2)}, u32[]{:S(2)}) collective-permute-start(bf16[512,256]{1,0:T(8,128)(2,1)S(1)} %get-tuple-element.561), channel_id=1, source_target_pairs={{8,0},{12,4},{16,8},{20,12},{24,16},{28,20},{32,24},{36,28},{40,32... | collective-permute-start | bytes 786440 | tf_op jit(solution)/shard_map/ppermute | solution.py:45
  294.2 34.9 %collective-permute-start.15 = (bf16[512,256]{1,0:T(8,128)(2,1)S(1)}, bf16[512,256]{1,0:T(8,128)(2,1)S(1)}, u32[]{:S(2)}, u32[]{:S(2)}) collective-permute-start(bf16[512,256]{1,0:T(8,128)(2,1)S(1)} %get-tuple-element.561), channel_id=1, source_target_pairs={{4,0},{8,4},{12,8},{16,12},{20,16},{24,20},{28,24},{32,28},{36,32}... | collective-permute-start | bytes 786440 | tf_op jit(solution)/shard_map/ppermute | solution.py:45
  295.5 33.6 %collective-permute-start.14 = (bf16[512,256]{1,0:T(8,128)(2,1)S(1)}, bf16[512,256]{1,0:T(8,128)(2,1)S(1)}, u32[]{:S(2)}, u32[]{:S(2)}) collective-permute-start(bf16[512,256]{1,0:T(8,128)(2,1)S(1)} %get-tuple-element.561), channel_id=1, source_target_pairs={{0,4},{4,8},{8,12},{12,16},{16,20},{20,24},{24,28},{28,32},{32,36}... | collective-permute-start | bytes 786440 | tf_op jit(solution)/shard_map/ppermute | solution.py:45
  300.0 29.0 %collective-permute-start.13 = (bf16[512,256]{1,0:T(8,128)(2,1)S(1)}, bf16[512,256]{1,0:T(8,128)(2,1)}, u32[]{:S(2)}, u32[]{:S(2)}) collective-permute-start(bf16[512,256]{1,0:T(8,128)(2,1)S(1)} %get-tuple-element.561), channel_id=1, source_target_pairs={{0,8},{4,12},{8,16},{12,20},{16,24},{20,28},{24,32},{28,36},{32,40... | collective-permute-start | bytes 786440 | tf_op jit(solution)/shard_map/ppermute | solution.py:45
  596.7 40.5 %collective-permute-start.34 = (bf16[345,256]{0,1:T(8,128)(2,1)}, bf16[345,256]{0,1:T(8,128)(2,1)S(1)}, u32[]{:S(2)}, u32[]{:S(2)}) collective-permute-start(bf16[345,256]{0,1:T(8,128)(2,1)} %bitcast.68), channel_id=1, source_target_pairs={{12,0},{16,4},{20,8},{24,12},{28,16},{32,20},{36,24},{40,28},{44,3... | collective-permute-start | bytes 529928 | tf_op jit(solution)/shard_map/ppermute | solution.py:45
  617.0 28.9 %collective-permute-start.35 = (bf16[345,256]{0,1:T(8,128)(2,1)}, bf16[345,256]{0,1:T(8,128)(2,1)}, u32[]{:S(2)}, u32[]{:S(2)}) collective-permute-start(bf16[345,256]{0,1:T(8,128)(2,1)} %bitcast.69), channel_id=1, source_target_pairs={{0,12},{4,16},{8,20},{12,24},{16,28},{20,32},{24,36},{28,40},{32,4... | collective-permute-start | bytes 529928 | tf_op jit(solution)/shard_map/ppermute | solution.py:45
  750.0 50.3 %all-to-all-start.14 = ((bf16[4,128,1024]{1,2,0:T(8,128)(2,1)}), bf16[4,128,1024]{1,2,0:T(8,128)(2,1)S(1)}, u32[]{:S(2)}, u32[]{:S(2)}) async-start(bf16[4,128,1024]{1,2,0:T(8,128)(2,1)} %broadcast_in_dim.127), calls=%async_computation.14 | async-start | bytes 2097152 | tf_op jit(solution)/shard_map/all_to_all | solution.py:16
  877.9 35.7 %collective-permute-start.46 = (bf16[345,256]{0,1:T(8,128)(2,1)}, bf16[345,256]{0,1:T(8,128)(2,1)S(1)}, u32[]{:S(2)}, u32[]{:S(2)}) collective-permute-start(bf16[345,256]{0,1:T(8,128)(2,1)} %bitcast.91), channel_id=1, source_target_pairs={{12,0},{16,4},{20,8},{24,12},{28,16},{32,20},{36,24},{40,28},{44,3... | collective-permute-start | bytes 529928 | tf_op jit(solution)/shard_map/ppermute | solution.py:45
  895.0 27.3 %collective-permute-start.47 = (bf16[345,256]{0,1:T(8,128)(2,1)}, bf16[345,256]{0,1:T(8,128)(2,1)}, u32[]{:S(2)}, u32[]{:S(2)}) collective-permute-start(bf16[345,256]{0,1:T(8,128)(2,1)} %bitcast.92), channel_id=1, source_target_pairs={{0,12},{4,16},{8,20},{12,24},{16,28},{20,32},{24,36},{28,40},{32,4... | collective-permute-start | bytes 529928 | tf_op jit(solution)/shard_map/ppermute | solution.py:45
  910.8 28.7 %collective-permute-start.36 = (bf16[512,256]{0,1:T(8,128)(2,1)}, bf16[512,256]{0,1:T(8,128)(2,1)S(1)}, u32[]{:S(2)}, u32[]{:S(2)}) collective-permute-start(bf16[512,256]{0,1:T(8,128)(2,1)} %bitcast.79), channel_id=1, source_target_pairs={{4,0},{8,4},{12,8},{16,12},{20,16},{24,20},{28,24},{32,28},{36,32}... | collective-permute-start | bytes 786440 | tf_op jit(solution)/shard_map/ppermute | solution.py:45
  912.1 27.4 %collective-permute-start.38 = (bf16[512,256]{0,1:T(8,128)(2,1)}, bf16[512,256]{0,1:T(8,128)(2,1)}, u32[]{:S(2)}, u32[]{:S(2)}) collective-permute-start(bf16[512,256]{0,1:T(8,128)(2,1)} %bitcast.81), channel_id=1, source_target_pairs={{8,0},{12,4},{16,8},{20,12},{24,16},{28,20},{32,24},{36,28},{40,32... | collective-permute-start | bytes 786440 | tf_op jit(solution)/shard_map/ppermute | solution.py:45
  953.1 27.3 %all-to-all-start.15 = ((bf16[4,128,1024]{2,1,0:T(8,128)(2,1)}), bf16[4,128,1024]{2,1,0:T(8,128)(2,1)}, u32[]{:S(2)}, u32[]{:S(2)}) async-start(bf16[4,128,1024]{2,1,0:T(8,128)(2,1)} %bitcast.93), calls=%async_computation.15 | async-start | bytes 2097152 | tf_op jit(solution)/shard_map/all_to_all | solution.py:38
  957.5 173.6 %all-reduce.3.cloned.1.call-start = ((), (), s32[]{:S(2)}) async-start(), calls=%async_computation.17 | async-start | bytes 131072 | tf_op jit(solution)/shard_map/psum | solution.py:428
  983.9 289.2 %reduce-scatter.2.cloned.1.call-start = ((), (), s32[]{:S(2)}) async-start(), calls=%async_computation.18 | async-start | bytes 12976128 | tf_op jit(solution)/shard_map/reduce_scatter | solution.py:54
  (173 other events, 2533.7 us)
Sparse Core Ops, SparseCore 0:
  984.1 146.9 all-reduce.2
Sparse Core Ops, SparseCore 1:
  1013.6 259.5 reduce-scatter.1
where the time goes:
time: 1300 us; the launch traced here: 1290 us
  waiting for transfers between devices  280 us (22%)
  local copies, waits for them, and re-layouts  234 us (18%)
  starting transfers between devices  233 us (18%)
  matrix products  216 us (17%)
  blocking collectives  178 us (14%)
  other arithmetic  128 us (10%)
  between operations  18.4 us (1%)
    ppermute x48, starting transfers between devices, shifted(): lax.ppermute(value, axis, [(source, source + steps) for source in range(i...  193 us
    reduce_scatter x1, waiting for transfers between devices, one_scatter(): lax.psum_scatter(lines, axis, tiled=True).reshape(-1)  141 us
    psum x1, blocking collectives, shards(): vector_sums = lax.psum(vector_stack, ('dp', 'tensor'))  74.5 us
    all_to_all x4, blocking collectives, sum_at_owner(): lax.all_to_all(parts, axis, split_axis=0, concat_axis=0, tiled=True)  67.7 us
    all_to_all x6, waiting for transfers between devices, copy_for_each(): return lax.all_to_all(copies, axis, split_axis=0, concat_axis=0, tiled=True)  50.2 us
    convert_element_type x2, other arithmetic, attend_backward(): grad_scores = (probs * (grad_probs - inner)).astype(jnp.bfloat16)  46.4 us
    psum x1, waiting for transfers between devices, shards(): vector_sums = lax.psum(vector_stack, ('dp', 'tensor'))  39.6 us
    concatenate x4, local copies, waits for them, and re-layouts, shards(): vals_win = jnp.concatenate(lower_vals + [vals_own] + upper_vals, 0)  37.1 us
  transfers between devices with their start and end apart: 60, of which 12 were waited for; matrix products, arithmetic and copies ran while one was open for 16% of the time, Pallas kernels for 0%

commit v1 on v0

v1 whole, which is shorter than its diff:
```python
import functools

import jax
import jax.numpy as jnp
from jax import lax
from jax.experimental import pallas as pl
from jax.experimental.pallas import tpu as pltpu
from jax.sharding import PartitionSpec as P

MESH = pl.DeviceIdType.MESH
BF = jnp.bfloat16
F32 = jnp.float32
VM = pl.BlockSpec(memory_space=pltpu.VMEM)
SM = pl.BlockSpec(memory_space=pltpu.SMEM)

HEAD_DIM = 64
IMG_LEN = 1370
EPS = 1e-06
NEG = -1e30

R = 128
S = 512
D = 1024
LW = 256
HL = LW // HEAD_DIM
F = 1024
TOTAL = 16384
NDP = 32
FAR3 = 384
OWN0 = FAR3 + 2 * S
NW = 2 * OWN0 + S
QB = 256
KB = 256
NB = NW // KB
C = 2
RC = R // C
MB = 1 << 20


def mm(a, b):
    return jnp.dot(a, b, preferred_element_type=F32)


def mm_rt(a, b):
    return lax.dot_general(a, b, (((1,), (1,)), ((), ())), preferred_element_type=F32)


def mm_lt(a, b):
    return lax.dot_general(a, b, (((0,), (0,)), ((), ())), preferred_element_type=F32)


class Place:
    def __init__(self):
        self.t = lax.axis_index("tensor")
        self.core = lax.rem(self.t, 2)
        self.mate = self.t + 1 - 2 * self.core
        self.cp = lax.rem(self.t + 2, 4)
        self.own = pl.multiple_of(self.t * R, R)
        self.opp = pl.multiple_of(self.cp * R, R)
        self.near = pl.multiple_of((self.t - self.core) * R, 2 * R)
        self.far = pl.multiple_of(2 * R - self.near, 2 * R)
        self.dp = lax.axis_index("dp")
        self.up = lax.rem(self.dp + 1, NDP)
        self.dn = lax.rem(self.dp + NDP - 1, NDP)


def greet(devices):
    barrier = pltpu.get_barrier_semaphore()
    for device in devices:
        pl.semaphore_signal(barrier, inc=1, device_id=device, device_id_type=MESH)
    pl.semaphore_wait(barrier, len(devices))


class Wires:
    def __init__(self, send, recv):
        self.send, self.recv, self.count, self.open = send, recv, 0, []

    def push(self, src, dst, device):
        k = self.count
        self.count += 1
        copy = pltpu.make_async_remote_copy(
            src, dst, self.send.at[k], self.recv.at[k], device_id=device, device_id_type=MESH
        )
        copy.start()
        self.open.append(copy)
        return copy

    def left(self, copy):
        copy.wait_send()
        self.open = [c for c in self.open if c is not copy]

    def close(self):
        for copy in self.open:
            copy.wait_send()


AG_SEMS = 2 * C + 1
RS_SEMS = 2 * C + 1


class Gather:
    def __init__(self, wires, at, buf):
        self.wires, self.at, self.buf = wires, at, buf
        own = at.own
        self.across = []
        for c in range(C):
            part = buf.at[pl.ds(own + c * RC, RC)]
            self.across.append(wires.push(part, part, {"tensor": at.cp}))
        part = buf.at[pl.ds(own, R)]
        self.beside = wires.push(part, part, {"tensor": at.mate})

    def near(self):
        self.beside.wait_recv()

    def far(self):
        passed = []
        for c in range(C):
            self.across[c].wait_recv()
            part = self.buf.at[pl.ds(self.at.opp + c * RC, RC)]
            passed.append(self.wires.push(part, part, {"tensor": self.at.mate}))
        for copy in passed:
            copy.wait_recv()


class Scatter:
    def __init__(self, wires, at, part, send1, recv1, send2, recv2, send3, recv3):
        self.wires, self.at, self.part = wires, at, part
        self.send1, self.recv1 = send1, recv1
        self.send2, self.recv2 = send2, recv2
        self.send3, self.recv3 = send3, recv3

    def far(self):
        at, wires = self.at, self.wires
        first = []
        for c in range(C):
            rows = pl.ds(c * RC, RC)
            src = pl.ds(pl.multiple_of((1 - at.core) * R + c * RC, RC), RC)
            self.send1[rows, :] = self.part[src, :].astype(BF)
            first.append(wires.push(self.send1.at[rows], self.recv1.at[rows], {"tensor": at.mate}))
        self.second = []
        for c in range(C):
            rows = pl.ds(c * RC, RC)
            src = pl.ds(pl.multiple_of(at.core * R + c * RC, RC), RC)
            first[c].wait_recv()
            total = self.part[src, :] + self.recv1[rows, :].astype(F32)
            self.send2[rows, :] = total.astype(BF)
            self.second.append(
                wires.push(self.send2.at[rows], self.recv2.at[rows], {"tensor": at.cp})
            )

    def near(self):
        at = self.at
        src = pl.ds(pl.multiple_of((1 - at.core) * R, R), R)
        self.send3[...] = self.part[src, :].astype(BF)
        self.third = self.wires.push(self.send3, self.recv3, {"tensor": at.mate})

    def total(self):
        self.third.wait_recv()
        for copy in self.second:
            copy.wait_recv()
        own = self.part[pl.ds(pl.multiple_of(self.at.core * R, R), R), :]
        return own + self.recv3[...].astype(F32) + self.recv2[...].astype(F32)


def scatter_scratch():
    return [pltpu.VMEM((2 * R, D), F32)] + [pltpu.VMEM((R, D), BF) for _ in range(6)]


def normalized(v):
    centered = v - jnp.mean(v, axis=-1, keepdims=True)
    scale = lax.rsqrt(jnp.mean(centered * centered, axis=-1, keepdims=True) + EPS)
    return centered * scale, scale


def norm_back(v, gain, grad):
    x_hat, scale = normalized(v)
    u = grad * gain
    grad_in = scale * (
        u
        - jnp.mean(u, axis=-1, keepdims=True)
        - x_hat * jnp.mean(u * x_hat, axis=-1, keepdims=True)
    )
    return (
        grad_in,
        jnp.sum(grad * x_hat, axis=0, keepdims=True),
        jnp.sum(grad, axis=0, keepdims=True),
    )


def call(kernel, name, cid, ins, outs, scratch, sems, limit=56, specs=None):
    shapes = [jax.ShapeDtypeStruct(shape, dtype) for shape, dtype in outs]
    extra = []
    if sems:
        extra = [pltpu.SemaphoreType.DMA((sems,)), pltpu.SemaphoreType.DMA((sems,))]
    params = dict(vmem_limit_bytes=limit * MB)
    if cid is not None:
        params.update(collective_id=cid, has_side_effects=True)
    return pl.pallas_call(
        kernel,
        out_shape=shapes,
        in_specs=specs or [VM] * len(ins),
        out_specs=[VM] * len(outs),
        scratch_shapes=list(scratch) + extra,
        compiler_params=pltpu.CompilerParams(**params),
        name=name,
    )(*ins)


def inward_kernel(h, gain, bias, b3, w, rows, q, win, ss, rs):
    at = Place()
    wires = Wires(ss, rs)
    greet([{"tensor": at.mate}, {"tensor": at.cp}, {"dp": at.up}, {"dp": at.dn}])
    x_hat, _ = normalized(h[...])
    rows[pl.ds(at.own, R), :] = (x_hat * gain[...] + bias[...]).astype(BF)
    gather = Gather(wires, at, rows)

    def project(first):
        out = (mm(rows[pl.ds(first, 2 * R), :], w[...]) + b3[...]).astype(BF)
        q[pl.ds(first, 2 * R), :] = out[:, :LW]
        win[pl.ds(OWN0 + first, 2 * R), :] = out[:, LW:]

    def hop(base, step, device):
        src = win.at[pl.ds(pl.multiple_of(base, 128), 2 * R)]
        dst = win.at[pl.ds(pl.multiple_of(base + step, 128), 2 * R)]
        return wires.push(src, dst, {"dp": device})

    gather.near()
    project(at.near)
    up1, dn1 = [hop(OWN0 + at.near, -S, at.up)], [hop(OWN0 + at.near, S, at.dn)]
    gather.far()
    project(at.far)
    up1.append(hop(OWN0 + at.far, -S, at.up))
    dn1.append(hop(OWN0 + at.far, S, at.dn))
    up2, dn2 = [], []
    for k, first in enumerate((at.near, at.far)):
        up1[k].wait_recv()
        up2.append(hop(OWN0 - S + first, -S, at.up))
        dn1[k].wait_recv()
        dn2.append(hop(OWN0 + S + first, S, at.dn))
    for copy in up2:
        copy.wait_recv()
    up3 = wires.push(
        win.at[pl.ds(OWN0 - S - FAR3, FAR3)], win.at[pl.ds(0, FAR3)], {"dp": at.up}
    )
    for copy in dn2:
        copy.wait_recv()
    dn3 = wires.push(
        win.at[pl.ds(OWN0 + 2 * S, FAR3)], win.at[pl.ds(OWN0 + 3 * S, FAR3)], {"dp": at.dn}
    )
    up3.wait_recv()
    dn3.wait_recv()
    wires.close()


def inward(cid, h, gain, bias, b3, w):
    return call(
        inward_kernel,
        "inward%d" % cid,
        cid,
        [h, gain, bias, b3, w],
        [((S, D), BF), ((S, LW), BF), ((NW, 2 * LW), BF)],
        [],
        AG_SEMS + 10,
    )


def ids_of(position, starts):
    total = jnp.zeros_like(position)
    for k in range(starts.shape[0]):
        first = starts[k]
        total += (position >= first).astype(jnp.int32)
        total += (position >= first + IMG_LEN).astype(jnp.int32)
    return jnp.where((position >= 0) & (position < TOTAL), total, -1)


def key_range(base, block, starts):
    first = base + block * QB
    last = first + QB - 1
    low, high = jnp.int32(0), jnp.int32(TOTAL)
    for k in range(starts.shape[0]):
        for edge in (starts[k], starts[k] + IMG_LEN):
            low = jnp.where(edge <= first, jnp.maximum(low, edge), low)
            high = jnp.where(edge > last, jnp.minimum(high, edge), high)
    low_block = lax.div(jnp.maximum(low - base + OWN0, 0), KB)
    high_block = lax.div(jnp.minimum(high - base + OWN0, NW) + KB - 1, KB)
    return low_block, high_block


def spread_heads(value, out):
    lane = lax.broadcasted_iota(jnp.int32, (QB, LW), 1)
    for head in range(HL):
        mine = (lane >= head * HEAD_DIM) & (lane < (head + 1) * HEAD_DIM)
        out[pl.ds(head * QB, QB), :] = jnp.where(mine, value, 0.0).astype(BF)


def pick_heads(parts):
    lane = lax.broadcasted_iota(jnp.int32, (QB, LW), 1)
    out = parts(0)
    for head in range(1, HL):
        out = jnp.where(lane >= head * HEAD_DIM, parts(head), out)
    return out


def attend_kernel(starts, q, win, out, lt, qm, sbuf, high, low, acc):
    base = lax.axis_index("dp") * S
    for block in range(S // QB):
        spread_heads(q[pl.ds(block * QB, QB), :].astype(F32) * 0.125, qm)
        qid = ids_of(
            base + block * QB + lax.broadcasted_iota(jnp.int32, (QB, 1), 0), starts
        )
        first, end = key_range(base, block, starts)
        high[...] = jnp.full_like(high, NEG)
        low[...] = jnp.zeros_like(low)
        acc[...] = jnp.zeros_like(acc)

        def scores(kb, carry):
            at = pl.multiple_of(kb * KB, KB)
            s = mm_rt(qm[...], win[pl.ds(at, KB), :LW])
            kid = ids_of(base - OWN0 + at + lax.broadcasted_iota(jnp.int32, (1, KB), 1), starts)
            bias = jnp.where(qid == kid, 0.0, NEG)
            for head in range(HL):
                rows = pl.ds(head * QB, QB)
                one = s[head * QB : (head + 1) * QB, :] + bias
                sbuf[kb, rows, :] = one
                high[rows, :] = jnp.maximum(
                    high[rows, :], jnp.maximum(one[:, :128], one[:, 128:])
                )
            return carry

        lax.fori_loop(first, end, scores, 0)
        top = jnp.max(high[...], axis=1, keepdims=True)
        high[...] = jnp.broadcast_to(top, high.shape)

        def values(kb, carry):
            at = pl.multiple_of(kb * KB, KB)
            v = win[pl.ds(at, KB), LW:]
            for head in range(HL):
                rows = pl.ds(head * QB, QB)
                p = jnp.exp(sbuf[kb, rows, :] - high[rows, :1])
                low[rows, :] += p[:, :128] + p[:, 128:]
                acc[rows, :] += mm(p.astype(BF), v)
            return carry

        lax.fori_loop(first, end, values, 0)
        total = jnp.sum(low[...], axis=1, keepdims=True)
        inv = 1.0 / total
        out[pl.ds(block * QB, QB), :] = pick_heads(
            lambda head: acc[pl.ds(head * QB, QB), :] * inv[head * QB : (head + 1) * QB, :]
        ).astype(BF)
        flat = jnp.transpose(jnp.broadcast_to(top + jnp.log(total), (HL * QB, 128)))
        lt[pl.ds(block * 8, 8), :] = flat[:8, :]


def attend(starts, q, win):
    return call(
        attend_kernel,
        "attend",
        None,
        [starts, q, win],
        [((S, LW), BF), ((8 * (S // QB), HL * QB), F32)],
        [
            pltpu.VMEM((HL * QB, LW), BF),
            pltpu.VMEM((NB, HL * QB, KB), F32),
            pltpu.VMEM((HL * QB, 128), F32),
            pltpu.VMEM((HL * QB, 128), F32),
            pltpu.VMEM((HL * QB, LW), F32),
        ],
        0,
        specs=[SM, VM, VM],
    )


def attend_back_kernel(starts, q, win, grad, att, lt, dq, dwin, qm, gm, dqa, dkv):
    base = lax.axis_index("dp") * S
    dkv[...] = jnp.zeros_like(dkv)
    head_row = lax.broadcasted_iota(jnp.int32, (8, LW), 0)
    lane_head = lax.div(lax.broadcasted_iota(jnp.int32, (8, LW), 1), HEAD_DIM)
    sums = (head_row == lane_head).astype(F32)
    for block in range(S // QB):
        rows = pl.ds(block * QB, QB)
        spread_heads(q[rows, :].astype(F32) * 0.125, qm)
        grad_rows = grad[rows, :].astype(F32)
        spread_heads(grad_rows, gm)
        both = grad_rows * att[rows, :].astype(F32)
        by_head = lax.dot_general(
            sums,
            both,
            (((1,), (1,)), ((), ())),
            precision=lax.Precision.HIGHEST,
            preferred_element_type=F32,
        )
        inner = jnp.concatenate([by_head[h : h + 1, :] for h in range(HL)], axis=1)
        logs = lt[pl.ds(block * 8, 1), :]
        qid = ids_of(
            base + block * QB + lax.broadcasted_iota(jnp.int32, (1, QB), 1), starts
        )
        first, end = key_range(base, block, starts)
        dqa[...] = jnp.zeros_like(dqa)

        def one(kb, carry):
            at = pl.multiple_of(kb * KB, KB)
            keys = win[pl.ds(at, KB), :LW]
            vals = win[pl.ds(at, KB), LW:]
            kid = ids_of(base - OWN0 + at + lax.broadcasted_iota(jnp.int32, (KB, 1), 0), starts)
            bias = jnp.where(kid == qid, 0.0, NEG)
            st = mm_rt(keys, qm[...])
            dp = mm_rt(vals, gm[...])
            p = jnp.exp((st - logs) + jnp.concatenate([bias] * HL, axis=1))
            ds = (p * (dp - inner)).astype(BF)
            dkv[pl.ds(at, KB), LW:] += mm(p.astype(BF), gm[...])
            dkv[pl.ds(at, KB), :LW] += mm(ds, qm[...])
            dqa[...] += mm_lt(ds, keys)
            return carry

        lax.fori_loop(first, end, one, 0)
        dq[rows, :] = (pick_heads(lambda head: dqa[pl.ds(head * QB, QB), :]) * 0.125).astype(BF)
    dwin[...] = dkv[...].astype(BF)


def attend_back(starts, q, win, grad, att, lt):
    return call(
        attend_back_kernel,
        "attend_back",
        None,
        [starts, q, win, grad, att, lt],
        [((S, LW), BF), ((NW, 2 * LW), BF)],
        [
            pltpu.VMEM((HL * QB, LW), BF),
            pltpu.VMEM((HL * QB, LW), BF),
            pltpu.VMEM((HL * QB, LW), F32),
            pltpu.VMEM((NW, 2 * LW), F32),
        ],
        0,
        specs=[SM] + [VM] * 5,
    )


def outward_kernel(
    att, h, wp, sc, ob, gain, bias, w1, b1, w2,
    mixed, br1, br2, nxt, rows, act, slope,
    part, sa, ra, sb, rb, s3, r3, sa2, ra2, sb2, rb2, s32, r32, ss, rs,
):
    at = Place()
    wires = Wires(ss, rs)
    greet([{"tensor": at.mate}, {"tensor": at.cp}])
    scatter = Scatter(wires, at, part, sa, ra, sb, rb, s3, r3)
    part[...] = mm(att[pl.ds(at.far, 2 * R), :], wp[...])
    scatter.far()
    part[...] = mm(att[pl.ds(at.near, 2 * R), :], wp[...])
    scatter.near()
    one = scatter.total()
    br1[...] = one
    mix = h[...] + sc[0:1, :] * (one + ob[0:1, :])
    mixed[...] = mix
    x_hat, _ = normalized(mix)
    rows[pl.ds(at.own, R), :] = (x_hat * gain[...] + bias[...]).astype(BF)
    gather = Gather(wires, at, rows)

    def hidden(first):
        x = rows[pl.ds(first, 2 * R), :]
        for j in range(F // 256):
            cols = pl.ds(j * 256, 256)
            pre = mm(x, w1[:, cols]) + b1[:, cols]
            half = 0.5 * (1.0 + lax.erf(pre * (0.5**0.5)))
            act[pl.ds(first, 2 * R), cols] = (pre * half).astype(BF)
            bell = jnp.exp(-0.5 * pre * pre) * 0.3989422804014327
            slope[pl.ds(first, 2 * R), cols] = (half + pre * bell).astype(BF)

    gather.near()
    hidden(at.near)
    gather.far()
    hidden(at.far)
    scatter = Scatter(wires, at, part, sa2, ra2, sb2, rb2, s32, r32)
    part[...] = mm(act[pl.ds(at.far, 2 * R), :], w2[...])
    scatter.far()
    part[...] = mm(act[pl.ds(at.near, 2 * R), :], w2[...])
    scatter.near()
    two = scatter.total()
    br2[...] = two
    nxt[...] = mix + sc[1:2, :] * (two + ob[1:2, :])
    wires.close()


def outward(cid, att, h, wp, sc, ob, gain, bias, w1, b1, w2):
    one = ((R, D), F32)
    return call(
        outward_kernel,
        "outward%d" % cid,
        cid,
        [att, h, wp, sc, ob, gain, bias, w1, b1, w2],
        [one, one, one, one, ((S, D), BF), ((S, F), BF), ((S, F), BF)],
        scatter_scratch() + scatter_scratch()[1:],
        AG_SEMS + 2 * RS_SEMS,
    )


def back_out_kernel(
    g, sc, ob, gain, mixed, br1, br2, act, slope, rows, att, w1, w2, wp,
    gmix, gatt, dw2, dw1, dwp, vec, fb,
    g2, gp, g1, part, sa, ra, sb, rb, s3, r3, ss, rs,
):
    at = Place()
    wires = Wires(ss, rs)
    greet([{"tensor": at.mate}, {"tensor": at.cp}])
    grad = g[...]
    g2[pl.ds(at.own, R), :] = (grad * sc[1:2, :]).astype(BF)
    gather = Gather(wires, at, g2)
    vec[0:1, :] = jnp.sum(grad * (br2[...] + ob[1:2, :]), axis=0, keepdims=True)
    vec[1:2, :] = sc[1:2, :] * jnp.sum(grad, axis=0, keepdims=True)

    def hidden(first):
        x = g2[pl.ds(first, 2 * R), :]
        for j in range(F // 256):
            cols = pl.ds(j * 256, 256)
            up = mm_rt(x, w2[cols, :])
            gp[pl.ds(first, 2 * R), cols] = (
                up * slope[pl.ds(first, 2 * R), cols].astype(F32)
            ).astype(BF)

    gather.near()
    hidden(at.near)
    gather.far()
    hidden(at.far)
    scatter = Scatter(wires, at, part, sa, ra, sb, rb, s3, r3)
    part[...] = mm_rt(gp[pl.ds(at.far, 2 * R), :], w1[...])
    scatter.far()
    part[...] = mm_rt(gp[pl.ds(at.near, 2 * R), :], w1[...])
    scatter.near()
    for j in range(D // 256):
        cols = pl.ds(j * 256, 256)
        dw2[cols, :] = mm_lt(g2[:, cols], act[...]).astype(BF)
        dw1[cols, :] = mm_lt(rows[:, cols], gp[...]).astype(BF)
    fb[...] = jnp.broadcast_to(jnp.sum(gp[...].astype(F32), axis=0, keepdims=True), fb.shape)
    grad_in, grad_gain, grad_shift = norm_back(mixed[...], gain[...], scatter.total())
    mix = grad + grad_in
    gmix[...] = mix
    g1[pl.ds(at.own, R), :] = (mix * sc[0:1, :]).astype(BF)
    gather = Gather(wires, at, g1)
    vec[2:3, :] = grad_gain
    vec[3:4, :] = grad_shift
    vec[4:5, :] = jnp.sum(mix * (br1[...] + ob[0:1, :]), axis=0, keepdims=True)
    vec[5:6, :] = sc[0:1, :] * jnp.sum(mix, axis=0, keepdims=True)
    vec[6:8, :] = jnp.zeros((2, D), F32)
    gather.near()
    gatt[pl.ds(at.near, 2 * R), :] = mm_rt(g1[pl.ds(at.near, 2 * R), :], wp[...]).astype(BF)
    gather.far()
    gatt[pl.ds(at.far, 2 * R), :] = mm_rt(g1[pl.ds(at.far, 2 * R), :], wp[...]).astype(BF)
    dwp[...] = mm_lt(g1[...], att[...]).astype(BF)
    wires.close()


def back_out(cid, *ins):
    return call(
        back_out_kernel,
        "back_out%d" % cid,
        cid,
        list(ins),
        [
            ((R, D), F32), ((S, LW), BF), ((D, F), BF), ((D, F), BF), ((D, LW), BF),
            ((8, D), F32), ((8, F), F32),
        ],
        [pltpu.VMEM((S, D), BF), pltpu.VMEM((S, F), BF), pltpu.VMEM((S, D), BF)]
        + scatter_scratch(),
        2 * AG_SEMS + RS_SEMS,
    )


def back_in_kernel(
    dq, dwin, rows, w, gmix, h, gain,
    g, dw, vec, qb,
    proj, da, db, dc, ua, ub, uc, sdb, sdc, sub, suc, part, sa, ra, sb, rb, s3, r3, ss, rs,
):
    at = Place()
    wires = Wires(ss, rs)
    greet([{"tensor": at.mate}, {"tensor": at.cp}, {"dp": at.up}, {"dp": at.dn}])
    up, dn = {"dp": at.up}, {"dp": at.dn}
    cut = FAR3 - 256
    d1 = [
        wires.push(dwin.at[pl.ds(0, cut)], da.at[pl.ds(0, cut)], dn),
        wires.push(dwin.at[pl.ds(cut, 256)], da.at[pl.ds(cut, 256)], dn),
    ]
    top = NW - FAR3
    u1 = [
        wires.push(dwin.at[pl.ds(top, 256)], ua.at[pl.ds(0, 256)], up),
        wires.push(dwin.at[pl.ds(top + 256, cut)], ua.at[pl.ds(256, cut)], up),
    ]
    proj[:, :LW] = dq[...]
    dw[:, :LW] = mm_lt(rows[...], dq[...]).astype(BF)

    def plus(first, count, other):
        return (dwin[pl.ds(first, count), :].astype(F32) + other.astype(F32)).astype(BF)

    d2, u2 = [], []
    low2, high2 = FAR3, OWN0 + 2 * S
    d1[0].wait_recv()
    sdb[0 : 256 - cut, :] = dwin[pl.ds(low2, 256 - cut), :]
    sdb[256 - cut : 256, :] = plus(low2 + 256 - cut, cut, da[0:cut, :])
    d2.append(wires.push(sdb.at[pl.ds(0, 256)], db.at[pl.ds(0, 256)], dn))
    u1[0].wait_recv()
    sub[0:256, :] = plus(high2, 256, ua[0:256, :])
    u2.append(wires.push(sub.at[pl.ds(0, 256)], ub.at[pl.ds(0, 256)], up))
    d1[1].wait_recv()
    sdb[256:512, :] = plus(low2 + 256, 256, da[cut : cut + 256, :])
    d2.append(wires.push(sdb.at[pl.ds(256, 256)], db.at[pl.ds(256, 256)], dn))
    u1[1].wait_recv()
    sub[256 : 256 + cut, :] = plus(high2 + 256, cut, ua[256 : 256 + cut, :])
    sub[256 + cut : 512, :] = dwin[pl.ds(high2 + 256 + cut, 256 - cut), :]
    u2.append(wires.push(sub.at[pl.ds(256, 256)], ub.at[pl.ds(256, 256)], up))
    d3, u3 = [], []
    for k in range(2):
        half = pl.ds(256 * k, 256)
        d2[k].wait_recv()
        sdc[half, :] = plus(OWN0 - S + 256 * k, 256, db[half, :])
        d3.append(wires.push(sdc.at[half], dc.at[half], dn))
        u2[k].wait_recv()
        suc[half, :] = plus(OWN0 + S + 256 * k, 256, ub[half, :])
        u3.append(wires.push(suc.at[half], uc.at[half], up))
    for k in range(2):
        half = pl.ds(256 * k, 256)
        d3[k].wait_recv()
        u3[k].wait_recv()
        own = dwin[pl.ds(OWN0 + 256 * k, 256), :].astype(F32)
        proj[half, LW:] = (own + dc[half, :].astype(F32) + uc[half, :].astype(F32)).astype(BF)
    scatter = Scatter(wires, at, part, sa, ra, sb, rb, s3, r3)
    part[...] = mm_rt(proj[pl.ds(at.far, 2 * R), :], w[...])
    scatter.far()
    part[...] = mm_rt(proj[pl.ds(at.near, 2 * R), :], w[...])
    scatter.near()
    dw[:, LW:] = mm_lt(rows[...], proj[:, LW:]).astype(BF)
    qb[...] = jnp.broadcast_to(jnp.sum(proj[...].astype(F32), axis=0, keepdims=True), qb.shape)
    grad_in, grad_gain, grad_shift = norm_back(h[...], gain[...], scatter.total())
    g[...] = gmix[...] + grad_in
    vec[0:1, :] = grad_gain
    vec[1:2, :] = grad_shift
    vec[2:8, :] = jnp.zeros((6, D), F32)
    wires.close()


def back_in(cid, *ins):
    whole = pltpu.VMEM((S, 2 * LW), BF)
    three = pltpu.VMEM((FAR3, 2 * LW), BF)
    return call(
        back_in_kernel,
        "back_in%d" % cid,
        cid,
        list(ins),
        [((R, D), F32), ((D, 3 * LW), BF), ((8, D), F32), ((8, 3 * LW), F32)],
        [pltpu.VMEM((S, 3 * LW), BF), three, whole, whole, three, whole, whole]
        + [whole] * 4
        + scatter_scratch(),
        RS_SEMS + 12,
    )


class Ring:
    def __init__(self, wires, chunk, me, up, dn, bufs):
        self.wires, self.chunk, self.me, self.up, self.dn = wires, chunk, me, up, dn
        self.from_dn, self.from_up, self.send_up, self.send_dn, self.last_dn, self.last_up = bufs

    def half(self, ref, k):
        width = ref.shape[-1] // 2
        return ref.at[..., pl.ds(k * width, width)]

    def position(self, step):
        return lax.rem(self.me + step, 4)

    def start(self):
        push, chunk = self.wires.push, self.chunk
        p1, p2, p3 = self.position(1), self.position(2), self.position(3)
        self.a = push(chunk(p2, 0), self.from_dn, self.up)
        self.b = push(chunk(p2, 1), self.from_up, self.dn)
        self.c = push(chunk(p1, 1), self.half(self.last_dn, 1), self.up)
        self.d = push(chunk(p3, 0), self.half(self.last_up, 0), self.dn)

    def forward(self):
        push, chunk = self.wires.push, self.chunk
        p1, p3 = self.position(1), self.position(3)
        self.a.wait_recv()
        self.send_up[...] = (chunk(p1, 0)[...].astype(F32) + self.from_dn[...].astype(F32)).astype(
            BF
        )
        self.e = push(self.send_up, self.half(self.last_dn, 0), self.up)
        self.b.wait_recv()
        self.send_dn[...] = (chunk(p3, 1)[...].astype(F32) + self.from_up[...].astype(F32)).astype(
            BF
        )
        self.f = push(self.send_dn, self.half(self.last_up, 1), self.dn)

    def finish(self, out):
        for copy in (self.c, self.d, self.e, self.f):
            copy.wait_recv()
        for k in range(2):
            part = self.chunk(self.me, k)[...].astype(F32)
            part += self.half(self.last_dn, k)[...].astype(F32)
            part += self.half(self.last_up, k)[...].astype(F32)
            self.half(out, k)[...] = part.astype(out.dtype)


WIDTHS = (F, F, 3 * LW, LW)
MODES = (0, 1, 0, 1, 1, 0, 1, 0)


def ring_scratch(lead, width):
    half = pltpu.VMEM((*lead, width // 2), BF)
    full = pltpu.VMEM((*lead, width), BF)
    return [half, half, half, half, full, full]


PIECE_SCRATCH = 14


def piece_scratch(mode, width):
    lead = (4, 2, R // 4) if mode == 0 else (2, 4, R // 4)
    small = (2, R // 4)
    return (
        ring_scratch(lead, width)
        + [pltpu.VMEM((*lead, width), BF)]
        + ring_scratch(small, width)
        + [pltpu.VMEM((*small, width), BF)]
    )


def reduce_kernel(*refs):
    count = 2 * len(WIDTHS)
    ins, refs = refs[:count], refs[count:]
    va1, va0, vb1, vb0, fb1, fb0, qb1, qb0 = refs[:8]
    outs, vout = refs[8 : 8 + count], refs[8 + count]
    refs = refs[9 + count :]
    scratch = [refs[k * (PIECE_SCRATCH + 1) : (k + 1) * (PIECE_SCRATCH + 1)] for k in range(count)]
    vec, vmate, vcp, vy, vx, vz, ss, rs = refs[count * (PIECE_SCRATCH + 1) :]
    t = lax.axis_index("tensor")
    i = lax.axis_index("dp")
    y = lax.rem(i, 4)
    x = lax.div(i, 8)
    zh = lax.rem(lax.div(i, 4), 2)
    mate = {"tensor": t + 1 - 2 * lax.rem(t, 2)}
    cp = {"tensor": lax.rem(t + 2, 4)}
    along_y = [{"dp": i - y + lax.rem(y + k, 4)} for k in (1, 2, 3)]
    along_x = [{"dp": lax.rem(i + 8 * k, 32)} for k in (1, 2, 3)]
    beyond = {"dp": i + 4 - 8 * zh}
    greet([mate, cp, beyond] + along_y + along_x)
    wires = Wires(ss, rs)
    push = wires.push

    vec[...] = jnp.zeros_like(vec)
    for k, (va, vb) in enumerate(((va0, vb0), (va1, vb1))):
        vec[8 * k : 8 * k + 6, :] = va[0:6, :]
        vec[8 * k + 6 : 8 * k + 8, :] = vb[0:2, :]
    vec[16:17, :] = fb0[0:1, :]
    vec[17:18, :] = fb1[0:1, :]
    vec[18:19, : 3 * LW] = qb0[0:1, :]
    vec[19:20, : 3 * LW] = qb1[0:1, :]

    rings, second, rests = [], [], []
    for k in range(count):
        w, sc, mode = ins[k], scratch[k], MODES[k]
        width = w.shape[-1] // 2

        def wide(pos, half, w=w, mode=mode, width=width):
            cols = pl.ds(half * width, width)
            return w.at[:, :, pos, :, cols] if mode == 0 else w.at[pos, :, :, :, cols]

        def narrow(pos, half, acc=sc[6], mode=mode, width=width):
            cols = pl.ds(half * width, width)
            return acc.at[pos, :, :, cols] if mode == 0 else acc.at[:, pos, :, cols]

        ring_y = (y, along_y[0], along_y[2])
        ring_x = (x, along_x[0], along_x[2])
        one, two = (ring_y, ring_x) if mode == 0 else (ring_x, ring_y)
        rings.append(Ring(wires, wide, *one, sc[0:6]))
        second.append(Ring(wires, narrow, *two, sc[7:13]))

    to_mate = push(vec.at[pl.ds(0, 16)], vmate, mate)
    for ring in rings:
        ring.start()
    to_mate.wait_recv()
    wires.left(to_mate)
    vec[0:16, :] = vec[0:16, :] + vmate[...]
    to_cp = push(vec.at[pl.ds(0, 16)], vcp, cp)
    for ring in rings[:4]:
        ring.forward()
    to_cp.wait_recv()
    wires.left(to_cp)
    vy[y] = vec[...]
    vy[y, 0:16, :] = vec[0:16, :] + vcp[...]
    sent = [push(vy.at[y], vy.at[y], device) for device in along_y]
    for ring in rings[4:]:
        ring.forward()
    for k in range(4):
        rings[k].finish(scratch[k][6])
        second[k].start()
    for copy in sent:
        copy.wait_recv()
    vx[x] = vy[0] + vy[1] + vy[2] + vy[3]
    sent = [push(vx.at[x], vx.at[x], device) for device in along_x]
    for k in range(4, count):
        rings[k].finish(scratch[k][6])
        second[k].start()
    for ring in second:
        ring.forward()
    for copy in sent:
        copy.wait_recv()
    vec[...] = vx[0] + vx[1] + vx[2] + vx[3]
    to_z = push(vec, vz, beyond)
    rests = []
    for k in range(count):
        acc, rest = scratch[k][13], scratch[k][14]
        second[k].finish(acc)
        rests.append(push(acc.at[1 - zh], rest, beyond))
    to_z.wait_recv()
    vout[...] = vec[...] + vz[...]
    for k in range(count):
        acc, rest = scratch[k][13], scratch[k][14]
        rests[k].wait_recv()
        outs[k][...] = acc[zh].astype(F32) + rest[...].astype(F32)
    wires.close()


def reduce_all(cid, weights, vectors):
    ins = [w.reshape(4, 2, 4, R // 4, w.shape[-1]) for w in weights]
    widths = [w.shape[-1] for w in weights]
    scratch = []
    for width, mode in zip(widths, MODES):
        scratch += piece_scratch(mode, width) + [pltpu.VMEM((R // 4, width), BF)]
    rows = (24, D)
    scratch += [pltpu.VMEM(rows, F32), pltpu.VMEM((16, D), F32), pltpu.VMEM((16, D), F32)]
    scratch += [pltpu.VMEM((4, *rows), F32), pltpu.VMEM((4, *rows), F32), pltpu.VMEM(rows, F32)]
    return call(
        reduce_kernel,
        "reduce_all",
        cid,
        ins + list(vectors),
        [((R // 4, width), F32) for width in widths] + [(rows, F32)],
        scratch,
        13 * len(widths) + 9,
        limit=60,
    )


def shards(
    tokens_in,
    image_starts,
    norm_gain,
    norm_bias,
    qkv_weight,
    qv_bias,
    proj_weight,
    out_bias,
    layer_scale,
    fc1_weight,
    fc1_bias,
    fc2_weight,
    out_grad,
):
    layers = qkv_weight.shape[0]
    hidden = tokens_in.astype(F32)
    saved = []
    for l in range(layers):
        w_qkv = qkv_weight[l].reshape(D, 3 * LW)
        b3 = jnp.concatenate([qv_bias[l, 0], jnp.zeros((LW,), F32), qv_bias[l, 1]])[None]
        rows_one, q, win = inward(
            2 * l, hidden, norm_gain[l, 0:1], norm_bias[l, 0:1], b3, w_qkv
        )
        att, lt = attend(image_starts, q, win)
        mixed, br1, br2, nxt, rows_two, act, slope = outward(
            2 * l + 1, att, hidden, proj_weight[l], layer_scale[l], out_bias[l],
            norm_gain[l, 1:2], norm_bias[l, 1:2], fc1_weight[l], fc1_bias[l : l + 1],
            fc2_weight[l],
        )
        saved.append((w_qkv, rows_one, q, win, att, lt, hidden, mixed, br1, br2, rows_two, act, slope))
        hidden = nxt
    grad = out_grad
    weights, va, vb, fbs, qbs = [], [], [], [], []
    for l in reversed(range(layers)):
        w_qkv, rows_one, q, win, att, lt, h, mixed, br1, br2, rows_two, act, slope = saved[l]
        gmix, gatt, dw2, dw1, dwp, vec_a, fb = back_out(
            4 + 2 * l, grad, layer_scale[l], out_bias[l], norm_gain[l, 1:2], mixed, br1, br2,
            act, slope, rows_two, att, fc1_weight[l], fc2_weight[l], proj_weight[l],
        )
        dq, dwin = attend_back(image_starts, q, win, gatt, att, lt)
        grad, dwq, vec_b, qb = back_in(
            5 + 2 * l, dq, dwin, rows_one, w_qkv, gmix, h, norm_gain[l, 0:1]
        )
        weights += [dw2, dw1, dwq, dwp]
        va.append(vec_a)
        vb.append(vec_b)
        fbs.append(fb)
        qbs.append(qb)
    *sums, vec = reduce_all(8, weights, va + vb + fbs + qbs)
    g2_1, g1_1, gq_1, gp_1, g2_0, g1_0, gq_0, gp_0 = sums
    rows = vec[:16].reshape(2, 8, D)
    return (
        hidden.astype(BF),
        grad,
        jnp.stack([rows[:, 6], rows[:, 2]], 1),
        jnp.stack([rows[:, 7], rows[:, 3]], 1),
        jnp.stack([gq_0, gq_1]).reshape(2, R // 4, 3, LW),
        jnp.stack([vec[18:20, :LW], vec[18:20, 2 * LW : 3 * LW]], 1),
        jnp.stack([gp_0.T, gp_1.T]),
        jnp.stack([rows[:, 5], rows[:, 1]], 1),
        jnp.stack([rows[:, 4], rows[:, 0]], 1),
        jnp.stack([g1_0, g1_1]),
        vec[16:18],
        jnp.stack([g2_0.T, g2_1.T]),
    )


def solution(mesh):
    return jax.shard_map(
        shards,
        mesh=mesh,
        in_specs=(
            P(("dp", "tensor"), None),
            P(),
            P(),
            P(),
            P(None, None, None, "tensor"),
            P(None, None, "tensor"),
            P(None, "tensor", None),
            P(),
            P(),
            P(None, None, "tensor"),
            P(None, "tensor"),
            P(None, "tensor", None),
            P(("dp", "tensor"), None),
        ),
        out_specs=(
            P(("dp", "tensor"), None),
            P(("dp", "tensor"), None),
            P(),
            P(),
            P(None, "dp", None, "tensor"),
            P(None, None, "tensor"),
            P(None, "tensor", "dp"),
            P(),
            P(),
            P(None, "dp", "tensor"),
            P(None, "tensor"),
            P(None, "tensor", "dp"),
        ),
        check_vma=False,
    )
```

time: 1300 us -> 609 us (0.47)
  Pallas kernels: 0 us -> 566 us
  waiting for transfers between devices: 280 us -> 0 us
  starting transfers between devices: 233 us -> 0 us
  matrix products: 216 us -> 0 us
  local copies, waits for them, and re-layouts: 234 us -> 29.4 us
  blocking collectives: 178 us -> 0 us
  other arithmetic: 128 us -> 8.99 us
  between operations: 18.4 us -> 1 us
    pallas_call x0 -> x13, Pallas kernels: none -> 566 us  [call(): pl.pallas_call(kernel, out_shape=shapes, in_specs=specs or [VM] * len(ins...]
    dot_general x36 -> x0, matrix products: 216 us -> none  [the longest x2 33.8 us: attend_backward(): jnp.einsum('qhe,khe->hqk', grad_heads, val_heads, preferred_element_type=...]
    ppermute x48 -> x0, starting transfers between devices: 193 us -> none  [shifted(): lax.ppermute(value, axis, [(source, source + steps) for source in range(i...]
    reduce_scatter x1 -> x0, waiting for transfers between devices: 141 us -> none  [one_scatter(): lax.psum_scatter(lines, axis, tiled=True).reshape(-1)]
    all_to_all x6 -> x0, blocking collectives: 103 us -> none  [the longest x4 67.7 us: sum_at_owner(): lax.all_to_all(parts, axis, split_axis=0, concat_axis=0, tiled=True)]
    psum x1 -> x0, blocking collectives: 74.5 us -> none  [shards(): vector_sums = lax.psum(vector_stack, ('dp', 'tensor'))]
    all_to_all x10 -> x0, waiting for transfers between devices: 72.9 us -> none  [the longest x6 50.2 us: copy_for_each(): return lax.all_to_all(copies, axis, split_axis=0, concat_axis=0, tiled=True)]
    concatenate x8 -> x0, local copies, waits for them, and re-layouts: 60 us -> none  [the longest x4 37.1 us: shards(): vals_win = jnp.concatenate(lower_vals + [vals_own] + upper_vals, 0)]
  transfers between devices with their start and end apart: 60 -> 0, of which waited for: 12 -> 0; matrix products, arithmetic and copies ran while one was open for 16% -> 0% of each run, Pallas kernels for 0% -> 0%
where the time goes in v1:
time: 609 us; the launch traced here: 605 us
  Pallas kernels  566 us (93%)
  local copies, waits for them, and re-layouts  29.4 us (5%)
  other arithmetic  8.99 us (1%)
    pallas_call x13, Pallas kernels, call(): pl.pallas_call(kernel, out_shape=shapes, in_specs=specs or [VM] * len(ins...  566 us

profile of v1, /device:TPU:0, one launch (start us, length us, event | category | flops | bytes accessed | tf_op | source)
XLA Modules:
  0.0 605.4 jit_solution(12849050350320784389)
XLA Ops:
  2.6 1.4 fusion.4
  4.0 1.4 slice_bitcast_fusion.11
  6.8 1.8 convert_element_type.6.h
  8.5 2.3 slice_bitcast_fusion.4
  10.8 3.3 fusion.2
  14.1 1.7 copy.39
  15.8 1.6 copy.33.w
  18.3 1.6 copy.31.w
  19.9 81.9 %inward0.1 = (bf16[512,1024]{1,0:T(8,128)(2,1)}, bf16[512,256]{1,0:T(8,128)(2,1)}, bf16[3328,512]{1,0:T(8,128)(2,1)}) custom-call(f32[128,1024]{1,0:T(8,128)} %convert_element_type.6.h, f32[1,1024]{1,0:T(1,128)} %get-tuple-element.193.gain, f32[1,1024]{1,0:T(1,128)} %get-tuple-element.174.bias, f32[1,768]{1,0:T(1,128)} %broadcast_in_dim.6.b3, ...), custom_call_target="tpu_custom_call" | custom-call | tf_op jit(solution)/shard_map/inward0/pallas_call | solution.py:198
  101.8 15.3 %attend.2 = (bf16[512,256]{1,0:T(8,128)(2,1)}, f32[16,1024]{1,0:T(8,128)}) custom-call(s32[11]{0:T(128)} %starts.7, bf16[512,256]{1,0:T(8,128)(2,1)} %get-tuple-element.71.q, bf16[3328,512]{1,0:T(8,128)(2,1)} %get-tuple-element.72.win), custom_call_target="tpu_custom_call" | custom-call | tf_op jit(solution)/shard_map/attend/pallas_call | solution.py:198
  117.1 4.9 slice_bitcast_fusion
  122.0 34.0 %outward1.1 = (f32[128,1024]{1,0:T(8,128)}, f32[128,1024]{1,0:T(8,128)}, f32[128,1024]{1,0:T(8,128)}, f32[128,1024]{1,0:T(8,128)}, bf16[512,1024]{1,0:T(8,128)(2...) custom-call(bf16[512,256]{1,0:T(8,128)(2,1)} %get-tuple-element.73.att, f32[128,1024]{1,0:T(8,128)} %convert_element_type.6.h, ...), custom_call_target="tpu_custom_call" | custom-call | tf_op jit(solution)/shard_map/outward1/pallas_call | solution.py:198
  156.1 76.3 %inward2.1 = (bf16[512,1024]{1,0:T(8,128)(2,1)}, bf16[512,256]{1,0:T(8,128)(2,1)}, bf16[3328,512]{1,0:T(8,128)(2,1)}) custom-call(f32[128,1024]{1,0:T(8,128)} %get-tuple-element.74.h, f32[1,1024]{1,0:T(1,128)} %get-tuple-element.192.gain, f32[1,1024]{1,0:T(1,128)} %get-tuple-element.175.bias, f32[1,768]{1,0:T(1,128)} %broadcast_in_dim.7.b3, ...), custom_call_target="tpu_custom_call" | custom-call | tf_op jit(solution)/shard_map/inward2/pallas_call | solution.py:198
  232.3 15.0 %attend.3 = (bf16[512,256]{1,0:T(8,128)(2,1)}, f32[16,1024]{1,0:T(8,128)}) custom-call(s32[11]{0:T(128)} %starts.7, bf16[512,256]{1,0:T(8,128)(2,1)} %get-tuple-element.75.q, bf16[3328,512]{1,0:T(8,128)(2,1)} %get-tuple-element.76.win), custom_call_target="tpu_custom_call" | custom-call | tf_op jit(solution)/shard_map/attend/pallas_call | solution.py:198
  247.4 33.7 %outward3.1 = (f32[128,1024]{1,0:T(8,128)}, f32[128,1024]{1,0:T(8,128)}, f32[128,1024]{1,0:T(8,128)}, f32[128,1024]{1,0:T(8,128)}, bf16[512,1024]{1,0:T(8,128)(2...) custom-call(bf16[512,256]{1,0:T(8,128)(2,1)} %get-tuple-element.77.att, f32[128,1024]{1,0:T(8,128)} %get-tuple-element.74.h, ...), custom_call_target="tpu_custom_call" | custom-call | tf_op jit(solution)/shard_map/outward3/pallas_call | solution.py:198
  281.1 1.8 convert_element_type.7
  282.8 32.6 %back_out6.1 = (f32[128,1024]{1,0:T(8,128)}, bf16[512,256]{1,0:T(8,128)(2,1)}, bf16[1024,1024]{1,0:T(8,128)(2,1)}, bf16[1024,1024]{1,0:T(8,128)(2,1)}, bf16[1024...) custom-call(f32[128,1024]{1,0:T(8,128)} %g.1, f32[2,1024]{1,0:T(2,128)} %get-tuple-element.199.sc, ...), custom_call_target="tpu_custom_call" | custom-call | tf_op jit(solution)/shard_map/back_out6/pallas_call | solution.py:198
  315.5 22.5 %attend_back.2 = (bf16[512,256]{1,0:T(8,128)(2,1)}, bf16[3328,512]{1,0:T(8,128)(2,1)}) custom-call(s32[11]{0:T(128)} %starts.7, bf16[512,256]{1,0:T(8,128)(2,1)} %get-tuple-element.75.q, bf16[3328,512]{1,0:T(8,128)(2,1)} %get-tuple-element.76.win, bf16[512,256]{1,0:T(8,128)(2,1)} %get-tuple-element.85.grad, bf16[512,256]{1,0:T(8,128)(2,1)} %get-tuple-element.77.att, ...), custom_call_target="tpu_custom_call" | custom-call | tf_op jit(solution)/shard_map/attend_back/pallas_call | solution.py:198
  337.9 56.0 %back_in7.1 = (f32[128,1024]{1,0:T(8,128)}, bf16[1024,768]{1,0:T(8,128)(2,1)}, f32[8,1024]{1,0:T(8,128)}, f32[8,768]{1,0:T(8,128)}) custom-call(bf16[512,256]{1,0:T(8,128)(2,1)} %get-tuple-element.87.dq, bf16[3328,512]{1,0:T(8,128)(2,1)} %get-tuple-element.88.dwin, bf16[512,1024]{1,0:T(8,128)(2,1)} %get-tuple-element.89.rows, bf16[1024,768]{1,0:T(8,128)(2,1)} %copy.33.w, ...), custom_call_target="tpu_custom_call" | custom-call | tf_op jit(solution)/shard_map/back_in7/pallas_call | solution.py:198
  393.9 33.1 %back_out4.1 = (f32[128,1024]{1,0:T(8,128)}, bf16[512,256]{1,0:T(8,128)(2,1)}, bf16[1024,1024]{1,0:T(8,128)(2,1)}, bf16[1024,1024]{1,0:T(8,128)(2,1)}, bf16[1024...) custom-call(f32[128,1024]{1,0:T(8,128)} %get-tuple-element.91.g, f32[2,1024]{1,0:T(2,128)} %get-tuple-element.198.sc, ...), custom_call_target="tpu_custom_call" | custom-call | tf_op jit(solution)/shard_map/back_out4/pallas_call | solution.py:198
  427.0 22.3 %attend_back.3 = (bf16[512,256]{1,0:T(8,128)(2,1)}, bf16[3328,512]{1,0:T(8,128)(2,1)}) custom-call(s32[11]{0:T(128)} %starts.7, bf16[512,256]{1,0:T(8,128)(2,1)} %get-tuple-element.71.q, bf16[3328,512]{1,0:T(8,128)(2,1)} %get-tuple-element.72.win, bf16[512,256]{1,0:T(8,128)(2,1)} %get-tuple-element.98.grad, bf16[512,256]{1,0:T(8,128)(2,1)} %get-tuple-element.73.att, ...), custom_call_target="tpu_custom_call" | custom-call | tf_op jit(solution)/shard_map/attend_back/pallas_call | solution.py:198
  449.3 55.8 %back_in5.1 = (f32[128,1024]{1,0:T(8,128)}, bf16[1024,768]{1,0:T(8,128)(2,1)}, f32[8,1024]{1,0:T(8,128)}, f32[8,768]{1,0:T(8,128)}) custom-call(bf16[512,256]{1,0:T(8,128)(2,1)} %get-tuple-element.100.dq, bf16[3328,512]{1,0:T(8,128)(2,1)} %get-tuple-element.101.dwin, bf16[512,1024]{1,0:T(8,128)(2,1)} %get-tuple-element.102.rows, bf16[1024,768]{1,0:T(8,128)(2,1)} %copy.31.w, ...), custom_call_target="tpu_custom_call" | custom-call | tf_op jit(solution)/shard_map/back_in5/pallas_call | solution.py:198
  505.1 87.6 %reduce_all.1 = (f32[32,1024]{1,0:T(8,128)}, f32[32,1024]{1,0:T(8,128)}, f32[32,768]{1,0:T(8,128)}, f32[32,256]{1,0:T(8,128)}, f32[32,1024]{1,0:T(8,128)}, /*ind...) custom-call(bf16[4,2,4,32,1024]{4,3,2,1,0:T(8,128)(2,1)} %bitcast.72, ...), custom_call_target="tpu_custom_call" | custom-call | tf_op jit(solution)/shard_map/reduce_all/pallas_call | solution.py:198
  599.9 1.4 pad_maximum_fusion.3
  (36 shorter events, 15.2 us)
Async XLA Ops:
  19.9 97.2 %copy-start = (bf16[2,1024,1024]{2,1,0:T(8,128)(2,1)S(1)}, bf16[2,1024,1024]{2,1,0:T(8,128)(2,1)}, u32[]{:S(2)}) copy-start(bf16[2,1024,1024]{2,1,0:T(8,128)(2,1)} %param.24) | copy-start | bytes 12582916
  592.7 10.3 %copy-start.4 = (f32[32,1024]{1,0:T(8,128)S(1)}, f32[32,1024]{1,0:T(8,128)}, u32[]{:S(2)}) copy-start(f32[32,1024]{1,0:T(8,128)} %get-tuple-element.127) | copy-start | bytes 393220
  592.7 10.3 %copy-start.5 = (f32[32,1024]{1,0:T(8,128)S(1)}, f32[32,1024]{1,0:T(8,128)}, u32[]{:S(2)}) copy-start(f32[32,1024]{1,0:T(8,128)} %get-tuple-element.126) | copy-start | bytes 393220
  592.7 11.0 %copy-start.2 = (f32[32,1024]{1,0:T(8,128)S(1)}, f32[32,1024]{1,0:T(8,128)}, u32[]{:S(2)}) copy-start(f32[32,1024]{1,0:T(8,128)} %get-tuple-element.129) | copy-start | bytes 393220
  592.8 11.0 %copy-start.3 = (f32[32,1024]{1,0:T(8,128)S(1)}, f32[32,1024]{1,0:T(8,128)}, u32[]{:S(2)}) copy-start(f32[32,1024]{1,0:T(8,128)} %get-tuple-element.128) | copy-start | bytes 393220
  592.8 11.7 %copy-start.1 = (f32[128,1024]{1,0:T(8,128)S(1)}, f32[128,1024]{1,0:T(8,128)}, u32[]{:S(2)}) copy-start(f32[128,1024]{1,0:T(8,128)} %get-tuple-element.213) | copy-start | bytes 1572868

commit v2 on v1

v2 whole, which is shorter than its diff:
```python
import functools

import jax
import jax.numpy as jnp
from jax import lax
from jax.experimental import pallas as pl
from jax.experimental.pallas import tpu as pltpu
from jax.sharding import PartitionSpec as P

MESH = pl.DeviceIdType.MESH
BF = jnp.bfloat16
F32 = jnp.float32
VM = pl.BlockSpec(memory_space=pltpu.VMEM)
SM = pl.BlockSpec(memory_space=pltpu.SMEM)
ANY = pl.BlockSpec(memory_space=pl.ANY)

HEAD_DIM = 64
IMG_LEN = 1370
EPS = 1e-06
NEG = -1e30

R = 128
S = 512
D = 1024
LW = 256
HL = LW // HEAD_DIM
F = 1024
TOTAL = 16384
NDP = 32
FAR3 = 384
OWN0 = FAR3 + 2 * S
NW = 2 * OWN0 + S
QB = 256
KB = 256
NB = NW // KB
C = 2
RC = R // C
MB = 1 << 20


def mm(a, b):
    return jnp.dot(a, b, preferred_element_type=F32)


def mm_rt(a, b):
    return lax.dot_general(a, b, (((1,), (1,)), ((), ())), preferred_element_type=F32)


def mm_lt(a, b):
    return lax.dot_general(a, b, (((0,), (0,)), ((), ())), preferred_element_type=F32)


class Place:
    def __init__(self):
        self.t = lax.axis_index("tensor")
        self.core = lax.rem(self.t, 2)
        self.mate = self.t + 1 - 2 * self.core
        self.cp = lax.rem(self.t + 2, 4)
        self.own = pl.multiple_of(self.t * R, R)
        self.opp = pl.multiple_of(self.cp * R, R)
        self.near = pl.multiple_of((self.t - self.core) * R, 2 * R)
        self.far = pl.multiple_of(2 * R - self.near, 2 * R)
        self.dp = lax.axis_index("dp")
        self.up = lax.rem(self.dp + 1, NDP)
        self.dn = lax.rem(self.dp + NDP - 1, NDP)


def greet(devices):
    barrier = pltpu.get_barrier_semaphore()
    for device in devices:
        pl.semaphore_signal(barrier, inc=1, device_id=device, device_id_type=MESH)
    pl.semaphore_wait(barrier, len(devices))


class Wires:
    def __init__(self, send, recv):
        self.send, self.recv, self.count, self.open = send, recv, 0, []

    def push(self, src, dst, device):
        k = self.count
        self.count += 1
        copy = pltpu.make_async_remote_copy(
            src, dst, self.send.at[k], self.recv.at[k], device_id=device, device_id_type=MESH
        )
        copy.start()
        self.open.append(copy)
        return copy

    def left(self, copy):
        copy.wait_send()
        self.open = [c for c in self.open if c is not copy]

    def close(self):
        for copy in self.open:
            copy.wait_send()


class Chain:
    def __init__(self, wires, at, up, relay):
        self.wires, self.at, self.relay = wires, at, relay
        y = lax.rem(at.dp, 4)
        self.edge = (y == 3) if up else (y == 0)
        self.plain = jnp.logical_not(self.edge)
        self.device = at.up if up else at.dn
        self.items = []

    def send(self, src, dst, partner_dst=None, when=True, partner_when=True):
        wires, at = self.wires, self.at
        slot = self.relay.at[len(self.items)]
        k = wires.count
        wires.count += 2

        def copy(source, target, n, device):
            return lambda: pltpu.make_async_remote_copy(
                source, target, wires.send.at[n], wires.recv.at[n],
                device_id=device, device_id_type=MESH,
            )

        direct = copy(src, dst, k, {"dp": self.device})
        first = copy(src, slot, k + 1, {"tensor": at.cp})
        target = dst if partner_dst is None else partner_dst
        second = copy(slot, target, k, {"dp": self.device, "tensor": at.cp})
        pl.when(self.plain & when)(lambda: direct().start())
        pl.when(self.edge & when)(lambda: first().start())
        item = (direct, first, second, when, partner_when)
        self.items.append(item)
        return item

    def hand_on(self, item):
        _, first, second, _, partner_when = item

        @pl.when(self.edge & partner_when)
        def _():
            first().wait_recv()
            second().start()

    def arrive(self, item):
        pl.when(item[3])(lambda: item[0]().wait_recv())

    def close(self):
        for direct, first, second, when, partner_when in self.items:
            pl.when(self.plain & when)(lambda c=direct: c().wait_send())
            pl.when(self.edge & when)(lambda c=first: c().wait_send())
            pl.when(self.edge & partner_when)(lambda c=second: c().wait_send())


class Line:
    def __init__(self, wires, device):
        self.wires, self.device = wires, device

    def send(self, src, dst):
        return self.wires.push(src, dst, self.device)

    def arrive(self, copy):
        copy.wait_recv()


def chain_partners(at):
    return [
        {"tensor": at.mate},
        {"tensor": at.cp},
        {"dp": at.up},
        {"dp": at.dn},
        {"dp": at.up, "tensor": at.cp},
        {"dp": at.dn, "tensor": at.cp},
    ]


AG_SEMS = 2 * C + 1
RS_SEMS = 2 * C + 1


class Gather:
    def __init__(self, wires, at, buf):
        self.wires, self.at, self.buf = wires, at, buf
        own = at.own
        self.across = []
        for c in range(C):
            part = buf.at[pl.ds(own + c * RC, RC)]
            self.across.append(wires.push(part, part, {"tensor": at.cp}))
        part = buf.at[pl.ds(own, R)]
        self.beside = wires.push(part, part, {"tensor": at.mate})

    def near(self):
        self.beside.wait_recv()

    def far(self):
        passed = []
        for c in range(C):
            self.across[c].wait_recv()
            part = self.buf.at[pl.ds(self.at.opp + c * RC, RC)]
            passed.append(self.wires.push(part, part, {"tensor": self.at.mate}))
        for copy in passed:
            copy.wait_recv()


class Scatter:
    def __init__(self, wires, at, part, send1, recv1, send2, recv2, send3, recv3):
        self.wires, self.at, self.part = wires, at, part
        self.send1, self.recv1 = send1, recv1
        self.send2, self.recv2 = send2, recv2
        self.send3, self.recv3 = send3, recv3

    def far(self):
        at, wires = self.at, self.wires
        first = []
        for c in range(C):
            rows = pl.ds(c * RC, RC)
            src = pl.ds(pl.multiple_of((1 - at.core) * R + c * RC, RC), RC)
            self.send1[rows, :] = self.part[src, :].astype(BF)
            first.append(wires.push(self.send1.at[rows], self.recv1.at[rows], {"tensor": at.mate}))
        self.second = []
        for c in range(C):
            rows = pl.ds(c * RC, RC)
            src = pl.ds(pl.multiple_of(at.core * R + c * RC, RC), RC)
            first[c].wait_recv()
            total = self.part[src, :] + self.recv1[rows, :].astype(F32)
            self.send2[rows, :] = total.astype(BF)
            self.second.append(
                wires.push(self.send2.at[rows], self.recv2.at[rows], {"tensor": at.cp})
            )

    def near(self):
        at = self.at
        src = pl.ds(pl.multiple_of((1 - at.core) * R, R), R)
        self.send3[...] = self.part[src, :].astype(BF)
        self.third = self.wires.push(self.send3, self.recv3, {"tensor": at.mate})

    def total(self):
        self.third.wait_recv()
        for copy in self.second:
            copy.wait_recv()
        own = self.part[pl.ds(pl.multiple_of(self.at.core * R, R), R), :]
        return own + self.recv3[...].astype(F32) + self.recv2[...].astype(F32)


def scatter_scratch():
    return [pltpu.VMEM((2 * R, D), F32)] + [pltpu.VMEM((R, D), BF) for _ in range(6)]


def fetch(src, dst, sem):
    copy = pltpu.make_async_copy(src, dst, sem)
    copy.start()
    return copy


def fetch_qkv(layer, w, buf, ls):
    return [
        fetch(w.at[layer, k], buf.at[:, pl.ds(k * LW, LW)], ls.at[k]) for k in range(3)
    ]


def normalized(v):
    centered = v - jnp.mean(v, axis=-1, keepdims=True)
    scale = lax.rsqrt(jnp.mean(centered * centered, axis=-1, keepdims=True) + EPS)
    return centered * scale, scale


def norm_back(v, gain, grad):
    x_hat, scale = normalized(v)
    u = grad * gain
    grad_in = scale * (
        u
        - jnp.mean(u, axis=-1, keepdims=True)
        - x_hat * jnp.mean(u * x_hat, axis=-1, keepdims=True)
    )
    return (
        grad_in,
        jnp.sum(grad * x_hat, axis=0, keepdims=True),
        jnp.sum(grad, axis=0, keepdims=True),
    )


def call(kernel, name, cid, ins, outs, scratch, sems, limit, specs=None, local=0, out_specs=None):
    shapes = [jax.ShapeDtypeStruct(shape, dtype) for shape, dtype in outs]
    extra = []
    if sems:
        extra = [pltpu.SemaphoreType.DMA((sems,)), pltpu.SemaphoreType.DMA((sems,))]
    if local:
        extra.append(pltpu.SemaphoreType.DMA((local,)))
    params = dict(vmem_limit_bytes=limit * MB)
    if cid is not None:
        params.update(collective_id=cid, has_side_effects=True)
    return pl.pallas_call(
        kernel,
        out_shape=shapes,
        in_specs=specs or [VM] * len(ins),
        out_specs=out_specs or [VM] * len(outs),
        scratch_shapes=list(scratch) + extra,
        compiler_params=pltpu.CompilerParams(**params),
        name=name,
    )(*ins)


def inward_kernel(layer, h, gain, bias, b2, w_hbm, rows, q, win, w, relay, ss, rs, ls):
    at = Place()
    wires = Wires(ss, rs)
    loads = fetch_qkv(layer, w_hbm, w, ls)
    x_hat, _ = normalized(h[...].astype(F32))
    mine = (x_hat * gain[layer, 0:1, :] + bias[layer, 0:1, :]).astype(BF)
    greet(chain_partners(at))
    rows[pl.ds(at.own, R), :] = mine
    gather = Gather(wires, at, rows)

    def project(first):
        out = mm(rows[pl.ds(first, 2 * R), :], w[...])
        q[pl.ds(first, 2 * R), :] = (out[:, :LW] + b2[layer, 0:1, :]).astype(BF)
        win[pl.ds(OWN0 + first, 2 * R), :LW] = out[:, LW : 2 * LW].astype(BF)
        win[pl.ds(OWN0 + first, 2 * R), LW:] = (out[:, 2 * LW :] + b2[layer, 1:2, :]).astype(BF)

    def part(first):
        return win.at[pl.ds(pl.multiple_of(first, R), R)]

    offs = [at.near, at.near + R, at.far, at.far + R]
    others = offs[2:] + offs[:2]
    chain_up, chain_dn = Chain(wires, at, True, relay), Chain(wires, at, False, relay)
    ups, dns = {}, {}

    def hop(n, k):
        own, other = offs[k], others[k]
        low, high = OWN0 - n * S, OWN0 + n * S
        if n < 3:
            ups[n, k] = chain_up.send(part(low + S + own), part(low + own), part(low + other))
            dns[n, k] = chain_dn.send(part(high - S + own), part(high + own), part(high + other))
            return
        ups[n, k] = chain_up.send(
            part(low + S + own),
            part(jnp.maximum(low + own, 0)),
            part(jnp.maximum(low + other, 0)),
            own > 0,
            other > 0,
        )
        dns[n, k] = chain_dn.send(
            part(high - S + own),
            part(jnp.minimum(high + own, NW - R)),
            part(jnp.minimum(high + other, NW - R)),
            own < S - R,
            other < S - R,
        )

    def onward(n, *ks):
        for k in ks:
            chain_up.arrive(ups[n, k])
            chain_dn.arrive(dns[n, k])
            if n < 3:
                hop(n + 1, k)

    def hand_on(n, *ks):
        for k in ks:
            chain_up.hand_on(ups[n, k])
            chain_dn.hand_on(dns[n, k])

    for copy in loads:
        copy.wait()
    gather.near()
    project(at.near)
    hop(1, 0)
    hop(1, 1)
    gather.far()
    hand_on(1, 0, 1)
    project(at.far)
    hop(1, 2)
    hop(1, 3)
    onward(1, 0, 1)
    hand_on(1, 2, 3)
    hand_on(2, 0, 1)
    onward(1, 2, 3)
    onward(2, 0, 1)
    hand_on(2, 2, 3)
    hand_on(3, 0, 1)
    onward(2, 2, 3)
    hand_on(3, 2, 3)
    onward(3, 0, 1, 2, 3)
    chain_up.close()
    chain_dn.close()
    wires.close()


def inward(cid, layer, h, gain, bias, b2, w):
    return call(
        functools.partial(inward_kernel, layer),
        "inward%d" % layer,
        cid,
        [h, gain, bias, b2, w],
        [((S, D), BF), ((S, LW), BF), ((NW, 2 * LW), BF)],
        [pltpu.VMEM((D, 3 * LW), BF), pltpu.VMEM((12, R, 2 * LW), BF)],
        AG_SEMS + 48,
        limit=20,
        specs=[VM] * 4 + [ANY],
        local=3,
    )


def ids_of(position, starts):
    total = jnp.zeros_like(position)
    for k in range(starts.shape[0]):
        first = starts[k]
        total += (position >= first).astype(jnp.int32)
        total += (position >= first + IMG_LEN).astype(jnp.int32)
    return jnp.where((position >= 0) & (position < TOTAL), total, -1)


def key_range(base, block, starts):
    first = base + block * QB
    last = first + QB - 1
    low, high = jnp.int32(0), jnp.int32(TOTAL)
    for k in range(starts.shape[0]):
        for edge in (starts[k], starts[k] + IMG_LEN):
            low = jnp.where(edge <= first, jnp.maximum(low, edge), low)
            high = jnp.where(edge > last, jnp.minimum(high, edge), high)
    low_block = lax.div(jnp.maximum(low - base + OWN0, 0), KB)
    high_block = lax.div(jnp.minimum(high - base + OWN0, NW) + KB - 1, KB)
    return low_block, high_block


def spread_heads(value, out):
    lane = lax.broadcasted_iota(jnp.int32, (QB, LW), 1)
    for head in range(HL):
        mine = (lane >= head * HEAD_DIM) & (lane < (head + 1) * HEAD_DIM)
        out[pl.ds(head * QB, QB), :] = jnp.where(mine, value, 0.0).astype(BF)


def pick_heads(parts):
    lane = lax.broadcasted_iota(jnp.int32, (QB, LW), 1)
    out = parts(0)
    for head in range(1, HL):
        out = jnp.where(lane >= head * HEAD_DIM, parts(head), out)
    return out


def attend_kernel(starts, q, win, out, lt, qm, sbuf, high, low, acc):
    base = lax.axis_index("dp") * S
    for block in range(S // QB):
        spread_heads(q[pl.ds(block * QB, QB), :].astype(F32) * 0.125, qm)
        qid = ids_of(
            base + block * QB + lax.broadcasted_iota(jnp.int32, (QB, 1), 0), starts
        )
        first, end = key_range(base, block, starts)
        high[...] = jnp.full_like(high, NEG)
        low[...] = jnp.zeros_like(low)
        acc[...] = jnp.zeros_like(acc)

        def scores(kb, carry):
            at = pl.multiple_of(kb * KB, KB)
            s = mm_rt(qm[...], win[pl.ds(at, KB), :LW])
            kid = ids_of(base - OWN0 + at + lax.broadcasted_iota(jnp.int32, (1, KB), 1), starts)
            bias = jnp.where(qid == kid, 0.0, NEG)
            for head in range(HL):
                rows = pl.ds(head * QB, QB)
                one = s[head * QB : (head + 1) * QB, :] + bias
                sbuf[kb, rows, :] = one
                high[rows, :] = jnp.maximum(
                    high[rows, :], jnp.maximum(one[:, :128], one[:, 128:])
                )
            return carry

        lax.fori_loop(first, end, scores, 0)
        top = jnp.max(high[...], axis=1, keepdims=True)
        high[...] = jnp.broadcast_to(top, high.shape)

        def values(kb, carry):
            at = pl.multiple_of(kb * KB, KB)
            v = win[pl.ds(at, KB), LW:]
            for head in range(HL):
                rows = pl.ds(head * QB, QB)
                p = jnp.exp(sbuf[kb, rows, :] - high[rows, :1])
                low[rows, :] += p[:, :128] + p[:, 128:]
                acc[rows, :] += mm(p.astype(BF), v)
            return carry

        lax.fori_loop(first, end, values, 0)
        total = jnp.sum(low[...], axis=1, keepdims=True)
        inv = 1.0 / total
        out[pl.ds(block * QB, QB), :] = pick_heads(
            lambda head: acc[pl.ds(head * QB, QB), :] * inv[head * QB : (head + 1) * QB, :]
        ).astype(BF)
        flat = jnp.transpose(jnp.broadcast_to(top + jnp.log(total), (HL * QB, 128)))
        lt[pl.ds(block * 8, 8), :] = flat[:8, :]


def attend(starts, q, win):
    return call(
        attend_kernel,
        "attend",
        None,
        [starts, q, win],
        [((S, LW), BF), ((8 * (S // QB), HL * QB), F32)],
        [
            pltpu.VMEM((HL * QB, LW), BF),
            pltpu.VMEM((NB, HL * QB, KB), F32),
            pltpu.VMEM((HL * QB, 128), F32),
            pltpu.VMEM((HL * QB, 128), F32),
            pltpu.VMEM((HL * QB, LW), F32),
        ],
        0,
        limit=30,
        specs=[SM, VM, VM],
    )


def attend_back_kernel(starts, q, win, grad, att, lt, dq, dwin, qm, gm, dqa, dkv):
    base = lax.axis_index("dp") * S
    dkv[...] = jnp.zeros_like(dkv)
    head_row = lax.broadcasted_iota(jnp.int32, (8, LW), 0)
    lane_head = lax.div(lax.broadcasted_iota(jnp.int32, (8, LW), 1), HEAD_DIM)
    sums = (head_row == lane_head).astype(F32)
    for block in range(S // QB):
        rows = pl.ds(block * QB, QB)
        spread_heads(q[rows, :].astype(F32) * 0.125, qm)
        grad_rows = grad[rows, :].astype(F32)
        spread_heads(grad_rows, gm)
        both = grad_rows * att[rows, :].astype(F32)
        by_head = lax.dot_general(
            sums,
            both,
            (((1,), (1,)), ((), ())),
            precision=lax.Precision.HIGHEST,
            preferred_element_type=F32,
        )
        inner = jnp.concatenate([by_head[h : h + 1, :] for h in range(HL)], axis=1)
        logs = lt[pl.ds(block * 8, 1), :]
        qid = ids_of(
            base + block * QB + lax.broadcasted_iota(jnp.int32, (1, QB), 1), starts
        )
        first, end = key_range(base, block, starts)
        dqa[...] = jnp.zeros_like(dqa)

        def one(kb, carry):
            at = pl.multiple_of(kb * KB, KB)
            keys = win[pl.ds(at, KB), :LW]
            vals = win[pl.ds(at, KB), LW:]
            kid = ids_of(base - OWN0 + at + lax.broadcasted_iota(jnp.int32, (KB, 1), 0), starts)
            bias = jnp.where(kid == qid, 0.0, NEG)
            st = mm_rt(keys, qm[...])
            dp = mm_rt(vals, gm[...])
            p = jnp.exp((st - logs) + jnp.concatenate([bias] * HL, axis=1))
            ds = (p * (dp - inner)).astype(BF)
            dkv[pl.ds(at, KB), LW:] += mm(p.astype(BF), gm[...])
            dkv[pl.ds(at, KB), :LW] += mm(ds, qm[...])
            dqa[...] += mm_lt(ds, keys)
            return carry

        lax.fori_loop(first, end, one, 0)
        dq[rows, :] = (pick_heads(lambda head: dqa[pl.ds(head * QB, QB), :]) * 0.125).astype(BF)
    dwin[...] = dkv[...].astype(BF)


def attend_back(starts, q, win, grad, att, lt):
    return call(
        attend_back_kernel,
        "attend_back",
        None,
        [starts, q, win, grad, att, lt],
        [((S, LW), BF), ((NW, 2 * LW), BF)],
        [
            pltpu.VMEM((HL * QB, LW), BF),
            pltpu.VMEM((HL * QB, LW), BF),
            pltpu.VMEM((HL * QB, LW), F32),
            pltpu.VMEM((NW, 2 * LW), F32),
        ],
        0,
        limit=28,
        specs=[SM] + [VM] * 5,
    )


def outward_kernel(
    layer, att, h, sc, ob, gain, bias, b1, wp_hbm, w1_hbm, w2_hbm,
    mixed, br1, br2, nxt, rows, act, slope,
    wp, w1, w2, part, sa, ra, sb, rb, s3, r3, sa2, ra2, sb2, rb2, s32, r32, ss, rs, ls,
):
    at = Place()
    wires = Wires(ss, rs)
    load_p = fetch(wp_hbm.at[layer], wp, ls.at[0])
    load_1 = fetch(w1_hbm.at[layer], w1, ls.at[1])
    load_2 = fetch(w2_hbm.at[layer], w2, ls.at[2])
    greet([{"tensor": at.mate}, {"tensor": at.cp}])
    scatter = Scatter(wires, at, part, sa, ra, sb, rb, s3, r3)
    load_p.wait()
    part[...] = mm(att[pl.ds(at.far, 2 * R), :], wp[...])
    scatter.far()
    part[...] = mm(att[pl.ds(at.near, 2 * R), :], wp[...])
    scatter.near()
    one = scatter.total()
    br1[...] = one
    mix = h[...].astype(F32) + sc[layer, 0:1, :] * (one + ob[layer, 0:1, :])
    mixed[...] = mix
    x_hat, _ = normalized(mix)
    rows[pl.ds(at.own, R), :] = (x_hat * gain[layer, 1:2, :] + bias[layer, 1:2, :]).astype(BF)
    gather = Gather(wires, at, rows)

    def hidden(first):
        x = rows[pl.ds(first, 2 * R), :]
        for j in range(F // 256):
            cols = pl.ds(j * 256, 256)
            pre = mm(x, w1[:, cols]) + b1[layer : layer + 1, cols]
            half = 0.5 * (1.0 + lax.erf(pre * (0.5**0.5)))
            act[pl.ds(first, 2 * R), cols] = (pre * half).astype(BF)
            bell = jnp.exp(-0.5 * pre * pre) * 0.3989422804014327
            slope[pl.ds(first, 2 * R), cols] = (half + pre * bell).astype(BF)

    load_1.wait()
    gather.near()
    hidden(at.near)
    gather.far()
    hidden(at.far)
    load_2.wait()
    scatter = Scatter(wires, at, part, sa2, ra2, sb2, rb2, s32, r32)
    part[...] = mm(act[pl.ds(at.far, 2 * R), :], w2[...])
    scatter.far()
    part[...] = mm(act[pl.ds(at.near, 2 * R), :], w2[...])
    scatter.near()
    two = scatter.total()
    br2[...] = two
    nxt[...] = (mix + sc[layer, 1:2, :] * (two + ob[layer, 1:2, :])).astype(nxt.dtype)
    wires.close()


def outward(cid, layer, last, *ins):
    one = ((R, D), F32)
    return call(
        functools.partial(outward_kernel, layer),
        "outward%d" % layer,
        cid,
        list(ins),
        [one, one, one, ((R, D), last), ((S, D), BF), ((S, F), BF), ((S, F), BF)],
        [pltpu.VMEM((LW, D), BF), pltpu.VMEM((D, F), BF), pltpu.VMEM((F, D), BF)]
        + scatter_scratch()
        + scatter_scratch()[1:],
        AG_SEMS + 2 * RS_SEMS,
        limit=28,
        specs=[VM] * 7 + [ANY] * 3,
        local=3,
    )


def back_out_kernel(layer, carry, *refs):
    g, sc, ob, gain, mixed, br1, br2, act, slope, rows, att, w1_hbm, w2_hbm, wp_hbm = refs[:14]
    refs = refs[14:]
    given, refs = refs[: 3 * carry], refs[3 * carry :]
    gmix, gatt, dw2_hbm, dw1_hbm, dwp, vec, fb = refs[:7]
    refs = refs[7:]
    sums, refs = refs[: NP * carry], refs[NP * carry :]
    wp, w1, w2, dw2, dw1, g2, gp, g1, part, sa, ra, sb, rb, s3, r3 = refs[:15]
    bufs = refs[15:-3]
    ss, rs, ls = refs[-3:]
    at = Place()
    wires = Wires(ss, rs)
    load_2 = fetch(w2_hbm.at[layer], w2, ls.at[0])
    load_1 = fetch(w1_hbm.at[layer], w1, ls.at[1])
    load_p = fetch(wp_hbm.at[layer], wp, ls.at[2])
    rings = Rings()
    wide = Wide(wires, rings, given, bufs, ls, 5) if carry else None
    greet([{"tensor": at.mate}, {"tensor": at.cp}] + rings.next_to() * carry)
    grad = g[...]
    g2[pl.ds(at.own, R), :] = (grad * sc[layer, 1:2, :]).astype(BF)
    gather = Gather(wires, at, g2)
    if carry:
        wide.start(*range(NP))
    vec[0:1, :] = jnp.sum(grad * (br2[...] + ob[layer, 1:2, :]), axis=0, keepdims=True)
    vec[1:2, :] = sc[layer, 1:2, :] * jnp.sum(grad, axis=0, keepdims=True)

    def hidden(first):
        x = g2[pl.ds(first, 2 * R), :]
        for j in range(F // 256):
            cols = pl.ds(j * 256, 256)
            up = mm_rt(x, w2[cols, :])
            gp[pl.ds(first, 2 * R), cols] = (
                up * slope[pl.ds(first, 2 * R), cols].astype(F32)
            ).astype(BF)

    load_2.wait()
    gather.near()
    hidden(at.near)
    gather.far()
    hidden(at.far)
    load_1.wait()
    scatter = Scatter(wires, at, part, sa, ra, sb, rb, s3, r3)
    part[...] = mm_rt(gp[pl.ds(at.far, 2 * R), :], w1[...])
    scatter.far()
    part[...] = mm_rt(gp[pl.ds(at.near, 2 * R), :], w1[...])
    scatter.near()
    if carry:
        wide.forward(*range(NP))
    for j in range(D // 256):
        cols = pl.ds(j * 256, 256)
        dw2[cols, :] = mm_lt(g2[:, cols], act[...]).astype(BF)
    write_2 = fetch(dw2, dw2_hbm, ls.at[3])
    for j in range(D // 256):
        cols = pl.ds(j * 256, 256)
        dw1[cols, :] = mm_lt(rows[:, cols], gp[...]).astype(BF)
    write_1 = fetch(dw1, dw1_hbm, ls.at[4])
    fb[...] = jnp.broadcast_to(jnp.sum(gp[...].astype(F32), axis=0, keepdims=True), fb.shape)
    grad_in, grad_gain, grad_shift = norm_back(
        mixed[...], gain[layer, 1:2, :], scatter.total()
    )
    mix = grad + grad_in
    gmix[...] = mix
    g1[pl.ds(at.own, R), :] = (mix * sc[layer, 0:1, :]).astype(BF)
    gather = Gather(wires, at, g1)
    vec[2:3, :] = grad_gain
    vec[3:4, :] = grad_shift
    vec[4:5, :] = jnp.sum(mix * (br1[...] + ob[layer, 0:1, :]), axis=0, keepdims=True)
    vec[5:6, :] = sc[layer, 0:1, :] * jnp.sum(mix, axis=0, keepdims=True)
    vec[6:8, :] = jnp.zeros((2, D), F32)
    load_p.wait()
    gather.near()
    gatt[pl.ds(at.near, 2 * R), :] = mm_rt(g1[pl.ds(at.near, 2 * R), :], wp[...]).astype(BF)
    gather.far()
    gatt[pl.ds(at.far, 2 * R), :] = mm_rt(g1[pl.ds(at.far, 2 * R), :], wp[...]).astype(BF)
    dwp[...] = mm_lt(g1[...], att[...]).astype(BF)
    if carry:
        wide.finish(sums, *range(NP))
    write_2.wait()
    write_1.wait()
    wires.close()


def back_out(cid, layer, given, *ins):
    carry = int(bool(given))
    return call(
        functools.partial(back_out_kernel, layer, carry),
        "back_out%d" % layer,
        cid,
        [*ins, *given],
        [
            ((R, D), F32), ((S, LW), BF), ((D, F), BF), ((D, F), BF), ((D, LW), BF),
            ((8, D), F32), ((8, F), F32),
        ]
        + [wide_shape(width, mode) for _, _, width, mode in PIECES] * carry,
        [pltpu.VMEM((LW, D), BF), pltpu.VMEM((D, F), BF), pltpu.VMEM((F, D), BF)]
        + [pltpu.VMEM((D, F), BF), pltpu.VMEM((D, F), BF)]
        + [pltpu.VMEM((S, D), BF), pltpu.VMEM((S, F), BF), pltpu.VMEM((S, D), BF)]
        + scatter_scratch()
        + wide_scratch() * carry,
        2 * AG_SEMS + RS_SEMS + carry * 6 * NP,
        limit=30 + 20 * carry,
        specs=[VM] * 11 + [ANY] * (3 + 3 * carry),
        out_specs=[VM, VM, ANY, ANY, VM, VM, VM] + [VM] * (carry * NP),
        local=5 + carry * 3 * NP,
    )


def back_in_kernel(layer, last, *refs):
    dq, dwin, rows, gmix, h, gain, dwp, w_hbm = refs[:8]
    refs = refs[8:]
    if last:
        dw2, dw1 = refs[:2]
        accs1 = refs[2 : 2 + NP]
        va1, va0, vb1, fb1, fb0, qb1 = refs[2 + NP : 8 + NP]
        refs = refs[8 + NP :]
        g = refs[0]
        sums1, sums0 = refs[1 : 1 + NP], refs[1 + NP : 1 + 2 * NP]
        vout, dw, vec, qb = refs[1 + 2 * NP : 5 + 2 * NP]
        refs = refs[5 + 2 * NP :]
    else:
        g, dw, vec, qb = refs[:4]
        refs = refs[4:]
    w, proj, da, db, dc, ua, ub, uc, sdb, sdc, sub, suc = refs[:12]
    part, sa, ra, sb, rb, s3, r3 = refs[12:19]
    bufs = refs[19:-3]
    ss, rs, ls = refs[-3:]
    at = Place()
    wires = Wires(ss, rs)
    loads = fetch_qkv(layer, w_hbm, w, ls)
    partners = [{"tensor": at.mate}, {"tensor": at.cp}, {"dp": at.up}, {"dp": at.dn}]
    if last:
        rings = Rings()
        accs0, bufs = bufs[:NP], bufs[NP:]
        wide = Wide(wires, rings, (dw2, dw1, dw), bufs[: NP * WIDE_REFS], ls, 3)
        bufs = bufs[NP * WIDE_REFS :]
        narrow1 = Narrow(wires, rings, accs1, bufs[: NP * NARROW_REFS])
        bufs = bufs[NP * NARROW_REFS :]
        narrow0 = Narrow(wires, rings, accs0, bufs[: NP * NARROW_REFS])
        vectors = Vectors(wires, at, rings, bufs[NP * NARROW_REFS :])
        partners += [*rings.along_y, *rings.along_x, rings.other]
    greet(partners)
    chain_up, chain_dn = Line(wires, {"dp": at.up}), Line(wires, {"dp": at.dn})
    low3, low2, low1 = OWN0 - 3 * S, OWN0 - 2 * S, OWN0 - S
    high1, high2, high3 = OWN0 + S, OWN0 + 2 * S, OWN0 + 3 * S

    def chunk(ref, k, base=0):
        return ref.at[pl.ds(base + k * R, R)]

    def plus(base, k, other):
        mine = dwin[pl.ds(base + k * R, R), :].astype(F32)
        return (mine + other[pl.ds(k * R, R), :].astype(F32)).astype(BF)

    ups, dns = {}, {}

    def send(n, k, down, up):
        dns[n, k] = chain_dn.send(*down)
        ups[n, k] = chain_up.send(*up)

    def arrive(n, k):
        chain_dn.arrive(dns[n, k])
        chain_up.arrive(ups[n, k])

    def first(k):
        j = 3 - k
        send(
            1, k, (chunk(dwin, k, low3), chunk(da, k)), (chunk(dwin, j, high3), chunk(ua, j))
        )

    def second(k):
        j = 3 - k
        arrive(1, k)
        sdb[pl.ds(k * R, R), :] = plus(low2, k, da)
        sub[pl.ds(j * R, R), :] = plus(high2, j, ua)
        send(2, k, (chunk(sdb, k), chunk(db, k)), (chunk(sub, j), chunk(ub, j)))

    def third(k):
        j = 3 - k
        arrive(2, k)
        sdc[pl.ds(k * R, R), :] = plus(low1, k, db)
        suc[pl.ds(j * R, R), :] = plus(high1, j, ub)
        send(3, k, (chunk(sdc, k), chunk(dc, k)), (chunk(suc, j), chunk(uc, j)))

    for k in (1, 2, 3):
        first(k)
    send(2, 0, (chunk(dwin, 0, low2), chunk(db, 0)), (chunk(dwin, 3, high2), chunk(ub, 3)))
    def into(first, value):
        dw[:, :, :, :, pl.ds(first, value.shape[-1])] = as_blocks(value)

    proj[:, :LW] = dq[...]
    into(3 * LW, dwp[...])
    into(0, mm_lt(rows[...], dq[...]).astype(BF))
    for k in (1, 2, 3):
        second(k)
    for k in range(4):
        third(k)
    for k in range(4):
        arrive(3, k)
    if last:
        wide.start(0, 1)
    own = dwin[pl.ds(OWN0, S), :].astype(F32)
    proj[:, LW:] = (own + dc[...].astype(F32) + uc[...].astype(F32)).astype(BF)
    for copy in loads:
        copy.wait()
    scatter = Scatter(wires, at, part, sa, ra, sb, rb, s3, r3)
    part[...] = mm_rt(proj[pl.ds(at.far, 2 * R), :], w[...])
    scatter.far()
    part[...] = mm_rt(proj[pl.ds(at.near, 2 * R), :], w[...])
    scatter.near()
    into(LW, mm_lt(rows[...], proj[:, LW:]).astype(BF))
    if last:
        wide.start(2, 3)
        wide.forward(1)
        narrow1.start(*range(NP))
    qb[...] = jnp.broadcast_to(jnp.sum(proj[...].astype(F32), axis=0, keepdims=True), qb.shape)
    grad_in, grad_gain, grad_shift = norm_back(
        h[...].astype(F32), gain[layer, 0:1, :], scatter.total()
    )
    g[...] = gmix[...] + grad_in
    vec[0:1, :] = grad_gain
    vec[1:2, :] = grad_shift
    vec[2:8, :] = jnp.zeros((6, D), F32)
    if last:
        vectors.fill(((va0, vec, fb0, qb), (va1, vb1, fb1, qb1)))
        wide.forward(0)
        narrow1.forward(*range(NP))
        wide.finish(accs0, 1)
        narrow0.start(1)
        vectors.over_core()
        wide.forward(2, 3)
        narrow1.beyond(*range(NP))
        vectors.over_chip()
        wide.finish(accs0, 0)
        narrow0.start(0)
        narrow0.forward(1)
        vectors.over_y()
        wide.finish(accs0, 2, 3)
        narrow0.start(2, 3)
        narrow0.forward(0)
        vectors.over_x()
        narrow0.beyond(1)
        narrow0.forward(2, 3)
        narrow0.beyond(0, 2, 3)
        vectors.finish(vout)
        narrow1.finish(sums1)
        narrow0.finish(sums0)
    wires.close()


def back_in(cid, layer, final, *ins):
    last = bool(final)
    whole = pltpu.VMEM((S, 2 * LW), BF)
    blocks, eight, wide8 = (4, 2, 4, RP, 4 * LW), (8, D), (8, 3 * LW)
    outs = [((R, D), F32)]
    scratch = []
    if last:
        outs += reduced_shapes() * 2 + [(VEC, F32)]
        scratch += [pltpu.VMEM(blocks, BF), pltpu.VMEM(eight, F32), pltpu.VMEM(wide8, F32)]
    else:
        outs += [(blocks, BF), (eight, F32), (wide8, F32)]
    scratch += [pltpu.VMEM((D, 3 * LW), BF), pltpu.VMEM((S, 3 * LW), BF)]
    scratch += [whole] * 10 + scatter_scratch()
    if last:
        scratch += [pltpu.VMEM(*wide_shape(width, mode)) for _, _, width, mode in PIECES]
        scratch += wide_scratch() + narrow_scratch() * 2 + vector_scratch()
    return call(
        functools.partial(back_in_kernel, layer, last),
        "back_in%d" % layer,
        cid,
        [*ins, *final],
        outs,
        scratch,
        RS_SEMS + 22 + last * (6 * NP + 14 * NP + 9),
        limit=48 if last else 28,
        specs=[VM] * 7 + [ANY] + ([ANY] * 2 + [VM] * (NP + 6)) * last,
        local=3 + last * 3 * NP,
    )


class Ring:
    def __init__(self, wires, chunk, mine, side_up, side_dn, place, bufs):
        self.wires, self.chunk = wires, chunk
        self.mine, self.side_up, self.side_dn = mine, side_up, side_dn
        self.me, self.up, self.dn = place
        self.from_dn, self.from_up, self.send_up, self.send_dn, self.last_dn, self.last_up = bufs

    def half(self, ref, k):
        width = ref.shape[-1] // 2
        return ref.at[..., pl.ds(k * width, width)]

    def position(self, step):
        return lax.rem(self.me + step, 4)

    def start(self):
        push, chunk = self.wires.push, self.chunk
        p1, p2, p3 = self.position(1), self.position(2), self.position(3)
        self.a = push(chunk(p2, 0), self.from_dn, self.up)
        self.b = push(chunk(p2, 1), self.from_up, self.dn)
        self.c = push(chunk(p1, 1), self.half(self.last_dn, 1), self.up)
        self.d = push(chunk(p3, 0), self.half(self.last_up, 0), self.dn)

    def forward(self):
        push = self.wires.push
        self.a.wait_recv()
        total = self.side_up()[...].astype(F32) + self.from_dn[...].astype(F32)
        self.send_up[...] = total.astype(BF)
        self.e = push(self.send_up, self.half(self.last_dn, 0), self.up)
        self.b.wait_recv()
        total = self.side_dn()[...].astype(F32) + self.from_up[...].astype(F32)
        self.send_dn[...] = total.astype(BF)
        self.f = push(self.send_dn, self.half(self.last_up, 1), self.dn)

    def finish(self, out):
        for copy in (self.c, self.d, self.e, self.f):
            copy.wait_recv()
        part = self.mine()[...].astype(F32)
        out[...] = (
            part + self.last_dn[...].astype(F32) + self.last_up[...].astype(F32)
        ).astype(out.dtype)


PIECES = ((0, 0, F, 0), (1, 0, F, 1), (2, 0, 2 * LW, 0), (2, 2 * LW, 2 * LW, 1))
RP = R // 4
NP = len(PIECES)


class Rings:
    def __init__(self):
        i = lax.axis_index("dp")
        self.y = y = lax.rem(i, 4)
        self.x = lax.div(i, 8)
        self.zh = zh = lax.rem(lax.div(i, 4), 2)
        self.along_y = [{"dp": i - y + lax.rem(y + k, 4)} for k in (1, 2, 3)]
        self.along_x = [{"dp": lax.rem(i + 8 * k, 32)} for k in (1, 2, 3)]
        self.other = {"dp": i + 4 - 8 * zh}
        ring_y = (y, self.along_y[0], self.along_y[2])
        ring_x = (self.x, self.along_x[0], self.along_x[2])
        self.order = [(ring_y, ring_x), (ring_x, ring_y)]

    def next_to(self):
        return [*self.along_y[::2], *self.along_x[::2]]


def ring_scratch(lead, width):
    half = pltpu.VMEM((*lead, width // 2), BF)
    full = pltpu.VMEM((*lead, width), BF)
    return [half, half, half, half, full, full]


def wide_shape(width, mode):
    return ((4, 2, RP, width) if mode == 0 else (2, 4, RP, width), BF)


WIDE_REFS, NARROW_REFS = 9, 8


def wide_scratch():
    out = []
    for _, _, width, mode in PIECES:
        lead = wide_shape(width, mode)[0][:3]
        half = pltpu.VMEM((*lead, width // 2), BF)
        out += ring_scratch(lead, width) + [pltpu.VMEM((*lead, width), BF), half, half]
    return out


def narrow_scratch():
    out = []
    for _, _, width, _ in PIECES:
        small, rest = pltpu.VMEM((2, RP, width), BF), pltpu.VMEM((RP, width), BF)
        out += ring_scratch((2, RP), width) + [small, rest]
    return out


def reduced_shapes():
    return [((RP, width), F32) for _, _, width, _ in PIECES]


def as_blocks(w):
    return w.reshape(4, 2, 4, RP, w.shape[-1])


class Wide:
    def __init__(self, wires, rings, ins, bufs, ls, first_sem):
        self.rings, self.loads = [], []
        for k, (which, column, width, mode) in enumerate(PIECES):
            refs = bufs[k * WIDE_REFS : (k + 1) * WIDE_REFS]
            mine, side_up, side_dn = refs[6:9]
            w = ins[which]

            def chunk(pos, half, w=w, mode=mode, column=column, size=width // 2):
                cols = pl.ds(column + half * size, size)
                return w.at[:, :, pos, :, cols] if mode == 0 else w.at[pos, :, :, :, cols]

            place = rings.order[mode][0]
            me = place[0]
            cols = pl.ds(column, width)
            whole = w.at[:, :, me, :, cols] if mode == 0 else w.at[me, :, :, :, cols]
            parts = (
                (chunk(lax.rem(me + 1, 4), 0), side_up),
                (chunk(lax.rem(me + 3, 4), 1), side_dn),
                (whole, mine),
            )
            sems = [ls.at[first_sem + 3 * k + j] for j in range(3)]
            self.loads.append(
                [pltpu.make_async_copy(src, dst, sem) for (src, dst), sem in zip(parts, sems)]
            )
            self.rings.append(
                Ring(
                    wires, chunk, lambda r=mine: r, lambda r=side_up: r, lambda r=side_dn: r,
                    place, refs[0:6],
                )
            )

    def start(self, *ks):
        for k in ks:
            for copy in self.loads[k]:
                copy.start()
            self.rings[k].start()

    def forward(self, *ks):
        for k in ks:
            for copy in self.loads[k]:
                copy.wait()
            self.rings[k].forward()

    def finish(self, accs, *ks):
        for k in ks:
            self.rings[k].finish(accs[k])


class Narrow:
    def __init__(self, wires, rings, accs, bufs):
        self.wires, self.rings, self.parts, self.last = wires, [], [], {}
        self.zh, self.other = rings.zh, rings.other
        for k, (_, _, width, mode) in enumerate(PIECES):
            refs = bufs[k * NARROW_REFS : (k + 1) * NARROW_REFS]
            acc = accs[k]
            place = rings.order[mode][1]

            def chunk(pos, half, acc=acc, mode=mode, size=width // 2):
                cols = pl.ds(half * size, size)
                return acc.at[pos, :, :, cols] if mode == 0 else acc.at[:, pos, :, cols]

            def mine(acc=acc, mode=mode, pos=place[0]):
                return acc.at[pos] if mode == 0 else acc.at[:, pos]

            self.rings.append(
                Ring(
                    wires, chunk, mine,
                    lambda n=chunk, p=lax.rem(place[0] + 1, 4): n(p, 0),
                    lambda n=chunk, p=lax.rem(place[0] + 3, 4): n(p, 1),
                    place, refs[0:6],
                )
            )
            self.parts.append(refs[6:8])

    def start(self, *ks):
        for k in ks:
            self.rings[k].start()

    def forward(self, *ks):
        for k in ks:
            self.rings[k].forward()

    def beyond(self, *ks):
        for k in ks:
            small, rest = self.parts[k]
            self.rings[k].finish(small)
            self.last[k] = self.wires.push(small.at[1 - self.zh], rest, self.other)

    def finish(self, outs):
        for k, out in enumerate(outs):
            small, rest = self.parts[k]
            self.last[k].wait_recv()
            out[...] = small[self.zh].astype(F32) + rest[...].astype(F32)


VEC = (24, D)


def vector_scratch():
    few, whole, four = (
        pltpu.VMEM((16, D), F32), pltpu.VMEM(VEC, F32), pltpu.VMEM((4, *VEC), F32),
    )
    return [whole, few, few, four, four, whole]


class Vectors:
    def __init__(self, wires, at, rings, bufs):
        self.wires, self.at, self.rings = wires, at, rings
        self.vec, self.vmate, self.vcp, self.vy, self.vx, self.vz = bufs

    def fill(self, layers):
        vec = self.vec
        vec[...] = jnp.zeros_like(vec)
        for k, (va, vb, fb, qb) in enumerate(layers):
            vec[8 * k : 8 * k + 6, :] = va[0:6, :]
            vec[8 * k + 6 : 8 * k + 8, :] = vb[0:2, :]
            vec[16 + k : 17 + k, :] = fb[0:1, :]
            vec[18 + k : 19 + k, : 3 * LW] = qb[0:1, :]
        self.one = self.wires.push(vec.at[pl.ds(0, 16)], self.vmate, {"tensor": self.at.mate})

    def over_core(self):
        vec = self.vec
        self.one.wait_recv()
        self.wires.left(self.one)
        vec[0:16, :] = vec[0:16, :] + self.vmate[...]
        self.two = self.wires.push(vec.at[pl.ds(0, 16)], self.vcp, {"tensor": self.at.cp})

    def over_chip(self):
        vec, vy, y = self.vec, self.vy, self.rings.y
        self.two.wait_recv()
        vy[y] = vec[...]
        vy[y, 0:16, :] = vec[0:16, :] + self.vcp[...]
        self.sent = [self.wires.push(vy.at[y], vy.at[y], d) for d in self.rings.along_y]

    def over_y(self):
        vx, vy, x = self.vx, self.vy, self.rings.x
        for copy in self.sent:
            copy.wait_recv()
        vx[x] = vy[0] + vy[1] + vy[2] + vy[3]
        self.sent = [self.wires.push(vx.at[x], vx.at[x], d) for d in self.rings.along_x]

    def over_x(self):
        vec, vx = self.vec, self.vx
        for copy in self.sent:
            copy.wait_recv()
        self.wires.left(self.two)
        vec[...] = vx[0] + vx[1] + vx[2] + vx[3]
        self.last = self.wires.push(vec, self.vz, self.rings.other)

    def finish(self, out):
        self.last.wait_recv()
        out[...] = self.vec[...] + self.vz[...]


def shards(
    tokens_in,
    image_starts,
    norm_gain,
    norm_bias,
    qkv_weight,
    qv_bias,
    proj_weight,
    out_bias,
    layer_scale,
    fc1_weight,
    fc1_bias,
    fc2_weight,
    out_grad,
):
    layers = qkv_weight.shape[0]
    w_qkv = jnp.transpose(qkv_weight, (0, 2, 1, 3))
    hidden = tokens_in
    saved = []
    for l in range(layers):
        rows_one, q, win = inward(2 * l, l, hidden, norm_gain, norm_bias, qv_bias, w_qkv)
        att, lt = attend(image_starts, q, win)
        mixed, br1, br2, nxt, rows_two, act, slope = outward(
            2 * l + 1, l, BF if l == layers - 1 else F32, att, hidden, layer_scale, out_bias,
            norm_gain, norm_bias, fc1_bias, proj_weight, fc1_weight, fc2_weight,
        )
        saved.append((rows_one, q, win, att, lt, hidden, mixed, br1, br2, rows_two, act, slope))
        hidden = nxt
    grad = out_grad
    given, accs, kept = (), (), None
    for l in reversed(range(layers)):
        rows_one, q, win, att, lt, h, mixed, br1, br2, rows_two, act, slope = saved[l]
        gmix, gatt, dw2, dw1, dwp, va, fb, *accs = back_out(
            4 + 2 * l, l, given, grad, layer_scale, out_bias, norm_gain, mixed, br1, br2,
            act, slope, rows_two, att, fc1_weight, fc2_weight, proj_weight,
        )
        dq, dwin = attend_back(image_starts, q, win, gatt, att, lt)
        final = ()
        if l == 0:
            va1, vb1, fb1, qb1 = kept
            final = (as_blocks(dw2), as_blocks(dw1), *accs, va1, va, vb1, fb1, fb, qb1)
        grad, *rest = back_in(
            5 + 2 * l, l, final, dq, dwin, rows_one, gmix, h, norm_gain, dwp, w_qkv
        )
        if l:
            dw, vb, qb = rest
            given = (as_blocks(dw2), as_blocks(dw1), dw)
            kept = (va, vb, fb, qb)
    a1, b1, c1, d1, a0, b0, c0, d0, vec = rest
    rows = vec[:16].reshape(2, 8, D)
    qkv = jnp.stack(
        [jnp.concatenate([c0, d0[:, :LW]], 1), jnp.concatenate([c1, d1[:, :LW]], 1)]
    )
    return (
        hidden,
        grad,
        jnp.stack([rows[:, 6], rows[:, 2]], 1),
        jnp.stack([rows[:, 7], rows[:, 3]], 1),
        qkv.reshape(2, RP, 3, LW),
        jnp.stack([vec[18:20, :LW], vec[18:20, 2 * LW : 3 * LW]], 1),
        jnp.stack([d0[:, LW:].T, d1[:, LW:].T]),
        jnp.stack([rows[:, 5], rows[:, 1]], 1),
        jnp.stack([rows[:, 4], rows[:, 0]], 1),
        jnp.stack([b0, b1]),
        vec[16:18],
        jnp.stack([a0.T, a1.T]),
    )


def solution(mesh):
    return jax.shard_map(
        shards,
        mesh=mesh,
        in_specs=(
            P(("dp", "tensor"), None),
            P(),
            P(),
            P(),
            P(None, None, None, "tensor"),
            P(None, None, "tensor"),
            P(None, "tensor", None),
            P(),
            P(),
            P(None, None, "tensor"),
            P(None, "tensor"),
            P(None, "tensor", None),
            P(("dp", "tensor"), None),
        ),
        out_specs=(
            P(("dp", "tensor"), None),
            P(("dp", "tensor"), None),
            P(),
            P(),
            P(None, "dp", None, "tensor"),
            P(None, None, "tensor"),
            P(None, "tensor", "dp"),
            P(),
            P(),
            P(None, "dp", "tensor"),
            P(None, "tensor"),
            P(None, "tensor", "dp"),
        ),
        check_vma=False,
    )
```

time: 609 us -> 490 us (0.80)
  Pallas kernels: 566 us -> 464 us
  local copies, waits for them, and re-layouts: 29.4 us -> 19.7 us
    pallas_call x13 -> x12, Pallas kernels: 566 us -> 464 us  [call(): pl.pallas_call(kernel, out_shape=shapes, in_specs=specs or [VM] * len(ins...]
    unnamed x17 -> x82, local copies, waits for them, and re-layouts: 4.7 us -> 18.9 us
    squeeze x4 -> x0, local copies, waits for them, and re-layouts: 9.98 us -> none  [the longest x1 4.9 us: shards(): fc2_weight[l]]
where the time goes in v2:
time: 490 us; the launch traced here: 489 us
  Pallas kernels  464 us (95%)
  local copies, waits for them, and re-layouts  19.7 us (4%)
    pallas_call x12, Pallas kernels, call(): pl.pallas_call(kernel, out_shape=shapes, in_specs=specs or [VM] * len(ins...  464 us
    unnamed x82, local copies, waits for them, and re-layouts  18.9 us

profile of v2, /device:TPU:0, one launch (start us, length us, event | category | flops | bytes accessed | tf_op | source)
XLA Modules:
  0.0 488.5 jit_solution(14609110265845931943)
XLA Ops:
  0.7 1.9 copy-done.3
  2.6 0.9 copy-done.11
  5.7 64.9 %inward0.1 = (bf16[512,1024]{1,0:T(8,128)(2,1)S(1)}, bf16[512,256]{1,0:T(8,128)(2,1)S(1)}, bf16[3328,512]{1,0:T(8,128)(2,1)S(1)}) custom-call(bf16[128,1024]{1,0:T(8,128)(2,1)S(1)} %copy-done.11, f32[2,2,1024]{2,1,0:T(2,128)S(1)} %copy-done.25, f32[2,2,1024]{2,1,0:T(2,128)S(1)} %copy-done.31, f32[2,2,256]{2,1,0:T(2,128)S(1)} %copy-done.36, ...), custom_call_target="tpu_custom_call" | custom-call | tf_op jit(solution)/shard_map/inward0/pallas_call | solution.py:284
  70.6 1.0 copy-done.16
  71.6 11.4 %attend.2 = (bf16[512,256]{1,0:T(8,128)(2,1)S(1)}, f32[16,1024]{1,0:T(8,128)S(1)}) custom-call(s32[11]{0:T(128)S(1)} %copy-done.38, bf16[512,256]{1,0:T(8,128)(2,1)S(1)} %get-tuple-element.72.q, bf16[3328,512]{1,0:T(8,128)(2,1)S(1)} %get-tuple-element.73.win), custom_call_target="tpu_custom_call" | custom-call | tf_op jit(solution)/shard_map/attend/pallas_call | solution.py:284
  83.0 2.2 copy-done.1
  85.2 29.4 %outward0.1 = (f32[128,1024]{1,0:T(8,128)S(1)}, f32[128,1024]{1,0:T(8,128)S(1)}, f32[128,1024]{1,0:T(8,128)S(1)}, f32[128,1024]{1,0:T(8,128)S(1)}, bf16[512,1024...) custom-call(bf16[512,256]{1,0:T(8,128)(2,1)S(1)} %get-tuple-element.74.att.refs_10_, ...), custom_call_target="tpu_custom_call" | custom-call | tf_op jit(solution)/shard_map/outward0/pallas_call | solution.py:284
  114.7 0.8 copy-done.28
  115.4 0.8 copy-done.30
  116.3 57.4 %inward1.1 = (bf16[512,1024]{1,0:T(8,128)(2,1)S(1)}, bf16[512,256]{1,0:T(8,128)(2,1)S(1)}, bf16[3328,512]{1,0:T(8,128)(2,1)S(1)}) custom-call(f32[128,1024]{1,0:T(8,128)S(1)} %get-tuple-element.75.h.refs_4_, f32[2,2,1024]{2,1,0:T(2,128)S(1)} %copy-done.26, f32[2,2,1024]{2,1,0:T(2,128)S(1)} %copy-done.32, f32[2,2,256]{2,1,0:T(2,128)S(1)} %copy-done.37, ...), custom_call_target="tpu_custom_call" | custom-call | tf_op jit(solution)/shard_map/inward1/pallas_call | solution.py:284
  173.7 1.0 copy-done.21
  174.7 11.7 %attend.3 = (bf16[512,256]{1,0:T(8,128)(2,1)S(1)}, f32[16,1024]{1,0:T(8,128)S(1)}) custom-call(s32[11]{0:T(128)S(1)} %copy-done.38, bf16[512,256]{1,0:T(8,128)(2,1)S(1)} %get-tuple-element.76.q, bf16[3328,512]{1,0:T(8,128)(2,1)S(1)} %get-tuple-element.77.win), custom_call_target="tpu_custom_call" | custom-call | tf_op jit(solution)/shard_map/attend/pallas_call | solution.py:284
  186.4 29.4 %outward1.1 = (f32[128,1024]{1,0:T(8,128)S(1)}, f32[128,1024]{1,0:T(8,128)S(1)}, f32[128,1024]{1,0:T(8,128)S(1)}, bf16[128,1024]{1,0:T(8,128)(2,1)S(1)}, bf16[51...) custom-call(bf16[512,256]{1,0:T(8,128)(2,1)S(1)} %get-tuple-element.78.att.refs_10_, ...), custom_call_target="tpu_custom_call" | custom-call | tf_op jit(solution)/shard_map/outward1/pallas_call | solution.py:284
  215.9 1.0 copy-done.23
  216.9 1.2 copy-done.24
  218.1 26.4 %back_out1.1 = (f32[128,1024]{1,0:T(8,128)S(1)}, bf16[512,256]{1,0:T(8,128)(2,1)S(1)}, bf16[1024,1024]{1,0:T(8,128)(2,1)S(1)}, bf16[1024,1024]{1,0:T(8,128)(2,1)...) custom-call(f32[128,1024]{1,0:T(8,128)S(1)} %copy-done.27, ...), custom_call_target="tpu_custom_call" | custom-call | tf_op jit(solution)/shard_map/back_out1/pallas_call | solution.py:284
  244.6 16.5 %attend_back.2 = (bf16[512,256]{1,0:T(8,128)(2,1)S(1)}, bf16[3328,512]{1,0:T(8,128)(2,1)S(1)}) custom-call(s32[11]{0:T(128)S(1)} %copy-done.38, bf16[512,256]{1,0:T(8,128)(2,1)S(1)} %get-tuple-element.76.q, bf16[3328,512]{1,0:T(8,128)(2,1)S(1)} %copy-done.9, bf16[512,256]{1,0:T(8,128)(2,1)S(1)} %get-tuple-element.86.grad, ...), custom_call_target="tpu_custom_call" | custom-call | tf_op jit(solution)/shard_map/attend_back/pallas_call | solution.py:284
  261.1 53.2 %back_in1.1 = (f32[128,1024]{1,0:T(8,128)S(1)}, bf16[4,2,4,32,1024]{4,3,2,1,0:T(8,128)(2,1)S(1)}, f32[8,1024]{1,0:T(8,128)S(1)}, f32[8,768]{1,0:T(8,128)S(1)}) custom-call(bf16[512,256]{1,0:T(8,128)(2,1)S(1)} %get-tuple-element.88.refs_0_, bf16[3328,512]{1,0:T(8,128)(2,1)S(1)} %get-tuple-element.89.refs_1_, bf16[512,1024]{1,0:T(8,128)(2,1)S(1)} %copy-done.22, ...), custom_call_target="tpu_custom_call" | custom-call | tf_op jit(solution)/shard_map/back_in1/pallas_call | solution.py:284
  314.3 1.3 copy-done.15
  315.6 37.5 %back_out0.1 = (f32[128,1024]{1,0:T(8,128)S(1)}, bf16[512,256]{1,0:T(8,128)(2,1)S(1)}, bf16[1024,1024]{1,0:T(8,128)(2,1)}, bf16[1024,1024]{1,0:T(8,128)(2,1)}, b...) custom-call(f32[128,1024]{1,0:T(8,128)S(1)} %get-tuple-element.93.re, ...), custom_call_target="tpu_custom_call" | custom-call | tf_op jit(solution)/shard_map/back_out0/pallas_call | solution.py:284
  353.2 16.6 %attend_back.3 = (bf16[512,256]{1,0:T(8,128)(2,1)S(1)}, bf16[3328,512]{1,0:T(8,128)(2,1)S(1)}) custom-call(s32[11]{0:T(128)S(1)} %copy-done.38, bf16[512,256]{1,0:T(8,128)(2,1)S(1)} %get-tuple-element.72.q, bf16[3328,512]{1,0:T(8,128)(2,1)S(1)} %copy-done.7, bf16[512,256]{1,0:T(8,128)(2,1)S(1)} %get-tuple-element.103.grad, ...), custom_call_target="tpu_custom_call" | custom-call | tf_op jit(solution)/shard_map/attend_back/pallas_call | solution.py:284
  369.8 1.7 copy-done.10
  371.5 109.7 %back_in0.1 = (f32[128,1024]{1,0:T(8,128)S(1)}, f32[32,1024]{1,0:T(8,128)S(1)}, f32[32,1024]{1,0:T(8,128)S(1)}, f32[32,512]{1,0:T(8,128)S(1)}, f32[32,512]{1,0:T...) custom-call(bf16[512,256]{1,0:T(8,128)(2,1)S(1)} %get-tuple-element., ...), custom_call_target="tpu_custom_call" | custom-call | tf_op jit(solution)/shard_map/back_in0/pallas_call | solution.py:284
  487.5 0.8 copy.33
  (86 shorter events, 8.5 us)
Async XLA Ops:
  0.6 70.9 %copy-start.38 = (s32[11]{0:T(128)S(1)}, s32[11]{0:T(128)}, u32[]{:S(2)}) copy-start(s32[11]{0:T(128)} %starts.7) | copy-start | bytes 136
  5.6 77.3 %copy-start = (bf16[2,1024,1024]{2,1,0:T(8,128)(2,1)S(1)}, bf16[2,1024,1024]{2,1,0:T(8,128)(2,1)}, u32[]{:S(2)}) copy-start(bf16[2,1024,1024]{2,1,0:T(8,128)(2,1)} %refs_11_.3) | copy-start | bytes 12582916
  5.6 77.3 %copy-start.5 = (bf16[2,256,1024]{2,1,0:T(8,128)(2,1)S(1)}, bf16[2,256,1024]{2,1,0:T(8,128)(2,1)}, u32[]{:S(2)}) copy-start(bf16[2,256,1024]{2,1,0:T(8,128)(2,1)} %refs_13_.3) | copy-start | bytes 3145732
  5.6 77.3 %copy-start.12 = (bf16[128,1024]{1,0:T(8,128)(2,1)S(1)}, bf16[128,1024]{1,0:T(8,128)(2,1)}, u32[]{:S(2)}) copy-start(bf16[128,1024]{1,0:T(8,128)(2,1)} %refs_4_.1) | copy-start | bytes 786436
  5.6 77.3 %copy-start.26 = (f32[2,2,1024]{2,1,0:T(2,128)S(1)}, f32[2,2,1024]{2,1,0:T(2,128)}, u32[]{:S(2)}) copy-start(f32[2,2,1024]{2,1,0:T(2,128)} %refs_5_.3) | copy-start | bytes 49156
  5.6 77.3 %copy-start.32 = (f32[2,2,1024]{2,1,0:T(2,128)S(1)}, f32[2,2,1024]{2,1,0:T(2,128)}, u32[]{:S(2)}) copy-start(f32[2,2,1024]{2,1,0:T(2,128)} %bias.7) | copy-start | bytes 49156
  5.6 77.3 %copy-start.33 = (f32[2,2,1024]{2,1,0:T(2,128)S(1)}, f32[2,2,1024]{2,1,0:T(2,128)}, u32[]{:S(2)}) copy-start(f32[2,2,1024]{2,1,0:T(2,128)} %refs_1_.3) | copy-start | bytes 49156
  5.7 77.3 %copy-start.34 = (f32[2,2,1024]{2,1,0:T(2,128)S(1)}, f32[2,2,1024]{2,1,0:T(2,128)}, u32[]{:S(2)}) copy-start(f32[2,2,1024]{2,1,0:T(2,128)} %refs_2_.3) | copy-start | bytes 49156
  5.7 77.3 %copy-start.35 = (f32[2,1024]{1,0:T(2,128)S(1)}, f32[2,1024]{1,0:T(2,128)}, u32[]{:S(2)}) copy-start(f32[2,1024]{1,0:T(2,128)} %b1.3) | copy-start | bytes 24580
  85.2 31.0 %copy-start.4 = (bf16[2,1024,3,256]{3,1,2,0:T(8,128)(2,1)S(1)}, bf16[2,1024,3,256]{3,1,2,0:T(8,128)(2,1)}, u32[]{:S(2)}) copy-start(bf16[2,1024,3,256]{3,1,2,0:T(8,128)(2,1)} %param.17) | copy-start | bytes 9437188
  85.2 31.1 %copy-start.37 = (f32[2,2,256]{2,1,0:T(2,128)S(1)}, f32[2,2,256]{2,1,0:T(2,128)}, u32[]{:S(2)}) copy-start(f32[2,2,256]{2,1,0:T(2,128)} %b2.3) | copy-start | bytes 12292
  116.2 58.5 %copy-start.18 = (bf16[512,1024]{1,0:T(8,128)(2,1)}, bf16[512,1024]{1,0:T(8,128)(2,1)S(1)}, u32[]{:S(2)}) copy-start(bf16[512,1024]{1,0:T(8,128)(2,1)S(1)} %get-tuple-element.99.refs_9_) | copy-start | bytes 3145732
  116.2 58.5 %copy-start.20 = (bf16[512,1024]{1,0:T(8,128)(2,1)}, bf16[512,1024]{1,0:T(8,128)(2,1)S(1)}, u32[]{:S(2)}) copy-start(bf16[512,1024]{1,0:T(8,128)(2,1)S(1)} %get-tuple-element.98.refs_8_) | copy-start | bytes 3145732
  116.2 70.2 %copy-start.19 = (bf16[512,1024]{1,0:T(8,128)(2,1)}, bf16[512,1024]{1,0:T(8,128)(2,1)S(1)}, u32[]{:S(2)}) copy-start(bf16[512,1024]{1,0:T(8,128)(2,1)S(1)} %get-tuple-element.97.refs_7_) | copy-start | bytes 3145732
  116.2 70.2 %copy-start.29 = (f32[128,1024]{1,0:T(8,128)}, f32[128,1024]{1,0:T(8,128)S(1)}, u32[]{:S(2)}) copy-start(f32[128,1024]{1,0:T(8,128)S(1)} %get-tuple-element.95.refs_5_) | copy-start | bytes 1572868
  116.3 70.1 %copy-start.2 = (bf16[2,1024,1024]{2,1,0:T(8,128)(2,1)S(1)}, bf16[2,1024,1024]{2,1,0:T(8,128)(2,1)}, u32[]{:S(2)}) copy-start(bf16[2,1024,1024]{2,1,0:T(8,128)(2,1)} %refs_12_.3) | copy-start | bytes 12582916
  174.7 41.1 %copy-start.8 = (bf16[3328,512]{1,0:T(8,128)(2,1)}, bf16[3328,512]{1,0:T(8,128)(2,1)S(1)}, u32[]{:S(2)}) copy-start(bf16[3328,512]{1,0:T(8,128)(2,1)S(1)} %get-tuple-element.77.win) | copy-start | bytes 10223620
  186.4 30.4 %copy-start.27 = (f32[128,1024]{1,0:T(8,128)S(1)}, f32[128,1024]{1,0:T(8,128)}, u32[]{:S(2)}) copy-start(f32[128,1024]{1,0:T(8,128)} %refs_0_.1) | copy-start | bytes 1572868
  218.1 26.5 %copy-start.9 = (bf16[3328,512]{1,0:T(8,128)(2,1)S(1)}, bf16[3328,512]{1,0:T(8,128)(2,1)}, u32[]{:S(2)}) copy-start(bf16[3328,512]{1,0:T(8,128)(2,1)} %copy-done.8) | copy-start | bytes 10223620
  244.5 69.8 %copy-start.13 = (bf16[1024,1024]{1,0:T(8,128)(2,1)}, bf16[1024,1024]{1,0:T(8,128)(2,1)S(1)}, u32[]{:S(2)}) copy-start(bf16[1024,1024]{1,0:T(8,128)(2,1)S(1)} %get-tuple-element.100) | copy-start | bytes 6291460
  244.5 69.8 %copy-start.14 = (bf16[1024,1024]{1,0:T(8,128)(2,1)}, bf16[1024,1024]{1,0:T(8,128)(2,1)S(1)}, u32[]{:S(2)}) copy-start(bf16[1024,1024]{1,0:T(8,128)(2,1)S(1)} %get-tuple-element.101) | copy-start | bytes 6291460
  244.5 16.5 %copy-start.22 = (bf16[512,1024]{1,0:T(8,128)(2,1)S(1)}, bf16[512,1024]{1,0:T(8,128)(2,1)}, u32[]{:S(2)}) copy-start(bf16[512,1024]{1,0:T(8,128)(2,1)} %copy-done.21) | copy-start | bytes 3145732
  315.6 37.6 %copy-start.7 = (bf16[3328,512]{1,0:T(8,128)(2,1)S(1)}, bf16[3328,512]{1,0:T(8,128)(2,1)}, u32[]{:S(2)}) copy-start(bf16[3328,512]{1,0:T(8,128)(2,1)} %copy-done.6) | copy-start | bytes 10223620
  353.2 18.3 %copy-start.17 = (bf16[512,1024]{1,0:T(8,128)(2,1)S(1)}, bf16[512,1024]{1,0:T(8,128)(2,1)}, u32[]{:S(2)}) copy-start(bf16[512,1024]{1,0:T(8,128)(2,1)} %copy-done.16) | copy-start | bytes 3145732
  (15 other events, 27.4 us)

commit v3 on v1

v3 whole, which is shorter than its diff:
```python
import functools

import jax
import jax.numpy as jnp
from jax import lax
from jax.experimental import pallas as pl
from jax.experimental.pallas import tpu as pltpu
from jax.sharding import PartitionSpec as P

MESH = pl.DeviceIdType.MESH
BF = jnp.bfloat16
F32 = jnp.float32
VM = pl.BlockSpec(memory_space=pltpu.VMEM)
SM = pl.BlockSpec(memory_space=pltpu.SMEM)
ANY = pl.BlockSpec(memory_space=pl.ANY)

HEAD_DIM = 64
IMG_LEN = 1370
EPS = 1e-06
NEG = -1e30

R = 128
S = 512
D = 1024
LW = 256
HL = LW // HEAD_DIM
F = 1024
TOTAL = 16384
NDP = 32
FAR3 = 384
OWN0 = FAR3 + 2 * S
NW = 2 * OWN0 + S
QB = 256
KB = 256
NB = NW // KB
C = 2
RC = R // C
MB = 1 << 20


def mm(a, b):
    return jnp.dot(a, b, preferred_element_type=F32)


def mm_rt(a, b):
    return lax.dot_general(a, b, (((1,), (1,)), ((), ())), preferred_element_type=F32)


def mm_lt(a, b):
    return lax.dot_general(a, b, (((0,), (0,)), ((), ())), preferred_element_type=F32)


class Place:
    def __init__(self):
        self.t = lax.axis_index("tensor")
        self.core = lax.rem(self.t, 2)
        self.mate = self.t + 1 - 2 * self.core
        self.cp = lax.rem(self.t + 2, 4)
        self.own = pl.multiple_of(self.t * R, R)
        self.opp = pl.multiple_of(self.cp * R, R)
        self.near = pl.multiple_of((self.t - self.core) * R, 2 * R)
        self.far = pl.multiple_of(2 * R - self.near, 2 * R)
        self.dp = lax.axis_index("dp")
        self.up = lax.rem(self.dp + 1, NDP)
        self.dn = lax.rem(self.dp + NDP - 1, NDP)


def greet(devices):
    barrier = pltpu.get_barrier_semaphore()
    for device in devices:
        pl.semaphore_signal(barrier, inc=1, device_id=device, device_id_type=MESH)
    pl.semaphore_wait(barrier, len(devices))


class Wires:
    def __init__(self, send, recv):
        self.send, self.recv, self.count, self.open = send, recv, 0, []

    def push(self, src, dst, device):
        k = self.count
        self.count += 1
        copy = pltpu.make_async_remote_copy(
            src, dst, self.send.at[k], self.recv.at[k], device_id=device, device_id_type=MESH
        )
        copy.start()
        self.open.append(copy)
        return copy

    def left(self, copy):
        copy.wait_send()
        self.open = [c for c in self.open if c is not copy]

    def close(self):
        for copy in self.open:
            copy.wait_send()


class Chain:
    def __init__(self, wires, at, up, relay):
        self.wires, self.at, self.relay = wires, at, relay
        y = lax.rem(at.dp, 4)
        self.edge = (y == 3) if up else (y == 0)
        self.plain = jnp.logical_not(self.edge)
        self.device = at.up if up else at.dn
        self.items = []

    def plan(self, src, dst, partner_dst=None, when=True, partner_when=True):
        wires, at = self.wires, self.at
        slot = self.relay.at[len(self.items)]
        k = wires.count
        wires.count += 2

        def copy(source, target, n, device):
            return lambda: pltpu.make_async_remote_copy(
                source, target, wires.send.at[n], wires.recv.at[n],
                device_id=device, device_id_type=MESH,
            )

        direct = copy(src, dst, k, {"dp": self.device})
        first = copy(src, slot, k + 1, {"tensor": at.cp})
        target = dst if partner_dst is None else partner_dst
        second = copy(slot, target, k, {"dp": self.device, "tensor": at.cp})
        item = (direct, first, second, when, partner_when)
        self.items.append(item)
        return item

    def send(self, item):
        direct, first, _, when, _ = item
        pl.when(self.plain & when)(lambda: direct().start())
        pl.when(self.edge & when)(lambda: first().start())

    def hand_on(self, item):
        _, first, second, _, partner_when = item

        @pl.when(self.edge & partner_when)
        def _():
            first().wait_recv()
            second().start()

    def arrive(self, item):
        pl.when(item[3])(lambda: item[0]().wait_recv())

    def close(self):
        for direct, first, second, when, partner_when in self.items:
            pl.when(self.plain & when)(lambda c=direct: c().wait_send())
            pl.when(self.edge & when)(lambda c=first: c().wait_send())
            pl.when(self.edge & partner_when)(lambda c=second: c().wait_send())


class Line:
    def __init__(self, wires, device):
        self.wires, self.device = wires, device

    def send(self, src, dst):
        return self.wires.push(src, dst, self.device)

    def arrive(self, copy):
        copy.wait_recv()


def chain_partners(at):
    return [
        {"tensor": at.mate},
        {"tensor": at.cp},
        {"dp": at.up},
        {"dp": at.dn},
        {"dp": at.up, "tensor": at.cp},
        {"dp": at.dn, "tensor": at.cp},
    ]


AG_SEMS = 2 * C + 1
RS_SEMS = 2 * C + 1


class Gather:
    def __init__(self, wires, at, buf):
        self.wires, self.at, self.buf = wires, at, buf
        own = at.own
        self.across, self.passed = [], []
        for c in range(C):
            part = buf.at[pl.ds(own + c * RC, RC)]
            self.across.append(wires.push(part, part, {"tensor": at.cp}))
        part = buf.at[pl.ds(own, R)]
        self.beside = wires.push(part, part, {"tensor": at.mate})

    def near(self):
        self.beside.wait_recv()

    def take(self, c):
        self.across[c].wait_recv()
        part = self.buf.at[pl.ds(self.at.opp + c * RC, RC)]
        self.passed.append(self.wires.push(part, part, {"tensor": self.at.mate}))

    def arrived(self, c):
        self.passed[c].wait_recv()

    def far(self):
        for c in range(C):
            self.take(c)
        for c in range(C):
            self.arrived(c)


class Rows:
    def __init__(self, at, chunk=None):
        if chunk is None:
            self.parts = [(at.near, 2 * R)]
        else:
            self.parts = [
                (pl.multiple_of(at.far + core * R + chunk * RC, RC), RC) for core in range(2)
            ]

    def load(self, ref, cols=slice(None)):
        parts = [ref[pl.ds(first, count), cols] for first, count in self.parts]
        return parts[0] if len(parts) == 1 else jnp.concatenate(parts, axis=0)

    def store(self, ref, value, cols=slice(None)):
        at = 0
        for first, count in self.parts:
            ref[pl.ds(first, count), cols] = value[at : at + count]
            at += count


class Scatter:
    def __init__(self, wires, at, bufs):
        self.wires, self.at = wires, at
        self.far, self.near = bufs[:2]
        self.send1, self.recv1, self.send2, self.recv2, self.send3, self.recv3 = bufs[2:]
        self.ones, self.twos = [], []

    def put(self, c, value):
        for core in range(2):
            self.far[pl.ds(core * R + c * RC, RC), :] = value[core * RC : (core + 1) * RC]

    def first(self, c):
        at = self.at
        rows = pl.ds(c * RC, RC)
        src = pl.ds(pl.multiple_of((1 - at.core) * R + c * RC, RC), RC)
        self.send1[rows, :] = self.far[src, :].astype(BF)
        self.ones.append(
            self.wires.push(self.send1.at[rows], self.recv1.at[rows], {"tensor": at.mate})
        )

    def second(self, c):
        at = self.at
        rows = pl.ds(c * RC, RC)
        src = pl.ds(pl.multiple_of(at.core * R + c * RC, RC), RC)
        self.ones[c].wait_recv()
        total = self.far[src, :] + self.recv1[rows, :].astype(F32)
        self.send2[rows, :] = total.astype(BF)
        self.twos.append(
            self.wires.push(self.send2.at[rows], self.recv2.at[rows], {"tensor": at.cp})
        )

    def third(self):
        at = self.at
        src = pl.ds(pl.multiple_of((1 - at.core) * R, R), R)
        self.send3[...] = self.near[src, :].astype(BF)
        self.three = self.wires.push(self.send3, self.recv3, {"tensor": at.mate})

    def everything(self, product):
        self.far[...] = product(self.at.far)
        for c in range(C):
            self.first(c)
        self.near[...] = product(self.at.near)
        for c in range(C):
            self.second(c)
        self.third()

    def total(self):
        self.three.wait_recv()
        for copy in self.twos:
            copy.wait_recv()
        own = self.near[pl.ds(pl.multiple_of(self.at.core * R, R), R), :]
        return own + self.recv3[...].astype(F32) + self.recv2[...].astype(F32)


def gather_hidden_scatter(at, gather, scatter, hidden, product, ready):
    gather.near()
    hidden(Rows(at))
    ready()
    gather.take(0)
    gather.arrived(0)
    rows = [Rows(at, c) for c in range(C)]
    hidden(rows[0])
    gather.take(1)
    scatter.put(0, product(rows[0]))
    scatter.first(0)
    gather.arrived(1)
    hidden(rows[1])
    scatter.second(0)
    scatter.put(1, product(rows[1]))
    scatter.first(1)
    scatter.near[...] = product(Rows(at))
    scatter.second(1)
    scatter.third()


SCATTER_REFS = 6


def scatter_scratch(count):
    return [pltpu.VMEM((2 * R, D), F32)] * 2 + [pltpu.VMEM((R, D), BF)] * (6 * count)


def scatter_refs(bufs, which):
    first = 2 + SCATTER_REFS * which
    return [*bufs[:2], *bufs[first : first + SCATTER_REFS]]


class Refs:
    def __init__(self, refs):
        self.refs = list(refs)

    def take(self, count):
        out, self.refs = self.refs[:count], self.refs[count:]
        return out


def fetch(src, dst, sem):
    copy = pltpu.make_async_copy(src, dst, sem)
    copy.start()
    return copy


def fetch_qkv(layer, w, buf, ls, base=0):
    return [
        fetch(w.at[layer, k], buf.at[:, pl.ds(k * LW, LW)], ls.at[base + k]) for k in range(3)
    ]


def normalized(v):
    centered = v - jnp.mean(v, axis=-1, keepdims=True)
    scale = lax.rsqrt(jnp.mean(centered * centered, axis=-1, keepdims=True) + EPS)
    return centered * scale, scale


def norm_back(v, gain, grad):
    x_hat, scale = normalized(v)
    u = grad * gain
    grad_in = scale * (
        u
        - jnp.mean(u, axis=-1, keepdims=True)
        - x_hat * jnp.mean(u * x_hat, axis=-1, keepdims=True)
    )
    return (
        grad_in,
        jnp.sum(grad * x_hat, axis=0, keepdims=True),
        jnp.sum(grad, axis=0, keepdims=True),
    )


def call(kernel, name, cid, ins, outs, scratch, sems, limit, specs=None, local=0, out_specs=None):
    shapes = [jax.ShapeDtypeStruct(shape, dtype) for shape, dtype in outs]
    extra = []
    if sems:
        extra = [pltpu.SemaphoreType.DMA((sems,)), pltpu.SemaphoreType.DMA((sems,))]
    if local:
        extra.append(pltpu.SemaphoreType.DMA((local,)))
    params = dict(vmem_limit_bytes=limit * MB)
    if cid is not None:
        params.update(collective_id=cid, has_side_effects=True)
    return pl.pallas_call(
        kernel,
        out_shape=shapes,
        in_specs=specs or [VM] * len(ins),
        out_specs=out_specs or [VM] * len(outs),
        scratch_shapes=list(scratch) + extra,
        compiler_params=pltpu.CompilerParams(**params),
        name=name,
    )(*ins)


class Ring:
    def __init__(self, wires, chunk, mine, side_up, side_dn, place, bufs):
        self.wires, self.chunk = wires, chunk
        self.mine, self.side_up, self.side_dn = mine, side_up, side_dn
        self.me, self.up, self.dn = place
        self.from_dn, self.from_up, self.send_up, self.send_dn, self.last_dn, self.last_up = bufs

    def half(self, ref, k):
        width = ref.shape[-1] // 2
        return ref.at[..., pl.ds(k * width, width)]

    def position(self, step):
        return lax.rem(self.me + step, 4)

    def start(self):
        push, chunk = self.wires.push, self.chunk
        p1, p2, p3 = self.position(1), self.position(2), self.position(3)
        self.a = push(chunk(p2, 0), self.from_dn, self.up)
        self.b = push(chunk(p2, 1), self.from_up, self.dn)
        self.c = push(chunk(p1, 1), self.half(self.last_dn, 1), self.up)
        self.d = push(chunk(p3, 0), self.half(self.last_up, 0), self.dn)

    def forward(self):
        push = self.wires.push
        self.a.wait_recv()
        total = self.side_up()[...].astype(F32) + self.from_dn[...].astype(F32)
        self.send_up[...] = total.astype(BF)
        self.e = push(self.send_up, self.half(self.last_dn, 0), self.up)
        self.b.wait_recv()
        total = self.side_dn()[...].astype(F32) + self.from_up[...].astype(F32)
        self.send_dn[...] = total.astype(BF)
        self.f = push(self.send_dn, self.half(self.last_up, 1), self.dn)

    def finish(self, out):
        for copy in (self.c, self.d, self.e, self.f):
            copy.wait_recv()
        part = self.mine()[...].astype(F32)
        out[...] = (
            part + self.last_dn[...].astype(F32) + self.last_up[...].astype(F32)
        ).astype(out.dtype)


PIECES = ((0, 0, F, 0), (1, 0, F, 1), (2, 0, 2 * LW, 0), (2, 2 * LW, 2 * LW, 1))
RP = R // 4
NP = len(PIECES)


class Rings:
    def __init__(self):
        i = lax.axis_index("dp")
        self.y = y = lax.rem(i, 4)
        self.x = lax.div(i, 8)
        self.zh = zh = lax.rem(lax.div(i, 4), 2)
        self.along_y = [{"dp": i - y + lax.rem(y + k, 4)} for k in (1, 2, 3)]
        self.along_x = [{"dp": lax.rem(i + 8 * k, 32)} for k in (1, 2, 3)]
        self.other = {"dp": i + 4 - 8 * zh}
        ring_y = (y, self.along_y[0], self.along_y[2])
        ring_x = (self.x, self.along_x[0], self.along_x[2])
        self.order = [(ring_y, ring_x), (ring_x, ring_y)]

    def next_to(self):
        return [*self.along_y[::2], *self.along_x[::2]]


def ring_scratch(lead, width):
    half = pltpu.VMEM((*lead, width // 2), BF)
    full = pltpu.VMEM((*lead, width), BF)
    return [half, half, half, half, full, full]


def wide_shape(width, mode):
    return ((4, 2, RP, width) if mode == 0 else (2, 4, RP, width), BF)


WIDE_REFS, NARROW_REFS = 9, 8


def wide_scratch():
    out = []
    for _, _, width, mode in PIECES:
        lead = wide_shape(width, mode)[0][:3]
        half = pltpu.VMEM((*lead, width // 2), BF)
        out += ring_scratch(lead, width) + [pltpu.VMEM((*lead, width), BF), half, half]
    return out


def narrow_scratch():
    out = []
    for _, _, width, _ in PIECES:
        small, rest = pltpu.VMEM((2, RP, width), BF), pltpu.VMEM((RP, width), BF)
        out += ring_scratch((2, RP), width) + [small, rest]
    return out


def reduced_shapes():
    return [((RP, width), F32) for _, _, width, _ in PIECES]


def as_blocks(w):
    return w.reshape(4, 2, 4, RP, w.shape[-1])


class Wide:
    def __init__(self, wires, rings, ins, bufs, ls, first_sem):
        self.rings, self.loads = [], []
        for k, (which, column, width, mode) in enumerate(PIECES):
            refs = bufs[k * WIDE_REFS : (k + 1) * WIDE_REFS]
            mine, side_up, side_dn = refs[6:9]
            w = ins[which]

            def chunk(pos, half, w=w, mode=mode, column=column, size=width // 2):
                cols = pl.ds(column + half * size, size)
                return w.at[:, :, pos, :, cols] if mode == 0 else w.at[pos, :, :, :, cols]

            place = rings.order[mode][0]
            me = place[0]
            cols = pl.ds(column, width)
            whole = w.at[:, :, me, :, cols] if mode == 0 else w.at[me, :, :, :, cols]
            parts = (
                (chunk(lax.rem(me + 1, 4), 0), side_up),
                (chunk(lax.rem(me + 3, 4), 1), side_dn),
                (whole, mine),
            )
            sems = [ls.at[first_sem + 3 * k + j] for j in range(3)]
            self.loads.append(
                [pltpu.make_async_copy(src, dst, sem) for (src, dst), sem in zip(parts, sems)]
            )
            self.rings.append(
                Ring(
                    wires, chunk, lambda r=mine: r, lambda r=side_up: r, lambda r=side_dn: r,
                    place, refs[0:6],
                )
            )

    def start(self, *ks):
        for k in ks:
            for copy in self.loads[k]:
                copy.start()
            self.rings[k].start()

    def forward(self, *ks):
        for k in ks:
            for copy in self.loads[k]:
                copy.wait()
            self.rings[k].forward()

    def finish(self, accs, *ks):
        for k in ks:
            self.rings[k].finish(accs[k])


class Narrow:
    def __init__(self, wires, rings, accs, bufs):
        self.wires, self.rings, self.parts, self.last = wires, [], [], {}
        self.zh, self.other = rings.zh, rings.other
        for k, (_, _, width, mode) in enumerate(PIECES):
            refs = bufs[k * NARROW_REFS : (k + 1) * NARROW_REFS]
            acc = accs[k]
            place = rings.order[mode][1]

            def chunk(pos, half, acc=acc, mode=mode, size=width // 2):
                cols = pl.ds(half * size, size)
                return acc.at[pos, :, :, cols] if mode == 0 else acc.at[:, pos, :, cols]

            def mine(acc=acc, mode=mode, pos=place[0]):
                return acc.at[pos] if mode == 0 else acc.at[:, pos]

            self.rings.append(
                Ring(
                    wires, chunk, mine,
                    lambda n=chunk, p=lax.rem(place[0] + 1, 4): n(p, 0),
                    lambda n=chunk, p=lax.rem(place[0] + 3, 4): n(p, 1),
                    place, refs[0:6],
                )
            )
            self.parts.append(refs[6:8])

    def start(self, *ks):
        for k in ks:
            self.rings[k].start()

    def forward(self, *ks):
        for k in ks:
            self.rings[k].forward()

    def beyond(self, *ks):
        for k in ks:
            small, rest = self.parts[k]
            self.rings[k].finish(small)
            self.last[k] = self.wires.push(small.at[1 - self.zh], rest, self.other)

    def finish(self, outs):
        for k, out in enumerate(outs):
            small, rest = self.parts[k]
            self.last[k].wait_recv()
            out[...] = small[self.zh].astype(F32) + rest[...].astype(F32)


VEC = (24, D)


def vector_scratch():
    few, whole, four = (
        pltpu.VMEM((16, D), F32), pltpu.VMEM(VEC, F32), pltpu.VMEM((4, *VEC), F32),
    )
    return [whole, few, few, four, four, whole]


class Vectors:
    def __init__(self, wires, at, rings, bufs):
        self.wires, self.at, self.rings = wires, at, rings
        self.vec, self.vmate, self.vcp, self.vy, self.vx, self.vz = bufs

    def fill(self, layers):
        vec = self.vec
        vec[...] = jnp.zeros_like(vec)
        for k, (va, vb, fb, qb) in enumerate(layers):
            vec[8 * k : 8 * k + 6, :] = va[0:6, :]
            vec[8 * k + 6 : 8 * k + 8, :] = vb[0:2, :]
            vec[16 + k : 17 + k, :] = fb[0:1, :]
            vec[18 + k : 19 + k, : 3 * LW] = qb[0:1, :]
        self.one = self.wires.push(vec.at[pl.ds(0, 16)], self.vmate, {"tensor": self.at.mate})

    def over_core(self):
        vec = self.vec
        self.one.wait_recv()
        self.wires.left(self.one)
        vec[0:16, :] = vec[0:16, :] + self.vmate[...]
        self.two = self.wires.push(vec.at[pl.ds(0, 16)], self.vcp, {"tensor": self.at.cp})

    def over_chip(self):
        vec, vy, y = self.vec, self.vy, self.rings.y
        self.two.wait_recv()
        vy[y] = vec[...]
        vy[y, 0:16, :] = vec[0:16, :] + self.vcp[...]
        self.sent = [self.wires.push(vy.at[y], vy.at[y], d) for d in self.rings.along_y]

    def over_y(self):
        vx, vy, x = self.vx, self.vy, self.rings.x
        for copy in self.sent:
            copy.wait_recv()
        vx[x] = vy[0] + vy[1] + vy[2] + vy[3]
        self.sent = [self.wires.push(vx.at[x], vx.at[x], d) for d in self.rings.along_x]

    def over_x(self):
        vec, vx = self.vec, self.vx
        for copy in self.sent:
            copy.wait_recv()
        self.wires.left(self.two)
        vec[...] = vx[0] + vx[1] + vx[2] + vx[3]
        self.last = self.wires.push(vec, self.vz, self.rings.other)

    def finish(self, out):
        self.last.wait_recv()
        out[...] = self.vec[...] + self.vz[...]


def inward_part(layer, at, wires, hidden, gain, bias, b2, w, loads, rows, q, win, relay):
    x_hat, _ = normalized(hidden)
    rows[pl.ds(at.own, R), :] = (x_hat * gain[layer, 0:1, :] + bias[layer, 0:1, :]).astype(BF)
    gather = Gather(wires, at, rows)

    def project(first):
        out = mm(rows[pl.ds(first, 2 * R), :], w[...])
        q[pl.ds(first, 2 * R), :] = (out[:, :LW] + b2[layer, 0:1, :]).astype(BF)
        win[pl.ds(OWN0 + first, 2 * R), :LW] = out[:, LW : 2 * LW].astype(BF)
        win[pl.ds(OWN0 + first, 2 * R), LW:] = (out[:, 2 * LW :] + b2[layer, 1:2, :]).astype(BF)

    def part(first):
        return win.at[pl.ds(pl.multiple_of(first, R), R)]

    offs = [at.near, at.near + R, at.far, at.far + R]
    others = offs[2:] + offs[:2]
    chain_up, chain_dn = Chain(wires, at, True, relay), Chain(wires, at, False, relay)
    ups, dns = {}, {}
    for n in range(1, 4):
        low, high = OWN0 - n * S, OWN0 + n * S
        for k, (own, other) in enumerate(zip(offs, others)):
            if n < 3:
                ups[n, k] = chain_up.plan(part(low + S + own), part(low + own), part(low + other))
                dns[n, k] = chain_dn.plan(
                    part(high - S + own), part(high + own), part(high + other)
                )
                continue
            ups[n, k] = chain_up.plan(
                part(low + S + own),
                part(jnp.maximum(low + own, 0)),
                part(jnp.maximum(low + other, 0)),
                own > 0,
                other > 0,
            )
            dns[n, k] = chain_dn.plan(
                part(high - S + own),
                part(jnp.minimum(high + own, NW - R)),
                part(jnp.minimum(high + other, NW - R)),
                own < S - R,
                other < S - R,
            )

    def hop(n, *ks):
        for k in ks:
            chain_up.send(ups[n, k])
            chain_dn.send(dns[n, k])

    for copy in loads:
        copy.wait()
    gather.near()
    project(at.near)
    hop(1, 0, 1)
    gather.far()
    for k in range(2):
        chain_up.hand_on(ups[1, k])
        chain_dn.hand_on(dns[1, k])
    project(at.far)
    hop(1, 2, 3)

    def hand_on(n, *ks):
        for k in ks:
            chain_up.hand_on(ups[n, k])
            chain_dn.hand_on(dns[n, k])

    def onward(n, *ks):
        for k in ks:
            chain_up.arrive(ups[n, k])
            chain_dn.arrive(dns[n, k])
            if n < 3:
                hop(n + 1, k)

    onward(1, 0, 1)
    hand_on(1, 2, 3)
    hand_on(2, 0, 1)
    onward(1, 2, 3)
    onward(2, 0, 1)
    hand_on(2, 2, 3)
    hand_on(3, 0, 1)
    onward(2, 2, 3)
    hand_on(3, 2, 3)
    onward(3, 0, 1, 2, 3)
    chain_up.close()
    chain_dn.close()


IN_OUTS = [((S, D), BF), ((S, LW), BF), ((NW, 2 * LW), BF)]
IN_SCRATCH = [pltpu.VMEM((D, 3 * LW), BF), pltpu.VMEM((12, R, 2 * LW), BF)]
IN_SEMS = AG_SEMS + 48


def inward_kernel(h, gain, bias, b2, w_hbm, rows, q, win, w, relay, ss, rs, ls):
    at = Place()
    wires = Wires(ss, rs)
    loads = fetch_qkv(0, w_hbm, w, ls)
    greet(chain_partners(at))
    inward_part(
        0, at, wires, h[...].astype(F32), gain, bias, b2, w, loads, rows, q, win, relay
    )
    wires.close()


def inward(cid, *ins):
    return call(
        inward_kernel, "inward", cid, ins, IN_OUTS, IN_SCRATCH, IN_SEMS,
        limit=14, specs=[VM] * 4 + [ANY], local=3,
    )


def ids_of(position, starts):
    total = jnp.zeros_like(position)
    for k in range(starts.shape[0]):
        first = starts[k]
        total += (position >= first).astype(jnp.int32)
        total += (position >= first + IMG_LEN).astype(jnp.int32)
    return jnp.where((position >= 0) & (position < TOTAL), total, -1)


def key_range(base, block, starts):
    first = base + block * QB
    last = first + QB - 1
    low, high = jnp.int32(0), jnp.int32(TOTAL)
    for k in range(starts.shape[0]):
        for edge in (starts[k], starts[k] + IMG_LEN):
            low = jnp.where(edge <= first, jnp.maximum(low, edge), low)
            high = jnp.where(edge > last, jnp.minimum(high, edge), high)
    edge = jnp.bool_(False)
    for k in range(starts.shape[0]):
        for at in (starts[k], starts[k] + IMG_LEN):
            edge = edge | ((at > first) & (at <= last))
    low, high = low - base + OWN0, high - base + OWN0
    low_block = lax.div(jnp.maximum(low, 0), KB)
    high_block = lax.div(jnp.minimum(high, NW) + KB - 1, KB)
    whole = lambda kb: jnp.logical_not(edge) & (kb * KB >= low) & (kb * KB + KB <= high)
    return low_block, high_block, whole


def spread_heads(value, out):
    lane = lax.broadcasted_iota(jnp.int32, (QB, LW), 1)
    for head in range(HL):
        mine = (lane >= head * HEAD_DIM) & (lane < (head + 1) * HEAD_DIM)
        out[pl.ds(head * QB, QB), :] = jnp.where(mine, value, 0.0).astype(BF)


def half_of(head):
    return head * HEAD_DIM // 128 * 128


def pick_heads(parts):
    lane = lax.broadcasted_iota(jnp.int32, (QB, 128), 1)
    halves = [
        jnp.where(lane < HEAD_DIM, parts(head), parts(head + 1)) for head in range(0, HL, 2)
    ]
    return jnp.concatenate(halves, axis=1)


def attend_kernel(starts, q, win, out, lt, qm, sbuf, high, low, acc):
    base = lax.axis_index("dp") * S
    for block in range(S // QB):
        spread_heads(q[pl.ds(block * QB, QB), :].astype(F32) * 0.125, qm)
        qid = ids_of(
            base + block * QB + lax.broadcasted_iota(jnp.int32, (QB, 1), 0), starts
        )
        first, end, whole = key_range(base, block, starts)
        high[...] = jnp.full_like(high, NEG)
        low[...] = jnp.zeros_like(low)
        acc[...] = jnp.zeros_like(acc)

        def scores(kb, carry):
            at = pl.multiple_of(kb * KB, KB)

            def put(masked):
                s = mm_rt(qm[...], win[pl.ds(at, KB), :LW])
                if masked:
                    kid = ids_of(
                        base - OWN0 + at + lax.broadcasted_iota(jnp.int32, (1, KB), 1), starts
                    )
                    bias = jnp.where(qid == kid, 0.0, NEG)
                for head in range(HL):
                    rows = pl.ds(head * QB, QB)
                    one = s[head * QB : (head + 1) * QB, :]
                    if masked:
                        one = one + bias
                    sbuf[kb, rows, :] = one
                    high[rows, :] = jnp.maximum(
                        high[rows, :], jnp.maximum(one[:, :128], one[:, 128:])
                    )

            pl.when(whole(kb))(lambda: put(False))
            pl.when(jnp.logical_not(whole(kb)))(lambda: put(True))
            return carry

        lax.fori_loop(first, end, scores, 0)
        top = jnp.max(high[...], axis=1, keepdims=True)
        high[...] = jnp.broadcast_to(top, high.shape)

        def values(kb, carry):
            at = pl.multiple_of(kb * KB, KB)
            for head in range(HL):
                rows = pl.ds(head * QB, QB)
                v = win[pl.ds(at, KB), pl.ds(LW + half_of(head), 128)]
                p = jnp.exp(sbuf[kb, rows, :] - high[rows, :1])
                low[rows, :] += p[:, :128] + p[:, 128:]
                acc[rows, :] += mm(p.astype(BF), v)
            return carry

        lax.fori_loop(first, end, values, 0)
        total = jnp.sum(low[...], axis=1, keepdims=True)
        inv = 1.0 / total
        out[pl.ds(block * QB, QB), :] = pick_heads(
            lambda head: acc[pl.ds(head * QB, QB), :] * inv[head * QB : (head + 1) * QB, :]
        ).astype(BF)
        flat = jnp.transpose(jnp.broadcast_to(top + jnp.log(total), (HL * QB, 128)))
        lt[pl.ds(block * 8, 8), :] = flat[:8, :]


def attend(starts, q, win):
    return call(
        attend_kernel,
        "attend",
        None,
        [starts, q, win],
        [((S, LW), BF), ((8 * (S // QB), HL * QB), F32)],
        [
            pltpu.VMEM((HL * QB, LW), BF),
            pltpu.VMEM((NB, HL * QB, KB), F32),
            pltpu.VMEM((HL * QB, 128), F32),
            pltpu.VMEM((HL * QB, 128), F32),
            pltpu.VMEM((HL * QB, 128), F32),
        ],
        0,
        limit=24,
        specs=[SM, VM, VM],
    )


def attend_back_kernel(starts, q, win, grad, att, lt, dq, dwin, qm, gm, dqa, dkv):
    base = lax.axis_index("dp") * S
    dkv[...] = jnp.zeros_like(dkv)
    head_row = lax.broadcasted_iota(jnp.int32, (8, LW), 0)
    lane_head = lax.div(lax.broadcasted_iota(jnp.int32, (8, LW), 1), HEAD_DIM)
    sums = (head_row == lane_head).astype(F32)
    for block in range(S // QB):
        rows = pl.ds(block * QB, QB)
        spread_heads(q[rows, :].astype(F32) * 0.125, qm)
        grad_rows = grad[rows, :].astype(F32)
        spread_heads(grad_rows, gm)
        both = grad_rows * att[rows, :].astype(F32)
        by_head = lax.dot_general(
            sums,
            both,
            (((1,), (1,)), ((), ())),
            precision=lax.Precision.HIGHEST,
            preferred_element_type=F32,
        )
        inner = jnp.concatenate([by_head[h : h + 1, :] for h in range(HL)], axis=1)
        logs = lt[pl.ds(block * 8, 1), :]
        qid = ids_of(
            base + block * QB + lax.broadcasted_iota(jnp.int32, (1, QB), 1), starts
        )
        first, end, whole = key_range(base, block, starts)
        dqa[...] = jnp.zeros_like(dqa)

        def one(kb, carry):
            at = pl.multiple_of(kb * KB, KB)

            def put(masked):
                keys = win[pl.ds(at, KB), :LW]
                vals = win[pl.ds(at, KB), LW:]
                st = mm_rt(keys, qm[...]) - logs
                dp = mm_rt(vals, gm[...])
                if masked:
                    kid = ids_of(
                        base - OWN0 + at + lax.broadcasted_iota(jnp.int32, (KB, 1), 0), starts
                    )
                    bias = jnp.where(kid == qid, 0.0, NEG)
                    st = st + jnp.concatenate([bias] * HL, axis=1)
                p = jnp.exp(st)
                ds = (p * (dp - inner)).astype(BF)
                dkv[pl.ds(at, KB), LW:] += mm(p.astype(BF), gm[...])
                dkv[pl.ds(at, KB), :LW] += mm(ds, qm[...])
                for head in range(HL):
                    part = keys[:, half_of(head) : half_of(head) + 128]
                    dqa[pl.ds(head * QB, QB), :] += mm_lt(ds[:, head * QB : (head + 1) * QB], part)

            pl.when(whole(kb))(lambda: put(False))
            pl.when(jnp.logical_not(whole(kb)))(lambda: put(True))
            return carry

        lax.fori_loop(first, end, one, 0)
        dq[rows, :] = (pick_heads(lambda head: dqa[pl.ds(head * QB, QB), :]) * 0.125).astype(BF)
    dwin[...] = dkv[...].astype(BF)


def attend_back(starts, q, win, grad, att, lt):
    return call(
        attend_back_kernel,
        "attend_back",
        None,
        [starts, q, win, grad, att, lt],
        [((S, LW), BF), ((NW, 2 * LW), BF)],
        [
            pltpu.VMEM((HL * QB, LW), BF),
            pltpu.VMEM((HL * QB, LW), BF),
            pltpu.VMEM((HL * QB, 128), F32),
            pltpu.VMEM((NW, 2 * LW), F32),
        ],
        0,
        limit=22,
        specs=[SM] + [VM] * 5,
    )


def outward_part(
    layer, at, wires, att, hidden_in, sc, ob, gain, bias, b1, wp, w1, w2, loads,
    mixed, br1, br2, rows, act, slope, bufs, between=None,
):
    load_p, load_1, load_2 = loads
    scatter = Scatter(wires, at, scatter_refs(bufs, 0))
    load_p.wait()
    scatter.everything(lambda first: mm(att[pl.ds(first, 2 * R), :], wp[...]))
    if between:
        between()
    one = scatter.total()
    br1[...] = one
    mix = hidden_in + sc[layer, 0:1, :] * (one + ob[layer, 0:1, :])
    mixed[...] = mix
    x_hat, _ = normalized(mix)
    rows[pl.ds(at.own, R), :] = (x_hat * gain[layer, 1:2, :] + bias[layer, 1:2, :]).astype(BF)
    gather = Gather(wires, at, rows)

    def hidden(part):
        x = part.load(rows)
        for j in range(F // 256):
            cols = pl.ds(j * 256, 256)
            pre = mm(x, w1[:, cols]) + b1[layer : layer + 1, cols]
            half = 0.5 * (1.0 + lax.erf(pre * (0.5**0.5)))
            part.store(act, (pre * half).astype(BF), cols)
            bell = jnp.exp(-0.5 * pre * pre) * 0.3989422804014327
            part.store(slope, (half + pre * bell).astype(BF), cols)

    load_1.wait()
    scatter = Scatter(wires, at, scatter_refs(bufs, 1))
    gather_hidden_scatter(
        at, gather, scatter, hidden, lambda part: mm(part.load(act), w2[...]), load_2.wait
    )
    two = scatter.total()
    br2[...] = two
    return mix + sc[layer, 1:2, :] * (two + ob[layer, 1:2, :])


OUT_SEMS = AG_SEMS + 2 * RS_SEMS
OUT_WEIGHTS = [pltpu.VMEM((LW, D), BF), pltpu.VMEM((D, F), BF), pltpu.VMEM((F, D), BF)]
OWN = ((R, D), F32)
TALL = ((S, D), BF)


def fetch_out(layer, wp_hbm, w1_hbm, w2_hbm, wp, w1, w2, ls, base):
    return [
        fetch(src.at[layer], dst, ls.at[base + k])
        for k, (src, dst) in enumerate(((wp_hbm, wp), (w1_hbm, w1), (w2_hbm, w2)))
    ]


def between_kernel(
    att, h, sc, ob, gain, bias, b1, b2, wp_hbm, w1_hbm, w2_hbm, w_hbm,
    mixed, br1, br2, nxt, rows_two, act, slope, rows_one, q, win,
    wp, w1, w2, w, relay, *rest,
):
    bufs = rest[:-3]
    ss, rs, ls = rest[-3:]
    at = Place()
    wires = Wires(ss, rs)
    loads = fetch_out(0, wp_hbm, w1_hbm, w2_hbm, wp, w1, w2, ls, 0)
    loads_qkv = fetch_qkv(1, w_hbm, w, ls, 3)
    greet(chain_partners(at))
    after = outward_part(
        0, at, wires, att, h[...].astype(F32), sc, ob, gain, bias, b1, wp, w1, w2, loads,
        mixed, br1, br2, rows_two, act, slope, bufs,
    )
    nxt[...] = after
    inward_part(
        1, at, wires, after, gain, bias, b2, w, loads_qkv, rows_one, q, win, relay
    )
    wires.close()


def between_layers(cid, *ins):
    return call(
        between_kernel, "between_layers", cid, ins,
        [OWN, OWN, OWN, OWN, TALL, TALL, TALL] + IN_OUTS,
        OUT_WEIGHTS + IN_SCRATCH + scatter_scratch(2),
        OUT_SEMS + IN_SEMS,
        limit=36, specs=[VM] * 8 + [ANY] * 4, local=6,
    )


def start_back(layer, at, wires, grad, sc, g2):
    g2[pl.ds(at.own, R), :] = (grad * sc[layer, 1:2, :]).astype(BF)
    return Gather(wires, at, g2)


def back_out_part(
    layer, at, wires, grad, gather, sc, ob, gain, mixed, br1, br2, act, slope, rows, att,
    wp, w1, w2, gmix, gatt, dw2_hbm, dw1_hbm, dwp, vec, fb, dw2, dw1, g2, gp, g1, bufs,
    ls, base, steps,
):
    vec[0:1, :] = jnp.sum(grad * (br2[...] + ob[layer, 1:2, :]), axis=0, keepdims=True)
    vec[1:2, :] = sc[layer, 1:2, :] * jnp.sum(grad, axis=0, keepdims=True)

    def hidden(part):
        x = part.load(g2)
        for j in range(F // 256):
            cols = pl.ds(j * 256, 256)
            up = mm_rt(x, w2[cols, :])
            part.store(gp, (up * part.load(slope, cols).astype(F32)).astype(BF), cols)

    scatter = Scatter(wires, at, bufs)
    gather_hidden_scatter(
        at, gather, scatter, hidden, lambda part: mm_rt(part.load(gp), w1[...]), lambda: None
    )
    steps(0)
    for j in range(D // 256):
        cols = pl.ds(j * 256, 256)
        dw2[cols, :] = mm_lt(g2[:, cols], act[...]).astype(BF)
    write_2 = fetch(dw2, dw2_hbm, ls.at[base])
    steps(1)
    for j in range(D // 256):
        cols = pl.ds(j * 256, 256)
        dw1[cols, :] = mm_lt(rows[:, cols], gp[...]).astype(BF)
    write_1 = fetch(dw1, dw1_hbm, ls.at[base + 1])
    fb[...] = jnp.broadcast_to(jnp.sum(gp[...].astype(F32), axis=0, keepdims=True), fb.shape)
    grad_in, grad_gain, grad_shift = norm_back(
        mixed[...], gain[layer, 1:2, :], scatter.total()
    )
    mix = grad + grad_in
    gmix[...] = mix
    g1[pl.ds(at.own, R), :] = (mix * sc[layer, 0:1, :]).astype(BF)
    gather = Gather(wires, at, g1)
    steps(2)
    vec[2:3, :] = grad_gain
    vec[3:4, :] = grad_shift
    vec[4:5, :] = jnp.sum(mix * (br1[...] + ob[layer, 0:1, :]), axis=0, keepdims=True)
    vec[5:6, :] = sc[layer, 0:1, :] * jnp.sum(mix, axis=0, keepdims=True)
    vec[6:8, :] = jnp.zeros((2, D), F32)
    gather.near()
    gatt[pl.ds(at.near, 2 * R), :] = mm_rt(g1[pl.ds(at.near, 2 * R), :], wp[...]).astype(BF)
    gather.far()
    steps(3)
    gatt[pl.ds(at.far, 2 * R), :] = mm_rt(g1[pl.ds(at.far, 2 * R), :], wp[...]).astype(BF)
    dwp[...] = mm_lt(g1[...], att[...]).astype(BF)
    steps(4)
    write_2.wait()
    write_1.wait()


BACK_OUTS = [
    OWN, ((S, LW), BF), ((D, F), BF), ((D, F), BF), ((D, LW), BF), ((8, D), F32), ((8, F), F32),
]
BACK_OUT_SPECS = [VM, VM, ANY, ANY, VM, VM, VM]
BACK_SCRATCH = [pltpu.VMEM((D, F), BF)] * 2 + [
    pltpu.VMEM((S, D), BF), pltpu.VMEM((S, F), BF), pltpu.VMEM((S, D), BF),
]
BACK_SEMS = 2 * AG_SEMS + RS_SEMS


def turn_kernel(
    att, h, sc, ob, gain, bias, b1, g, wp_hbm, w1_hbm, w2_hbm,
    out, gmix, gatt, dw2_hbm, dw1_hbm, dwp, vec, fb,
    wp, w1, w2, mixed, br1, br2, rows, act, slope, dw2, dw1, g2, gp, g1, *rest,
):
    bufs = rest[:-3]
    ss, rs, ls = rest[-3:]
    layer = 1
    at = Place()
    wires = Wires(ss, rs)
    loads = fetch_out(layer, wp_hbm, w1_hbm, w2_hbm, wp, w1, w2, ls, 0)
    greet([{"tensor": at.mate}, {"tensor": at.cp}])
    started = []
    after = outward_part(
        layer, at, wires, att, h[...].astype(F32), sc, ob, gain, bias, b1, wp, w1, w2, loads,
        mixed, br1, br2, rows, act, slope, bufs,
        lambda: started.append(start_back(layer, at, wires, g[...], sc, g2)),
    )
    out[...] = after.astype(BF)
    back_out_part(
        layer, at, wires, g[...], started[0], sc, ob, gain, mixed, br1, br2, act, slope, rows,
        att, wp, w1, w2, gmix, gatt, dw2_hbm, dw1_hbm, dwp, vec, fb, dw2, dw1, g2, gp, g1,
        scatter_refs(bufs, 2), ls, 3, lambda step: None,
    )
    wires.close()


def turn(cid, *ins):
    return call(
        turn_kernel, "turn", cid, ins,
        [((R, D), BF)] + BACK_OUTS,
        OUT_WEIGHTS
        + [pltpu.VMEM(*OWN)] * 3
        + [pltpu.VMEM(*TALL)] * 3
        + BACK_SCRATCH
        + scatter_scratch(3),
        OUT_SEMS + BACK_SEMS,
        limit=33, specs=[VM] * 8 + [ANY] * 3, local=5, out_specs=[VM] + BACK_OUT_SPECS,
    )


def back_in_part(
    layer, at, wires, dq, dwin, rows, gmix, h, gain, dwp, w, loads, dw, vec, qb, proj, lanes,
    bufs, steps,
):
    da, db, dc, ua, ub, uc, sdb, sdc, sub, suc = lanes
    chain_up, chain_dn = Line(wires, {"dp": at.up}), Line(wires, {"dp": at.dn})
    low3, low2, low1 = OWN0 - 3 * S, OWN0 - 2 * S, OWN0 - S
    high1, high2, high3 = OWN0 + S, OWN0 + 2 * S, OWN0 + 3 * S

    def chunk(ref, k, base=0):
        return ref.at[pl.ds(base + k * R, R)]

    def plus(base, k, other):
        mine = dwin[pl.ds(base + k * R, R), :].astype(F32)
        return (mine + other[pl.ds(k * R, R), :].astype(F32)).astype(BF)

    ups, dns = {}, {}

    def send(n, k, down, up):
        dns[n, k] = chain_dn.send(*down)
        ups[n, k] = chain_up.send(*up)

    def arrive(n, k):
        chain_dn.arrive(dns[n, k])
        chain_up.arrive(ups[n, k])

    def first(k):
        j = 3 - k
        send(
            1, k, (chunk(dwin, k, low3), chunk(da, k)), (chunk(dwin, j, high3), chunk(ua, j))
        )

    def second(k):
        j = 3 - k
        arrive(1, k)
        sdb[pl.ds(k * R, R), :] = plus(low2, k, da)
        sub[pl.ds(j * R, R), :] = plus(high2, j, ua)
        send(2, k, (chunk(sdb, k), chunk(db, k)), (chunk(sub, j), chunk(ub, j)))

    def third(k):
        j = 3 - k
        arrive(2, k)
        sdc[pl.ds(k * R, R), :] = plus(low1, k, db)
        suc[pl.ds(j * R, R), :] = plus(high1, j, ub)
        send(3, k, (chunk(sdc, k), chunk(dc, k)), (chunk(suc, j), chunk(uc, j)))

    for k in (1, 2, 3):
        first(k)
    send(2, 0, (chunk(dwin, 0, low2), chunk(db, 0)), (chunk(dwin, 3, high2), chunk(ub, 3)))
    def into(first, value):
        dw[:, :, :, :, pl.ds(first, value.shape[-1])] = as_blocks(value)

    proj[:, :LW] = dq[...]
    into(3 * LW, dwp[...])
    into(0, mm_lt(rows[...], dq[...]).astype(BF))
    for k in (1, 2, 3):
        second(k)
    for k in range(4):
        third(k)
    for k in range(4):
        arrive(3, k)
    steps(0)
    own = dwin[pl.ds(OWN0, S), :].astype(F32)
    proj[:, LW:] = (own + dc[...].astype(F32) + uc[...].astype(F32)).astype(BF)
    for copy in loads:
        copy.wait()
    scatter = Scatter(wires, at, bufs)
    scatter.everything(lambda first: mm_rt(proj[pl.ds(first, 2 * R), :], w[...]))
    into(LW, mm_lt(rows[...], proj[:, LW:]).astype(BF))
    steps(1)
    qb[...] = jnp.broadcast_to(jnp.sum(proj[...].astype(F32), axis=0, keepdims=True), qb.shape)
    grad_in, grad_gain, grad_shift = norm_back(
        h[...].astype(F32), gain[layer, 0:1, :], scatter.total()
    )
    vec[0:1, :] = grad_gain
    vec[1:2, :] = grad_shift
    vec[2:8, :] = jnp.zeros((6, D), F32)
    return gmix[...] + grad_in


BLOCKS = ((4, 2, 4, RP, 4 * LW), BF)
EIGHT, EIGHT3 = ((8, D), F32), ((8, 3 * LW), F32)
IN_BACK_SCRATCH = (
    [pltpu.VMEM((D, 3 * LW), BF), pltpu.VMEM((S, 3 * LW), BF)]
    + [pltpu.VMEM((S, 2 * LW), BF)] * 10
)
IN_BACK_SEMS = RS_SEMS + 22


def middle_kernel(*refs):
    take = Refs(refs).take
    dq, dwin, rows_one, gmix1, h, gain, dwp1, dw2_1, dw1_1 = take(9)
    sc, ob = take(2)
    late_hbm = take(7)
    wp_hbm, w1_hbm, w2_hbm, w_hbm = take(4)
    vec_in, qb, gmix, gatt, dw2_hbm, dw1_hbm, dwp, vec, fb = take(9)
    sums = take(NP)
    wp, w1, w2, dw2, dw1, g2, gp, g1 = take(8)
    w, proj = take(2)
    lanes = take(10)
    dw = take(1)[0]
    accs = take(NP)
    wide_bufs, narrow_bufs = take(NP * WIDE_REFS), take(NP * NARROW_REFS)
    bufs = take(2 + 2 * SCATTER_REFS)
    late = take(7)
    ss, rs, ls = take(3)
    at = Place()
    wires = Wires(ss, rs)
    loads = fetch_qkv(1, w_hbm, w, ls)
    loads_out = fetch_out(0, wp_hbm, w1_hbm, w2_hbm, wp, w1, w2, ls, 3)
    loads_out += [
        fetch(src, dst, ls.at[8 + 3 * NP + k]) for k, (src, dst) in enumerate(zip(late_hbm, late))
    ]
    mixed, br1, br2, act, slope, rows_two, att = late
    rings = Rings()
    wide = Wide(wires, rings, (dw2_1, dw1_1, dw), wide_bufs, ls, 8)
    narrow = Narrow(wires, rings, accs, narrow_bufs)
    greet(
        [{"tensor": at.mate}, {"tensor": at.cp}, {"dp": at.up}, {"dp": at.dn}]
        + rings.next_to()
        + [rings.other]
    )
    def steps_in(step):
        if step == 0:
            wide.start(0, 1)
        else:
            wide.start(2, 3)
            wide.forward(0, 1)

    def steps_out(step):
        if step == 0:
            wide.finish(accs, 0, 1)
            narrow.start(0, 1)
        elif step == 1:
            wide.finish(accs, 2, 3)
            narrow.start(2, 3)
            narrow.forward(0, 1)
        elif step == 2:
            narrow.forward(2, 3)
            narrow.beyond(0, 1)
        elif step == 3:
            narrow.beyond(2, 3)
        else:
            narrow.finish(sums)

    grad = back_in_part(
        1, at, wires, dq, dwin, rows_one, gmix1, h, gain, dwp1, w, loads, dw, vec_in, qb, proj,
        lanes, scatter_refs(bufs, 0), steps_in,
    )
    gather = start_back(0, at, wires, grad, sc, g2)
    wide.forward(2, 3)
    for copy in loads_out:
        copy.wait()
    back_out_part(
        0, at, wires, grad, gather, sc, ob, gain, mixed, br1, br2, act, slope, rows_two, att,
        wp, w1, w2, gmix, gatt, dw2_hbm, dw1_hbm, dwp, vec, fb, dw2, dw1, g2, gp, g1,
        scatter_refs(bufs, 1), ls, 6, steps_out,
    )
    wires.close()


def middle(cid, *ins):
    return call(
        middle_kernel, "middle", cid, ins,
        [EIGHT, EIGHT3] + BACK_OUTS + reduced_shapes(),
        OUT_WEIGHTS
        + BACK_SCRATCH
        + IN_BACK_SCRATCH
        + [pltpu.VMEM(*BLOCKS)]
        + [pltpu.VMEM(*wide_shape(width, mode)) for _, _, width, mode in PIECES]
        + wide_scratch()
        + narrow_scratch()
        + scatter_scratch(2)
        + [pltpu.VMEM(*OWN)] * 3
        + [pltpu.VMEM(*TALL)] * 3
        + [pltpu.VMEM((S, LW), BF)],
        IN_BACK_SEMS + BACK_SEMS + 13 * NP,
        limit=54,
        specs=[VM] * 7 + [ANY] * 2 + [VM] * 2 + [ANY] * 11,
        local=15 + 3 * NP,
        out_specs=[VM, VM] + BACK_OUT_SPECS + [VM] * NP,
    )


def final_kernel(*refs):
    take = Refs(refs).take
    dq, dwin, rows, gmix, h, gain, dwp = take(7)
    va1, va0, vb1, fb1, fb0, qb1 = take(6)
    dw2, dw1, w_hbm = take(3)
    g, vout = take(2)
    sums = take(NP)
    w, proj = take(2)
    lanes = take(10)
    dw, vec, qb = take(3)
    accs = take(NP)
    wide_bufs, narrow_bufs = take(NP * WIDE_REFS), take(NP * NARROW_REFS)
    vector_bufs = take(6)
    bufs = take(2 + SCATTER_REFS)
    ss, rs, ls = take(3)
    at = Place()
    wires = Wires(ss, rs)
    loads = fetch_qkv(0, w_hbm, w, ls)
    rings = Rings()
    wide = Wide(wires, rings, (dw2, dw1, dw), wide_bufs, ls, 3)
    narrow = Narrow(wires, rings, accs, narrow_bufs)
    vectors = Vectors(wires, at, rings, vector_bufs)
    greet(
        [{"tensor": at.mate}, {"tensor": at.cp}, {"dp": at.up}, {"dp": at.dn}]
        + [*rings.along_y, *rings.along_x, rings.other]
    )

    def steps(step):
        if step == 0:
            wide.start(0, 1)
        else:
            wide.forward(0, 1)
            wide.start(2, 3)

    g[...] = back_in_part(
        0, at, wires, dq, dwin, rows, gmix, h, gain, dwp, w, loads, dw, vec, qb, proj, lanes,
        bufs, steps,
    )
    vectors.fill(((va0, vec, fb0, qb), (va1, vb1, fb1, qb1)))
    wide.forward(2, 3)
    vectors.over_core()
    wide.finish(accs, 0, 1)
    narrow.start(0, 1)
    vectors.over_chip()
    wide.finish(accs, 2, 3)
    narrow.start(2, 3)
    vectors.over_y()
    narrow.forward(0, 1)
    narrow.forward(2, 3)
    vectors.over_x()
    narrow.beyond(0, 1, 2, 3)
    vectors.finish(vout)
    narrow.finish(sums)
    wires.close()


def final(cid, *ins):
    return call(
        final_kernel, "final", cid, ins,
        [OWN, (VEC, F32)] + reduced_shapes(),
        IN_BACK_SCRATCH
        + [pltpu.VMEM(*BLOCKS), pltpu.VMEM(*EIGHT), pltpu.VMEM(*EIGHT3)]
        + [pltpu.VMEM(*wide_shape(width, mode)) for _, _, width, mode in PIECES]
        + wide_scratch()
        + narrow_scratch()
        + vector_scratch()
        + scatter_scratch(1),
        IN_BACK_SEMS + 13 * NP + 9,
        limit=48,
        specs=[VM] * 13 + [ANY] * 3,
        local=3 + 3 * NP,
    )


def shards(
    tokens_in,
    image_starts,
    norm_gain,
    norm_bias,
    qkv_weight,
    qv_bias,
    proj_weight,
    out_bias,
    layer_scale,
    fc1_weight,
    fc1_bias,
    fc2_weight,
    out_grad,
):
    w_qkv = jnp.transpose(qkv_weight, (0, 2, 1, 3))
    norms = (norm_gain, norm_bias)
    out_weights = (proj_weight, fc1_weight, fc2_weight)
    one0, q0, win0 = inward(0, tokens_in, *norms, qv_bias, w_qkv)
    att0, lt0 = attend(image_starts, q0, win0)
    mixed, br1, br2, h1, two0, act, slope, one1, q1, win1 = between_layers(
        1, att0, tokens_in, layer_scale, out_bias, *norms, fc1_bias, qv_bias, *out_weights, w_qkv
    )
    att1, lt1 = attend(image_starts, q1, win1)
    hidden, gmix, gatt, dw2, dw1, dwp, va1, fb1 = turn(
        2, att1, h1, layer_scale, out_bias, *norms, fc1_bias, out_grad, *out_weights
    )
    dq, dwin = attend_back(image_starts, q1, win1, gatt, att1, lt1)
    vb1, qb1, gmix, gatt, dw2, dw1, dwp, va0, fb0, a1, b1, c1, d1 = middle(
        3, dq, dwin, one1, gmix, h1, norm_gain, dwp, as_blocks(dw2), as_blocks(dw1),
        layer_scale, out_bias, mixed, br1, br2, act, slope, two0, att0, *out_weights, w_qkv,
    )
    dq, dwin = attend_back(image_starts, q0, win0, gatt, att0, lt0)
    grad, vec, a0, b0, c0, d0 = final(
        4, dq, dwin, one0, gmix, tokens_in, norm_gain, dwp, va1, va0, vb1, fb1, fb0, qb1,
        as_blocks(dw2), as_blocks(dw1), w_qkv,
    )
    rows = vec[:16].reshape(2, 8, D)
    qkv = jnp.stack(
        [jnp.concatenate([c0, d0[:, :LW]], 1), jnp.concatenate([c1, d1[:, :LW]], 1)]
    )
    return (
        hidden,
        grad,
        jnp.stack([rows[:, 6], rows[:, 2]], 1),
        jnp.stack([rows[:, 7], rows[:, 3]], 1),
        qkv.reshape(2, RP, 3, LW),
        jnp.stack([vec[18:20, :LW], vec[18:20, 2 * LW : 3 * LW]], 1),
        jnp.stack([d0[:, LW:].T, d1[:, LW:].T]),
        jnp.stack([rows[:, 5], rows[:, 1]], 1),
        jnp.stack([rows[:, 4], rows[:, 0]], 1),
        jnp.stack([b0, b1]),
        vec[16:18],
        jnp.stack([a0.T, a1.T]),
    )


def solution(mesh):
    return jax.shard_map(
        shards,
        mesh=mesh,
        in_specs=(
            P(("dp", "tensor"), None),
            P(),
            P(),
            P(),
            P(None, None, None, "tensor"),
            P(None, None, "tensor"),
            P(None, "tensor", None),
            P(),
            P(),
            P(None, None, "tensor"),
            P(None, "tensor"),
            P(None, "tensor", None),
            P(("dp", "tensor"), None),
        ),
        out_specs=(
            P(("dp", "tensor"), None),
            P(("dp", "tensor"), None),
            P(),
            P(),
            P(None, "dp", None, "tensor"),
            P(None, None, "tensor"),
            P(None, "tensor", "dp"),
            P(),
            P(),
            P(None, "dp", "tensor"),
            P(None, "tensor"),
            P(None, "tensor", "dp"),
        ),
        check_vma=False,
    )
```

time: 609 us -> 481 us (0.79)
  Pallas kernels: 566 us -> 454 us
  local copies, waits for them, and re-layouts: 29.4 us -> 21.2 us
    pallas_call x13 -> x9, Pallas kernels: 566 us -> 454 us  [call(): pl.pallas_call(kernel, out_shape=shapes, in_specs=specs or [VM] * len(ins...]
    unnamed x17 -> x108, local copies, waits for them, and re-layouts: 4.7 us -> 20.4 us
    squeeze x4 -> x0, local copies, waits for them, and re-layouts: 9.98 us -> none  [the longest x1 4.9 us: shards(): fc2_weight[l]]
where the time goes in v3:
time: 481 us; the launch traced here: 480 us
  Pallas kernels  454 us (94%)
  local copies, waits for them, and re-layouts  21.2 us (4%)
    pallas_call x9, Pallas kernels, call(): pl.pallas_call(kernel, out_shape=shapes, in_specs=specs or [VM] * len(ins...  454 us
    unnamed x108, local copies, waits for them, and re-layouts  20.4 us

profile of v3, /device:TPU:0, one launch (start us, length us, event | category | flops | bytes accessed | tf_op | source)
XLA Modules:
  0.0 480.0 jit_solution(5665301714092457351)
XLA Ops:
  0.7 1.9 copy-done
  2.6 0.9 copy-done.11
  5.7 64.9 %inward.1 = (bf16[512,1024]{1,0:T(8,128)(2,1)S(1)}, bf16[512,256]{1,0:T(8,128)(2,1)S(1)}, bf16[3328,512]{1,0:T(8,128)(2,1)S(1)}) custom-call(bf16[128,1024]{1,0:T(8,128)(2,1)S(1)} %copy-done.11, f32[2,2,1024]{2,1,0:T(2,128)S(1)} %copy-done.31, f32[2,2,1024]{2,1,0:T(2,128)S(1)} %copy-done.36, f32[2,2,256]{2,1,0:T(2,128)S(1)} %copy-done.45, ...), custom_call_target="tpu_custom_call" | custom-call | tf_op jit(solution)/shard_map/inward/pallas_call | solution.py:364
  70.6 1.0 copy-done.17
  71.6 12.8 %attend.2 = (bf16[512,256]{1,0:T(8,128)(2,1)S(1)}, f32[16,1024]{1,0:T(8,128)S(1)}) custom-call(s32[11]{0:T(128)S(1)} %copy-done.47, bf16[512,256]{1,0:T(8,128)(2,1)S(1)} %get-tuple-element.60.q, bf16[3328,512]{1,0:T(8,128)(2,1)S(1)} %get-tuple-element.61.win), custom_call_target="tpu_custom_call" | custom-call | tf_op jit(solution)/shard_map/attend/pallas_call | solution.py:364
  84.5 86.5 %between_layers.1 = (f32[128,1024]{1,0:T(8,128)S(1)}, f32[128,1024]{1,0:T(8,128)S(1)}, f32[128,1024]{1,0:T(8,128)S(1)}, f32[128,1024]{1,0:T(8,128)S(1)}, bf16[51...) custom-call(bf16[512,256]{1,0:T(8,128)(2,1)S(1)} %get-tuple-element., ...), custom_call_target="tpu_custom_call" | custom-call | tf_op jit(solution)/shard_map/between_layers/pallas_call | solution.py:364
  171.0 1.0 copy-done.22
  172.0 13.0 %attend.3 = (bf16[512,256]{1,0:T(8,128)(2,1)S(1)}, f32[16,1024]{1,0:T(8,128)S(1)}) custom-call(s32[11]{0:T(128)S(1)} %copy-done.47, bf16[512,256]{1,0:T(8,128)(2,1)S(1)} %get-tuple-element.63.q, bf16[3328,512]{1,0:T(8,128)(2,1)S(1)} %get-tuple-element.64.win), custom_call_target="tpu_custom_call" | custom-call | tf_op jit(solution)/shard_map/attend/pallas_call | solution.py:364
  185.1 2.2 copy-done.3
  187.3 52.2 %turn.1 = (bf16[128,1024]{1,0:T(8,128)(2,1)S(1)}, f32[128,1024]{1,0:T(8,128)S(1)}, bf16[512,256]{1,0:T(8,128)(2,1)S(1)}, bf16[1024,1024]{1,0:T(8,128)(2,1)S(1)},...) custom-call(bf16[512,256]{1,0:T(8,128)(2,1)S(1)} %get-tuple-element., ...), custom_call_target="tpu_custom_call" | custom-call | tf_op jit(solution)/shard_map/turn/pallas_call | solution.py:364
  239.5 0.8 copy-done.29
  240.3 0.8 copy-done.30
  241.1 17.5 %attend_back.2 = (bf16[512,256]{1,0:T(8,128)(2,1)S(1)}, bf16[3328,512]{1,0:T(8,128)(2,1)S(1)}) custom-call(s32[11]{0:T(128)S(1)} %copy-done.47, bf16[512,256]{1,0:T(8,128)(2,1)S(1)} %get-tuple-element.63.q, bf16[3328,512]{1,0:T(8,128)(2,1)S(1)} %get-tuple-element.64.win, bf16[512,256]{1,0:T(8,128)(2,1)S(1)} %get-tuple-element.68.grad, ...), custom_call_target="tpu_custom_call" | custom-call | tf_op jit(solution)/shard_map/attend_back/pallas_call | solution.py:364
  258.7 1.7 copy-done.7
  261.1 92.5 %middle.1 = (f32[8,1024]{1,0:T(8,128)}, f32[8,768]{1,0:T(8,128)}, f32[128,1024]{1,0:T(8,128)}, bf16[512,256]{1,0:T(8,128)(2,1)}, bf16[1024,1024]{1,0:T(8,128)(2,...) custom-call(bf16[512,256]{1,0:T(8,128)(2,1)} %copy-done.34, ...), custom_call_target="tpu_custom_call" | custom-call | tf_op jit(solution)/shard_map/middle/pallas_call | solution.py:364
  353.7 1.1 copy-done.35
  354.8 17.7 %attend_back.3 = (bf16[512,256]{1,0:T(8,128)(2,1)S(1)}, bf16[3328,512]{1,0:T(8,128)(2,1)S(1)}) custom-call(s32[11]{0:T(128)S(1)} %copy-done.47, bf16[512,256]{1,0:T(8,128)(2,1)S(1)} %get-tuple-element.60.q, bf16[3328,512]{1,0:T(8,128)(2,1)S(1)} %copy-done.5, bf16[512,256]{1,0:T(8,128)(2,1)S(1)} %copy-done.35, bf16[512,256]{1,0:T(8,128)(2,1)S(1)} %copy-done.10, ...), custom_call_target="tpu_custom_call" | custom-call | tf_op jit(solution)/shard_map/attend_back/pallas_call | solution.py:364
  372.6 1.7 copy-done.8
  374.4 0.7 copy-done.42
  375.1 0.7 copy-done.44
  375.9 96.6 %final.1 = (f32[128,1024]{1,0:T(8,128)S(1)}, f32[24,1024]{1,0:T(8,128)S(1)}, f32[32,1024]{1,0:T(8,128)S(1)}, f32[32,1024]{1,0:T(8,128)S(1)}, f32[32,512]{1,0:T(8,128)S(1)}, /*index=5*/f32[32,512]{1,0:T(8,128)S(1)}) custom-call(bf16[512,256]{1,0:T(8,128)(2,1)S(1)} %get-tuple-element.85.refs_0_, bf16[3328,512]{1,0:T(8,128)(2,1)} %copy-done.8, ...), custom_call_target="tpu_custom_call" | custom-call | tf_op jit(solution)/shard_map/final/pallas_call | solution.py:364
  476.6 0.7 pad_maximum_fusion.1
  477.3 0.7 pad_maximum_fusion.2
  478.8 0.8 copy.33
  (109 shorter events, 7.8 us)
Async XLA Ops:
  0.6 70.9 %copy-start.47 = (s32[11]{0:T(128)S(1)}, s32[11]{0:T(128)}, u32[]{:S(2)}) copy-start(s32[11]{0:T(128)} %starts.7) | copy-start | bytes 136
  5.6 78.8 %copy-start.1 = (bf16[2,1024,3,256]{3,1,2,0:T(8,128)(2,1)S(1)}, bf16[2,1024,3,256]{3,1,2,0:T(8,128)(2,1)}, u32[]{:S(2)}) copy-start(bf16[2,1024,3,256]{3,1,2,0:T(8,128)(2,1)} %param.17) | copy-start | bytes 9437188
  5.6 78.8 %copy-start.6 = (bf16[2,256,1024]{2,1,0:T(8,128)(2,1)S(1)}, bf16[2,256,1024]{2,1,0:T(8,128)(2,1)}, u32[]{:S(2)}) copy-start(bf16[2,256,1024]{2,1,0:T(8,128)(2,1)} %refs_18_.1) | copy-start | bytes 3145732
  5.6 78.8 %copy-start.12 = (bf16[128,1024]{1,0:T(8,128)(2,1)S(1)}, bf16[128,1024]{1,0:T(8,128)(2,1)}, u32[]{:S(2)}) copy-start(bf16[128,1024]{1,0:T(8,128)(2,1)} %refs_4_.1) | copy-start | bytes 786436
  5.6 78.8 %copy-start.32 = (f32[2,2,1024]{2,1,0:T(2,128)S(1)}, f32[2,2,1024]{2,1,0:T(2,128)}, u32[]{:S(2)}) copy-start(f32[2,2,1024]{2,1,0:T(2,128)} %refs_5_.3) | copy-start | bytes 49156
  5.6 78.8 %copy-start.37 = (f32[2,2,1024]{2,1,0:T(2,128)S(1)}, f32[2,2,1024]{2,1,0:T(2,128)}, u32[]{:S(2)}) copy-start(f32[2,2,1024]{2,1,0:T(2,128)} %bias.5) | copy-start | bytes 49156
  5.6 78.8 %copy-start.38 = (f32[2,2,1024]{2,1,0:T(2,128)S(1)}, f32[2,2,1024]{2,1,0:T(2,128)}, u32[]{:S(2)}) copy-start(f32[2,2,1024]{2,1,0:T(2,128)} %refs_9_.1) | copy-start | bytes 49156
  5.7 78.8 %copy-start.39 = (f32[2,2,1024]{2,1,0:T(2,128)S(1)}, f32[2,2,1024]{2,1,0:T(2,128)}, u32[]{:S(2)}) copy-start(f32[2,2,1024]{2,1,0:T(2,128)} %refs_10_.1) | copy-start | bytes 49156
  5.7 78.8 %copy-start.43 = (f32[2,1024]{1,0:T(2,128)S(1)}, f32[2,1024]{1,0:T(2,128)}, u32[]{:S(2)}) copy-start(f32[2,1024]{1,0:T(2,128)} %b1.3) | copy-start | bytes 24580
  5.7 78.8 %copy-start.46 = (f32[2,2,256]{2,1,0:T(2,128)S(1)}, f32[2,2,256]{2,1,0:T(2,128)}, u32[]{:S(2)}) copy-start(f32[2,2,256]{2,1,0:T(2,128)} %b2.3) | copy-start | bytes 12292
  84.4 86.6 %copy-start.9 = (bf16[512,256]{1,0:T(8,128)(2,1)}, bf16[512,256]{1,0:T(8,128)(2,1)S(1)}, u32[]{:S(2)}) copy-start(bf16[512,256]{1,0:T(8,128)(2,1)S(1)} %get-tuple-element.62.att.refs_17_) | copy-start | bytes 786436
  84.5 100.6 %copy-start.2 = (bf16[2,1024,1024]{2,1,0:T(8,128)(2,1)S(1)}, bf16[2,1024,1024]{2,1,0:T(8,128)(2,1)}, u32[]{:S(2)}) copy-start(bf16[2,1024,1024]{2,1,0:T(8,128)(2,1)} %refs_19_.1) | copy-start | bytes 12582916
  172.0 67.5 %copy-start.15 = (f32[128,1024]{1,0:T(8,128)}, f32[128,1024]{1,0:T(8,128)S(1)}, u32[]{:S(2)}) copy-start(f32[128,1024]{1,0:T(8,128)S(1)} %get-tuple-element.66.h.refs_4_) | copy-start | bytes 1572868
  172.0 67.5 %copy-start.19 = (bf16[512,1024]{1,0:T(8,128)(2,1)}, bf16[512,1024]{1,0:T(8,128)(2,1)S(1)}, u32[]{:S(2)}) copy-start(bf16[512,1024]{1,0:T(8,128)(2,1)S(1)} %get-tuple-element.82.refs_16_) | copy-start | bytes 3145732
  172.0 67.5 %copy-start.20 = (bf16[512,1024]{1,0:T(8,128)(2,1)}, bf16[512,1024]{1,0:T(8,128)(2,1)S(1)}, u32[]{:S(2)}) copy-start(bf16[512,1024]{1,0:T(8,128)(2,1)S(1)} %get-tuple-element.80.refs_14_) | copy-start | bytes 3145732
  172.0 67.5 %copy-start.24 = (f32[128,1024]{1,0:T(8,128)}, f32[128,1024]{1,0:T(8,128)S(1)}, u32[]{:S(2)}) copy-start(f32[128,1024]{1,0:T(8,128)S(1)} %get-tuple-element.77.refs_11_) | copy-start | bytes 1572868
  172.0 67.5 %copy-start.25 = (f32[128,1024]{1,0:T(8,128)}, f32[128,1024]{1,0:T(8,128)S(1)}, u32[]{:S(2)}) copy-start(f32[128,1024]{1,0:T(8,128)S(1)} %get-tuple-element.78.refs_12_) | copy-start | bytes 1572868
  172.0 67.5 %copy-start.26 = (f32[128,1024]{1,0:T(8,128)}, f32[128,1024]{1,0:T(8,128)S(1)}, u32[]{:S(2)}) copy-start(f32[128,1024]{1,0:T(8,128)S(1)} %get-tuple-element.79.refs_13_) | copy-start | bytes 1572868
  261.1 92.6 %copy-start.5 = (bf16[3328,512]{1,0:T(8,128)(2,1)S(1)}, bf16[3328,512]{1,0:T(8,128)(2,1)}, u32[]{:S(2)}) copy-start(bf16[3328,512]{1,0:T(8,128)(2,1)} %copy-done.4) | copy-start | bytes 10223620
  261.1 92.6 %copy-start.10 = (bf16[512,256]{1,0:T(8,128)(2,1)S(1)}, bf16[512,256]{1,0:T(8,128)(2,1)}, u32[]{:S(2)}) copy-start(bf16[512,256]{1,0:T(8,128)(2,1)} %copy-done.9) | copy-start | bytes 786436
  375.8 99.2 %copy-start.51 = (f32[32,512]{1,0:T(8,128)S(1)}, f32[32,512]{1,0:T(8,128)}, u32[]{:S(2)}) copy-start(f32[32,512]{1,0:T(8,128)} %get-tuple-element.103) | copy-start | bytes 196612
  375.8 99.8 %copy-start.50 = (f32[32,512]{1,0:T(8,128)S(1)}, f32[32,512]{1,0:T(8,128)}, u32[]{:S(2)}) copy-start(f32[32,512]{1,0:T(8,128)} %get-tuple-element.102) | copy-start | bytes 196612
  375.9 100.8 %copy-start.49 = (f32[32,1024]{1,0:T(8,128)S(1)}, f32[32,1024]{1,0:T(8,128)}, u32[]{:S(2)}) copy-start(f32[32,1024]{1,0:T(8,128)} %get-tuple-element.105) | copy-start | bytes 393220
  375.9 101.5 %copy-start.48 = (f32[32,1024]{1,0:T(8,128)S(1)}, f32[32,1024]{1,0:T(8,128)}, u32[]{:S(2)}) copy-start(f32[32,1024]{1,0:T(8,128)} %get-tuple-element.107) | copy-start | bytes 393220
  (28 other events, 238.8 us)

commit v4 on v3

--- a/solution.py
+++ b/solution.py
@@ -758,11 +758,13 @@
     for k in range(starts.shape[0]):
         for at in (starts[k], starts[k] + IMG_LEN):
             edge = edge | ((at > first) & (at <= last))
-    low, high = low - base + OWN0, high - base + OWN0
-    low_block = lax.div(jnp.maximum(low, 0), KB)
-    high_block = lax.div(jnp.minimum(high, NW) + KB - 1, KB)
-    whole = lambda kb: jnp.logical_not(edge) & (kb * KB >= low) & (kb * KB + KB <= high)
-    return low_block, high_block, whole
+    low = jnp.maximum(low - base + OWN0, 0)
+    high = jnp.minimum(high - base + OWN0, NW)
+    start = lax.div(low, 128) * 128
+    tiles = lax.div(high - start + KB - 1, KB)
+    start = jnp.minimum(start, NW - tiles * KB)
+    whole = lambda at: jnp.logical_not(edge) & (at >= low) & (at + KB <= high)
+    return start, tiles, whole
 
 
 def spread_heads(value, out):
@@ -791,13 +793,13 @@
         qid = ids_of(
             base + block * QB + lax.broadcasted_iota(jnp.int32, (QB, 1), 0), starts
         )
-        first, end, whole = key_range(base, block, starts)
+        start, tiles, whole = key_range(base, block, starts)
         high[...] = jnp.full_like(high, NEG)
         low[...] = jnp.zeros_like(low)
         acc[...] = jnp.zeros_like(acc)
 
         def scores(kb, carry):
-            at = pl.multiple_of(kb * KB, KB)
+            at = pl.multiple_of(start + kb * KB, 128)
 
             def put(masked):
                 s = mm_rt(qm[...], win[pl.ds(at, KB), :LW])
@@ -816,16 +818,16 @@
                         high[rows, :], jnp.maximum(one[:, :128], one[:, 128:])
                     )
 
-            pl.when(whole(kb))(lambda: put(False))
-            pl.when(jnp.logical_not(whole(kb)))(lambda: put(True))
+            pl.when(whole(at))(lambda: put(False))
+            pl.when(jnp.logical_not(whole(at)))(lambda: put(True))
             return carry
 
-        lax.fori_loop(first, end, scores, 0)
+        lax.fori_loop(0, tiles, scores, 0)
         top = jnp.max(high[...], axis=1, keepdims=True)
         high[...] = jnp.broadcast_to(top, high.shape)
 
         def values(kb, carry):
-            at = pl.multiple_of(kb * KB, KB)
+            at = pl.multiple_of(start + kb * KB, 128)
             for head in range(HL):
                 rows = pl.ds(head * QB, QB)
                 v = win[pl.ds(at, KB), pl.ds(LW + half_of(head), 128)]
@@ -834,7 +836,7 @@
                 acc[rows, :] += mm(p.astype(BF), v)
             return carry
 
-        lax.fori_loop(first, end, values, 0)
+        lax.fori_loop(0, tiles, values, 0)
         total = jnp.sum(low[...], axis=1, keepdims=True)
         inv = 1.0 / total
         out[pl.ds(block * QB, QB), :] = pick_heads(
@@ -888,11 +890,11 @@
         qid = ids_of(
             base + block * QB + lax.broadcasted_iota(jnp.int32, (1, QB), 1), starts
         )
-        first, end, whole = key_range(base, block, starts)
+        start, tiles, whole = key_range(base, block, starts)
         dqa[...] = jnp.zeros_like(dqa)
 
         def one(kb, carry):
-            at = pl.multiple_of(kb * KB, KB)
+            at = pl.multiple_of(start + kb * KB, 128)
 
             def put(masked):
                 keys = win[pl.ds(at, KB), :LW]
@@ -913,11 +915,11 @@
                     part = keys[:, half_of(head) : half_of(head) + 128]
                     dqa[pl.ds(head * QB, QB), :] += mm_lt(ds[:, head * QB : (head + 1) * QB], part)
 
-            pl.when(whole(kb))(lambda: put(False))
-            pl.when(jnp.logical_not(whole(kb)))(lambda: put(True))
+            pl.when(whole(at))(lambda: put(False))
+            pl.when(jnp.logical_not(whole(at)))(lambda: put(True))
             return carry
 
-        lax.fori_loop(first, end, one, 0)
+        lax.fori_loop(0, tiles, one, 0)
         dq[rows, :] = (pick_heads(lambda head: dqa[pl.ds(head * QB, QB), :]) * 0.125).astype(BF)
     dwin[...] = dkv[...].astype(BF)
 
@@ -1131,7 +1133,7 @@
         + BACK_SCRATCH
         + scatter_scratch(3),
         OUT_SEMS + BACK_SEMS,
-        limit=33, specs=[VM] * 8 + [ANY] * 3, local=5, out_specs=[VM] + BACK_OUT_SPECS,
+        limit=44, specs=[VM] * 8 + [ANY] * 3, local=5, out_specs=[VM] + BACK_OUT_SPECS,
     )
 
 
@@ -1312,7 +1314,7 @@
         + [pltpu.VMEM(*TALL)] * 3
         + [pltpu.VMEM((S, LW), BF)],
         IN_BACK_SEMS + BACK_SEMS + 13 * NP,
-        limit=54,
+        limit=51,
         specs=[VM] * 7 + [ANY] * 2 + [VM] * 2 + [ANY] * 11,
         local=15 + 3 * NP,
         out_specs=[VM, VM] + BACK_OUT_SPECS + [VM] * NP,

time: 481 us -> 473 us (0.983); the launches traced: 480 us -> 467 us
  Pallas kernels: 454 us -> 445 us
    pallas_call x9, Pallas kernels: 454 us -> 445 us  [call(): pl.pallas_call(kernel, out_shape=shapes, in_specs=specs or [VM] * len(ins...]
    unnamed x108 -> x76, local copies, waits for them, and re-layouts: 20.4 us -> 16.2 us
where the time goes in v4:
time: 473 us; the launch traced here: 467 us
  Pallas kernels  445 us (94%)
  local copies, waits for them, and re-layouts  17 us (4%)
    pallas_call x9, Pallas kernels, call(): pl.pallas_call(kernel, out_shape=shapes, in_specs=specs or [VM] * len(ins...  445 us
    unnamed x76, local copies, waits for them, and re-layouts  16.2 us

profile of v4, /device:TPU:0, one launch (start us, length us, event | category | flops | bytes accessed | tf_op | source)
XLA Modules:
  0.0 466.9 jit_solution(5210468527633129298)
XLA Ops:
  0.7 1.9 copy-done
  2.6 0.9 copy-done.5
  3.5 0.7 copy-done.24
  4.2 0.7 copy-done.28
  5.7 64.9 %inward.1 = (bf16[512,1024]{1,0:T(8,128)(2,1)S(1)}, bf16[512,256]{1,0:T(8,128)(2,1)S(1)}, bf16[3328,512]{1,0:T(8,128)(2,1)S(1)}) custom-call(bf16[128,1024]{1,0:T(8,128)(2,1)S(1)} %copy-done.5, f32[2,2,1024]{2,1,0:T(2,128)S(1)} %copy-done.24, f32[2,2,1024]{2,1,0:T(2,128)S(1)} %copy-done.28, f32[2,2,256]{2,1,0:T(2,128)S(1)} %copy-done.33, ...), custom_call_target="tpu_custom_call" | custom-call | tf_op jit(solution)/shard_map/inward/pallas_call | solution.py:364
  70.6 1.0 copy-done.11
  71.6 11.4 %attend.2 = (bf16[512,256]{1,0:T(8,128)(2,1)S(1)}, f32[16,1024]{1,0:T(8,128)S(1)}) custom-call(s32[11]{0:T(128)S(1)} %copy-done.35, bf16[512,256]{1,0:T(8,128)(2,1)S(1)} %get-tuple-element.60.q, bf16[3328,512]{1,0:T(8,128)(2,1)S(1)} %get-tuple-element.61.win), custom_call_target="tpu_custom_call" | custom-call | tf_op jit(solution)/shard_map/attend/pallas_call | solution.py:364
  83.2 86.4 %between_layers.1 = (f32[128,1024]{1,0:T(8,128)S(1)}, f32[128,1024]{1,0:T(8,128)S(1)}, f32[128,1024]{1,0:T(8,128)S(1)}, f32[128,1024]{1,0:T(8,128)S(1)}, bf16[51...) custom-call(bf16[512,256]{1,0:T(8,128)(2,1)S(1)} %get-tuple-element., ...), custom_call_target="tpu_custom_call" | custom-call | tf_op jit(solution)/shard_map/between_layers/pallas_call | solution.py:364
  169.6 0.8 copy-done.20
  170.4 0.8 copy-done.21
  171.2 0.8 copy-done.22
  172.1 11.6 %attend.3 = (bf16[512,256]{1,0:T(8,128)(2,1)S(1)}, f32[16,1024]{1,0:T(8,128)S(1)}) custom-call(s32[11]{0:T(128)S(1)} %copy-done.35, bf16[512,256]{1,0:T(8,128)(2,1)S(1)} %get-tuple-element.63.q, bf16[3328,512]{1,0:T(8,128)(2,1)S(1)} %get-tuple-element.64.win), custom_call_target="tpu_custom_call" | custom-call | tf_op jit(solution)/shard_map/attend/pallas_call | solution.py:364
  183.7 52.1 %turn.1 = (bf16[128,1024]{1,0:T(8,128)(2,1)S(1)}, f32[128,1024]{1,0:T(8,128)S(1)}, bf16[512,256]{1,0:T(8,128)(2,1)S(1)}, bf16[1024,1024]{1,0:T(8,128)(2,1)S(1)},...) custom-call(bf16[512,256]{1,0:T(8,128)(2,1)S(1)} %get-tuple-element., ...), custom_call_target="tpu_custom_call" | custom-call | tf_op jit(solution)/shard_map/turn/pallas_call | solution.py:364
  235.8 0.8 copy-done.23
  237.3 15.5 %attend_back.2 = (bf16[512,256]{1,0:T(8,128)(2,1)S(1)}, bf16[3328,512]{1,0:T(8,128)(2,1)S(1)}) custom-call(s32[11]{0:T(128)S(1)} %copy-done.35, bf16[512,256]{1,0:T(8,128)(2,1)S(1)} %get-tuple-element.63.q, bf16[3328,512]{1,0:T(8,128)(2,1)S(1)} %get-tuple-element.64.win, bf16[512,256]{1,0:T(8,128)(2,1)S(1)} %get-tuple-element.68.grad, ...), custom_call_target="tpu_custom_call" | custom-call | tf_op jit(solution)/shard_map/attend_back/pallas_call | solution.py:364
  252.8 1.7 copy-done.3
  254.5 90.8 %middle.1 = (f32[8,1024]{1,0:T(8,128)S(1)}, f32[8,768]{1,0:T(8,128)S(1)}, f32[128,1024]{1,0:T(8,128)S(1)}, bf16[512,256]{1,0:T(8,128)(2,1)S(1)}, bf16[1024,1024]...) custom-call(bf16[512,256]{1,0:T(8,128)(2,1)S(1)} %get-tuple-element., ...), custom_call_target="tpu_custom_call" | custom-call | tf_op jit(solution)/shard_map/middle/pallas_call | solution.py:364
  345.4 15.7 %attend_back.3 = (bf16[512,256]{1,0:T(8,128)(2,1)S(1)}, bf16[3328,512]{1,0:T(8,128)(2,1)S(1)}) custom-call(s32[11]{0:T(128)S(1)} %copy-done.35, bf16[512,256]{1,0:T(8,128)(2,1)S(1)} %copy-done.18, bf16[3328,512]{1,0:T(8,128)(2,1)S(1)} %get-tuple-element.61.win, bf16[512,256]{1,0:T(8,128)(2,1)S(1)} %get-tuple-element.83.grad, ...), custom_call_target="tpu_custom_call" | custom-call | tf_op jit(solution)/shard_map/attend_back/pallas_call | solution.py:364
  361.1 1.7 copy-done.4
  362.8 96.6 %final.1 = (f32[128,1024]{1,0:T(8,128)S(1)}, f32[24,1024]{1,0:T(8,128)S(1)}, f32[32,1024]{1,0:T(8,128)S(1)}, f32[32,1024]{1,0:T(8,128)S(1)}, f32[32,512]{1,0:T(8,128)S(1)}, /*index=5*/f32[32,512]{1,0:T(8,128)S(1)}) custom-call(bf16[512,256]{1,0:T(8,128)(2,1)S(1)} %get-tuple-element.85.refs_0_, bf16[3328,512]{1,0:T(8,128)(2,1)} %copy-done.4, ...), custom_call_target="tpu_custom_call" | custom-call | tf_op jit(solution)/shard_map/final/pallas_call | solution.py:364
  462.8 0.7 copy.28
  463.5 0.7 pad_maximum_fusion.1
  464.2 0.7 pad_maximum_fusion.2
  465.6 0.8 copy.33
  (77 shorter events, 5.6 us)
Async XLA Ops:
  0.6 71.0 %copy-start.35 = (s32[11]{0:T(128)S(1)}, s32[11]{0:T(128)}, u32[]{:S(2)}) copy-start(s32[11]{0:T(128)} %starts.7) | copy-start | bytes 136
  0.7 1.9 copy-start
  5.6 77.4 %copy-start.1 = (bf16[2,1024,3,256]{3,1,2,0:T(8,128)(2,1)S(1)}, bf16[2,1024,3,256]{3,1,2,0:T(8,128)(2,1)}, u32[]{:S(2)}) copy-start(bf16[2,1024,3,256]{3,1,2,0:T(8,128)(2,1)} %param.17) | copy-start | bytes 9437188
  5.6 77.4 %copy-start.2 = (bf16[2,256,1024]{2,1,0:T(8,128)(2,1)S(1)}, bf16[2,256,1024]{2,1,0:T(8,128)(2,1)}, u32[]{:S(2)}) copy-start(bf16[2,256,1024]{2,1,0:T(8,128)(2,1)} %refs_18_.1) | copy-start | bytes 3145732
  5.6 77.5 %copy-start.6 = (bf16[128,1024]{1,0:T(8,128)(2,1)S(1)}, bf16[128,1024]{1,0:T(8,128)(2,1)}, u32[]{:S(2)}) copy-start(bf16[128,1024]{1,0:T(8,128)(2,1)} %refs_4_.1) | copy-start | bytes 786436
  5.6 77.5 %copy-start.25 = (f32[2,2,1024]{2,1,0:T(2,128)S(1)}, f32[2,2,1024]{2,1,0:T(2,128)}, u32[]{:S(2)}) copy-start(f32[2,2,1024]{2,1,0:T(2,128)} %refs_5_.3) | copy-start | bytes 49156
  5.6 77.5 %copy-start.29 = (f32[2,2,1024]{2,1,0:T(2,128)S(1)}, f32[2,2,1024]{2,1,0:T(2,128)}, u32[]{:S(2)}) copy-start(f32[2,2,1024]{2,1,0:T(2,128)} %bias.5) | copy-start | bytes 49156
  5.6 77.5 %copy-start.30 = (f32[2,2,1024]{2,1,0:T(2,128)S(1)}, f32[2,2,1024]{2,1,0:T(2,128)}, u32[]{:S(2)}) copy-start(f32[2,2,1024]{2,1,0:T(2,128)} %refs_9_.1) | copy-start | bytes 49156
  5.7 77.5 %copy-start.31 = (f32[2,2,1024]{2,1,0:T(2,128)S(1)}, f32[2,2,1024]{2,1,0:T(2,128)}, u32[]{:S(2)}) copy-start(f32[2,2,1024]{2,1,0:T(2,128)} %refs_10_.1) | copy-start | bytes 49156
  5.7 77.5 %copy-start.32 = (f32[2,1024]{1,0:T(2,128)S(1)}, f32[2,1024]{1,0:T(2,128)}, u32[]{:S(2)}) copy-start(f32[2,1024]{1,0:T(2,128)} %b1.3) | copy-start | bytes 24580
  5.7 77.5 %copy-start.34 = (f32[2,2,256]{2,1,0:T(2,128)S(1)}, f32[2,2,256]{2,1,0:T(2,128)}, u32[]{:S(2)}) copy-start(f32[2,2,256]{2,1,0:T(2,128)} %b2.3) | copy-start | bytes 12292
  71.6 11.5 %copy-start.17 = (bf16[512,256]{1,0:T(8,128)(2,1)}, bf16[512,256]{1,0:T(8,128)(2,1)S(1)}, u32[]{:S(2)}) copy-start(bf16[512,256]{1,0:T(8,128)(2,1)S(1)} %get-tuple-element.60.q) | copy-start | bytes 786436
  172.0 11.6 %copy-start.13 = (bf16[512,1024]{1,0:T(8,128)(2,1)}, bf16[512,1024]{1,0:T(8,128)(2,1)S(1)}, u32[]{:S(2)}) copy-start(bf16[512,1024]{1,0:T(8,128)(2,1)S(1)} %get-tuple-element.82.refs_16_) | copy-start | bytes 3145732
  172.0 11.6 %copy-start.14 = (bf16[512,1024]{1,0:T(8,128)(2,1)}, bf16[512,1024]{1,0:T(8,128)(2,1)S(1)}, u32[]{:S(2)}) copy-start(bf16[512,1024]{1,0:T(8,128)(2,1)S(1)} %get-tuple-element.80.refs_14_) | copy-start | bytes 3145732
  172.0 11.7 %copy-start.15 = (bf16[512,1024]{1,0:T(8,128)(2,1)}, bf16[512,1024]{1,0:T(8,128)(2,1)S(1)}, u32[]{:S(2)}) copy-start(bf16[512,1024]{1,0:T(8,128)(2,1)S(1)} %get-tuple-element.81.refs_15_) | copy-start | bytes 3145732
  172.0 63.8 %copy-start.9 = (f32[128,1024]{1,0:T(8,128)}, f32[128,1024]{1,0:T(8,128)S(1)}, u32[]{:S(2)}) copy-start(f32[128,1024]{1,0:T(8,128)S(1)} %get-tuple-element.66.h.refs_4_) | copy-start | bytes 1572868
  172.0 63.8 %copy-start.16 = (bf16[512,1024]{1,0:T(8,128)(2,1)}, bf16[512,1024]{1,0:T(8,128)(2,1)S(1)}, u32[]{:S(2)}) copy-start(bf16[512,1024]{1,0:T(8,128)(2,1)S(1)} %get-tuple-element.72.refs_2_) | copy-start | bytes 3145732
  172.0 11.6 %copy-start.19 = (f32[128,1024]{1,0:T(8,128)S(1)}, f32[128,1024]{1,0:T(8,128)}, u32[]{:S(2)}) copy-start(f32[128,1024]{1,0:T(8,128)} %g.1) | copy-start | bytes 1572868
  237.3 15.5 %copy-start.7 = (bf16[1024,1024]{1,0:T(8,128)(2,1)}, bf16[1024,1024]{1,0:T(8,128)(2,1)S(1)}, u32[]{:S(2)}) copy-start(bf16[1024,1024]{1,0:T(8,128)(2,1)S(1)} %get-tuple-element.75) | copy-start | bytes 6291460
  237.3 17.2 %copy-start.8 = (bf16[1024,1024]{1,0:T(8,128)(2,1)}, bf16[1024,1024]{1,0:T(8,128)(2,1)S(1)}, u32[]{:S(2)}) copy-start(bf16[1024,1024]{1,0:T(8,128)(2,1)S(1)} %get-tuple-element.76) | copy-start | bytes 6291460
  254.5 90.8 %copy-start.18 = (bf16[512,256]{1,0:T(8,128)(2,1)S(1)}, bf16[512,256]{1,0:T(8,128)(2,1)}, u32[]{:S(2)}) copy-start(bf16[512,256]{1,0:T(8,128)(2,1)} %copy-done.17) | copy-start | bytes 786436
  345.3 17.4 %copy-start.10 = (bf16[1024,1024]{1,0:T(8,128)(2,1)S(1)}, bf16[1024,1024]{1,0:T(8,128)(2,1)}, u32[]{:S(2)}) copy-start(bf16[1024,1024]{1,0:T(8,128)(2,1)} %get-tuple-element.96) | copy-start | bytes 6291460
  345.4 17.4 %copy-start.12 = (bf16[512,1024]{1,0:T(8,128)(2,1)S(1)}, bf16[512,1024]{1,0:T(8,128)(2,1)}, u32[]{:S(2)}) copy-start(bf16[512,1024]{1,0:T(8,128)(2,1)} %copy-done.11) | copy-start | bytes 3145732
  459.3 5.6 %copy-start.27 = (bf16[128,1024]{1,0:T(8,128)(2,1)S(1)}, bf16[128,1024]{1,0:T(8,128)(2,1)}, u32[]{:S(2)}) copy-start(bf16[128,1024]{1,0:T(8,128)(2,1)} %copy-done.26) | copy-start | bytes 786436
  (12 other events, 11.4 us)

commit v5 on v4

--- a/solution.py
+++ b/solution.py
@@ -1196,9 +1196,9 @@
         second(k)
     for k in range(4):
         third(k)
+    steps(0)
     for k in range(4):
         arrive(3, k)
-    steps(0)
     own = dwin[pl.ds(OWN0, S), :].astype(F32)
     proj[:, LW:] = (own + dc[...].astype(F32) + uc[...].astype(F32)).astype(BF)
     for copy in loads:
@@ -1367,11 +1367,12 @@
     vectors.over_chip()
     wide.finish(accs, 2, 3)
     narrow.start(2, 3)
+    narrow.forward(0, 1)
     vectors.over_y()
-    narrow.forward(0, 1)
     narrow.forward(2, 3)
+    narrow.beyond(0, 1)
     vectors.over_x()
-    narrow.beyond(0, 1, 2, 3)
+    narrow.beyond(2, 3)
     vectors.finish(vout)
     narrow.finish(sums)
     wires.close()

time: 473 us -> 469 us (level)
  no operation moved by 1% of the time
where the time goes in v5:
time: 469 us; the launch traced here: 466 us
  Pallas kernels  444 us (95%)
  local copies, waits for them, and re-layouts  17 us (4%)
    pallas_call x9, Pallas kernels, call(): pl.pallas_call(kernel, out_shape=shapes, in_specs=specs or [VM] * len(ins...  444 us
    unnamed x76, local copies, waits for them, and re-layouts  16.2 us

profile of v5, /device:TPU:0, one launch (start us, length us, event | category | flops | bytes accessed | tf_op | source)
XLA Modules:
  0.0 465.6 jit_solution(9833214427499214585)
XLA Ops:
  0.7 1.9 copy-done
  2.6 0.9 copy-done.5
  3.5 0.7 copy-done.24
  4.2 0.7 copy-done.28
  5.7 64.9 %inward.1 = (bf16[512,1024]{1,0:T(8,128)(2,1)S(1)}, bf16[512,256]{1,0:T(8,128)(2,1)S(1)}, bf16[3328,512]{1,0:T(8,128)(2,1)S(1)}) custom-call(bf16[128,1024]{1,0:T(8,128)(2,1)S(1)} %copy-done.5, f32[2,2,1024]{2,1,0:T(2,128)S(1)} %copy-done.24, f32[2,2,1024]{2,1,0:T(2,128)S(1)} %copy-done.28, f32[2,2,256]{2,1,0:T(2,128)S(1)} %copy-done.33, ...), custom_call_target="tpu_custom_call" | custom-call | tf_op jit(solution)/shard_map/inward/pallas_call | solution.py:364
  70.6 1.0 copy-done.11
  71.6 12.2 %attend.2 = (bf16[512,256]{1,0:T(8,128)(2,1)S(1)}, f32[16,1024]{1,0:T(8,128)S(1)}) custom-call(s32[11]{0:T(128)S(1)} %copy-done.35, bf16[512,256]{1,0:T(8,128)(2,1)S(1)} %get-tuple-element.60.q, bf16[3328,512]{1,0:T(8,128)(2,1)S(1)} %get-tuple-element.61.win), custom_call_target="tpu_custom_call" | custom-call | tf_op jit(solution)/shard_map/attend/pallas_call | solution.py:364
  83.9 86.4 %between_layers.1 = (f32[128,1024]{1,0:T(8,128)S(1)}, f32[128,1024]{1,0:T(8,128)S(1)}, f32[128,1024]{1,0:T(8,128)S(1)}, f32[128,1024]{1,0:T(8,128)S(1)}, bf16[51...) custom-call(bf16[512,256]{1,0:T(8,128)(2,1)S(1)} %get-tuple-element., ...), custom_call_target="tpu_custom_call" | custom-call | tf_op jit(solution)/shard_map/between_layers/pallas_call | solution.py:364
  170.3 0.8 copy-done.20
  171.1 0.8 copy-done.21
  171.9 0.8 copy-done.22
  172.8 12.4 %attend.3 = (bf16[512,256]{1,0:T(8,128)(2,1)S(1)}, f32[16,1024]{1,0:T(8,128)S(1)}) custom-call(s32[11]{0:T(128)S(1)} %copy-done.35, bf16[512,256]{1,0:T(8,128)(2,1)S(1)} %get-tuple-element.63.q, bf16[3328,512]{1,0:T(8,128)(2,1)S(1)} %get-tuple-element.64.win), custom_call_target="tpu_custom_call" | custom-call | tf_op jit(solution)/shard_map/attend/pallas_call | solution.py:364
  185.2 52.0 %turn.1 = (bf16[128,1024]{1,0:T(8,128)(2,1)S(1)}, f32[128,1024]{1,0:T(8,128)S(1)}, bf16[512,256]{1,0:T(8,128)(2,1)S(1)}, bf16[1024,1024]{1,0:T(8,128)(2,1)S(1)},...) custom-call(bf16[512,256]{1,0:T(8,128)(2,1)S(1)} %get-tuple-element., ...), custom_call_target="tpu_custom_call" | custom-call | tf_op jit(solution)/shard_map/turn/pallas_call | solution.py:364
  237.2 0.8 copy-done.23
  238.7 16.7 %attend_back.2 = (bf16[512,256]{1,0:T(8,128)(2,1)S(1)}, bf16[3328,512]{1,0:T(8,128)(2,1)S(1)}) custom-call(s32[11]{0:T(128)S(1)} %copy-done.35, bf16[512,256]{1,0:T(8,128)(2,1)S(1)} %get-tuple-element.63.q, bf16[3328,512]{1,0:T(8,128)(2,1)S(1)} %get-tuple-element.64.win, bf16[512,256]{1,0:T(8,128)(2,1)S(1)} %get-tuple-element.68.grad, ...), custom_call_target="tpu_custom_call" | custom-call | tf_op jit(solution)/shard_map/attend_back/pallas_call | solution.py:364
  255.4 1.7 copy-done.3
  257.1 91.2 %middle.1 = (f32[8,1024]{1,0:T(8,128)S(1)}, f32[8,768]{1,0:T(8,128)S(1)}, f32[128,1024]{1,0:T(8,128)S(1)}, bf16[512,256]{1,0:T(8,128)(2,1)S(1)}, bf16[1024,1024]...) custom-call(bf16[512,256]{1,0:T(8,128)(2,1)S(1)} %get-tuple-element., ...), custom_call_target="tpu_custom_call" | custom-call | tf_op jit(solution)/shard_map/middle/pallas_call | solution.py:364
  348.3 16.9 %attend_back.3 = (bf16[512,256]{1,0:T(8,128)(2,1)S(1)}, bf16[3328,512]{1,0:T(8,128)(2,1)S(1)}) custom-call(s32[11]{0:T(128)S(1)} %copy-done.35, bf16[512,256]{1,0:T(8,128)(2,1)S(1)} %copy-done.18, bf16[3328,512]{1,0:T(8,128)(2,1)S(1)} %get-tuple-element.61.win, bf16[512,256]{1,0:T(8,128)(2,1)S(1)} %get-tuple-element.83.grad, ...), custom_call_target="tpu_custom_call" | custom-call | tf_op jit(solution)/shard_map/attend_back/pallas_call | solution.py:364
  365.2 1.7 copy-done.4
  366.9 91.2 %final.1 = (f32[128,1024]{1,0:T(8,128)S(1)}, f32[24,1024]{1,0:T(8,128)S(1)}, f32[32,1024]{1,0:T(8,128)S(1)}, f32[32,1024]{1,0:T(8,128)S(1)}, f32[32,512]{1,0:T(8,128)S(1)}, /*index=5*/f32[32,512]{1,0:T(8,128)S(1)}) custom-call(bf16[512,256]{1,0:T(8,128)(2,1)S(1)} %get-tuple-element.85.refs_0_, bf16[3328,512]{1,0:T(8,128)(2,1)} %copy-done.4, ...), custom_call_target="tpu_custom_call" | custom-call | tf_op jit(solution)/shard_map/final/pallas_call | solution.py:364
  461.5 0.7 copy.28
  462.2 0.7 pad_maximum_fusion.1
  463.0 0.7 pad_maximum_fusion.2
  464.4 0.8 copy.33
  (77 shorter events, 5.6 us)
Async XLA Ops:
  0.6 71.0 %copy-start.35 = (s32[11]{0:T(128)S(1)}, s32[11]{0:T(128)}, u32[]{:S(2)}) copy-start(s32[11]{0:T(128)} %starts.7) | copy-start | bytes 136
  0.7 1.9 copy-start
  5.6 78.2 %copy-start.1 = (bf16[2,1024,3,256]{3,1,2,0:T(8,128)(2,1)S(1)}, bf16[2,1024,3,256]{3,1,2,0:T(8,128)(2,1)}, u32[]{:S(2)}) copy-start(bf16[2,1024,3,256]{3,1,2,0:T(8,128)(2,1)} %param.17) | copy-start | bytes 9437188
  5.6 78.2 %copy-start.2 = (bf16[2,256,1024]{2,1,0:T(8,128)(2,1)S(1)}, bf16[2,256,1024]{2,1,0:T(8,128)(2,1)}, u32[]{:S(2)}) copy-start(bf16[2,256,1024]{2,1,0:T(8,128)(2,1)} %refs_18_.1) | copy-start | bytes 3145732
  5.6 78.2 %copy-start.6 = (bf16[128,1024]{1,0:T(8,128)(2,1)S(1)}, bf16[128,1024]{1,0:T(8,128)(2,1)}, u32[]{:S(2)}) copy-start(bf16[128,1024]{1,0:T(8,128)(2,1)} %refs_4_.1) | copy-start | bytes 786436
  5.6 78.2 %copy-start.25 = (f32[2,2,1024]{2,1,0:T(2,128)S(1)}, f32[2,2,1024]{2,1,0:T(2,128)}, u32[]{:S(2)}) copy-start(f32[2,2,1024]{2,1,0:T(2,128)} %refs_5_.3) | copy-start | bytes 49156
  5.6 78.2 %copy-start.29 = (f32[2,2,1024]{2,1,0:T(2,128)S(1)}, f32[2,2,1024]{2,1,0:T(2,128)}, u32[]{:S(2)}) copy-start(f32[2,2,1024]{2,1,0:T(2,128)} %bias.5) | copy-start | bytes 49156
  5.6 78.2 %copy-start.30 = (f32[2,2,1024]{2,1,0:T(2,128)S(1)}, f32[2,2,1024]{2,1,0:T(2,128)}, u32[]{:S(2)}) copy-start(f32[2,2,1024]{2,1,0:T(2,128)} %refs_9_.1) | copy-start | bytes 49156
  5.7 78.2 %copy-start.31 = (f32[2,2,1024]{2,1,0:T(2,128)S(1)}, f32[2,2,1024]{2,1,0:T(2,128)}, u32[]{:S(2)}) copy-start(f32[2,2,1024]{2,1,0:T(2,128)} %refs_10_.1) | copy-start | bytes 49156
  5.7 78.2 %copy-start.32 = (f32[2,1024]{1,0:T(2,128)S(1)}, f32[2,1024]{1,0:T(2,128)}, u32[]{:S(2)}) copy-start(f32[2,1024]{1,0:T(2,128)} %b1.3) | copy-start | bytes 24580
  5.7 78.2 %copy-start.34 = (f32[2,2,256]{2,1,0:T(2,128)S(1)}, f32[2,2,256]{2,1,0:T(2,128)}, u32[]{:S(2)}) copy-start(f32[2,2,256]{2,1,0:T(2,128)} %b2.3) | copy-start | bytes 12292
  71.6 12.2 %copy-start.17 = (bf16[512,256]{1,0:T(8,128)(2,1)}, bf16[512,256]{1,0:T(8,128)(2,1)S(1)}, u32[]{:S(2)}) copy-start(bf16[512,256]{1,0:T(8,128)(2,1)S(1)} %get-tuple-element.60.q) | copy-start | bytes 786436
  172.7 12.4 %copy-start.13 = (bf16[512,1024]{1,0:T(8,128)(2,1)}, bf16[512,1024]{1,0:T(8,128)(2,1)S(1)}, u32[]{:S(2)}) copy-start(bf16[512,1024]{1,0:T(8,128)(2,1)S(1)} %get-tuple-element.82.refs_16_) | copy-start | bytes 3145732
  172.8 12.4 %copy-start.14 = (bf16[512,1024]{1,0:T(8,128)(2,1)}, bf16[512,1024]{1,0:T(8,128)(2,1)S(1)}, u32[]{:S(2)}) copy-start(bf16[512,1024]{1,0:T(8,128)(2,1)S(1)} %get-tuple-element.80.refs_14_) | copy-start | bytes 3145732
  172.8 12.4 %copy-start.15 = (bf16[512,1024]{1,0:T(8,128)(2,1)}, bf16[512,1024]{1,0:T(8,128)(2,1)S(1)}, u32[]{:S(2)}) copy-start(bf16[512,1024]{1,0:T(8,128)(2,1)S(1)} %get-tuple-element.81.refs_15_) | copy-start | bytes 3145732
  172.8 64.4 %copy-start.9 = (f32[128,1024]{1,0:T(8,128)}, f32[128,1024]{1,0:T(8,128)S(1)}, u32[]{:S(2)}) copy-start(f32[128,1024]{1,0:T(8,128)S(1)} %get-tuple-element.66.h.refs_4_) | copy-start | bytes 1572868
  172.8 64.4 %copy-start.16 = (bf16[512,1024]{1,0:T(8,128)(2,1)}, bf16[512,1024]{1,0:T(8,128)(2,1)S(1)}, u32[]{:S(2)}) copy-start(bf16[512,1024]{1,0:T(8,128)(2,1)S(1)} %get-tuple-element.72.refs_2_) | copy-start | bytes 3145732
  172.8 12.4 %copy-start.19 = (f32[128,1024]{1,0:T(8,128)S(1)}, f32[128,1024]{1,0:T(8,128)}, u32[]{:S(2)}) copy-start(f32[128,1024]{1,0:T(8,128)} %g.1) | copy-start | bytes 1572868
  238.7 16.7 %copy-start.7 = (bf16[1024,1024]{1,0:T(8,128)(2,1)}, bf16[1024,1024]{1,0:T(8,128)(2,1)S(1)}, u32[]{:S(2)}) copy-start(bf16[1024,1024]{1,0:T(8,128)(2,1)S(1)} %get-tuple-element.75) | copy-start | bytes 6291460
  238.7 18.4 %copy-start.8 = (bf16[1024,1024]{1,0:T(8,128)(2,1)}, bf16[1024,1024]{1,0:T(8,128)(2,1)S(1)}, u32[]{:S(2)}) copy-start(bf16[1024,1024]{1,0:T(8,128)(2,1)S(1)} %get-tuple-element.76) | copy-start | bytes 6291460
  257.1 91.2 %copy-start.18 = (bf16[512,256]{1,0:T(8,128)(2,1)S(1)}, bf16[512,256]{1,0:T(8,128)(2,1)}, u32[]{:S(2)}) copy-start(bf16[512,256]{1,0:T(8,128)(2,1)} %copy-done.17) | copy-start | bytes 786436
  348.3 18.6 %copy-start.10 = (bf16[1024,1024]{1,0:T(8,128)(2,1)S(1)}, bf16[1024,1024]{1,0:T(8,128)(2,1)}, u32[]{:S(2)}) copy-start(bf16[1024,1024]{1,0:T(8,128)(2,1)} %get-tuple-element.96) | copy-start | bytes 6291460
  348.3 18.6 %copy-start.12 = (bf16[512,1024]{1,0:T(8,128)(2,1)S(1)}, bf16[512,1024]{1,0:T(8,128)(2,1)}, u32[]{:S(2)}) copy-start(bf16[512,1024]{1,0:T(8,128)(2,1)} %copy-done.11) | copy-start | bytes 3145732
  458.1 5.6 %copy-start.27 = (bf16[128,1024]{1,0:T(8,128)(2,1)S(1)}, bf16[128,1024]{1,0:T(8,128)(2,1)}, u32[]{:S(2)}) copy-start(bf16[128,1024]{1,0:T(8,128)(2,1)} %copy-done.26) | copy-start | bytes 786436
  (12 other events, 11.4 us)
